TPU v7x, 32 devices: a whole 2x2x4 slice. The times are simulated.
32 devices in a mesh: group: 2 (over y), lon: 4 (over z), lat: 2 (over x), lev: 2 (over core).
Axes of the slice: x: 2, y: 2, z: 4, core: 2. Of those that a mesh axis runs over, the one named last changes fastest.
Arguments:
- fields: float32 [6, 64, 32, 512], P('lev', None, ('group', 'lat'), 'lon'), parts along dimension 2, may hold values from -6 to 6
- in_scale: float32 [6, 64], P('lev'), may hold values from 0.5 to 2
- out_scale: float32 [6, 64], P('lev'), may hold values from 0.3 to 1.5
- w_in: bfloat16 [256, 384], replicated, may hold values from -0.3125 to 0.3125
- w_mid: bfloat16 [3, 256, 256], replicated, may hold values from -0.375 to 0.375
- w_out: bfloat16 [384, 256], replicated, may hold values from -0.375 to 0.375
- storm_mask: int32 [32, 512], P(('group', 'lat'), 'lon'), parts along dimension 0, may hold values 0 or 1
- balance: int32 [32, 4], P(('group', 'lat')), parts along dimension 0, may hold values from -1 to 3, as said below
- substeps: int32 [64], replicated, may hold values from 1 to 3
- courant: float32 [2, 64], replicated, as said below
Outputs:
- advected: float32 [6, 64, 32, 512], P('lev', None, ('group', 'lat'), 'lon'), parts along dimension 2
There are 2 independent parts, one for each index of `group`. A program takes and returns all parts, laid end to end along the dimension named above; an argument that names none is the same for every part. Nothing has to cross between parts.
Inputs may be any that keep to these rules, and one draw needn't show every extreme that they name: `balance`: entry (i, d) is -1, d, or a neighbour (d - 1) or (d + 1) modulo 4. Within the 8 rows of one latitude block, at most 2 spans of a block go to each neighbour, and every block computes at most 4 spans: those it keeps plus those it receives. |courant[k, l]| <= 0.95 * substeps[l].
All inputs are finite; a program needn't handle non-finite values. No bound on the sum of `storm_mask` on one device may be relied on, other than what follows from the above.
Results may differ from a plain program's by a relative error of at most 0.0019.
Values may be sent and summed in bfloat16 or wider, within the bound.
No kernel may reach another device: no remote copies, remote signals or barrier semaphores. Data moves between devices by JAX's collectives and lax.ppermute only.
A program may use at most 64 MiB of HBM per device.

v0:
```python
import jax
import jax.numpy as jnp
from jax import lax
from jax.sharding import PartitionSpec as P

SUBS = 3


def shifted(block, axis, distance):
    devices = range(lax.axis_size(axis))
    route = [((i - distance) % len(devices), i) for i in devices]
    return lax.ppermute(block, axis, route)


def with_halo(array, sides, width, wrap):
    for axis, dim in sides:
        size, length = (lax.axis_size(axis), array.shape[dim])
        up = [(i, (i + 1) % size) for i in range(size if wrap else size - 1)]
        down = [(j, i) for i, j in up]
        last = lax.slice_in_dim(array, length - width, length, axis=dim)
        initial = lax.slice_in_dim(array, 0, width, axis=dim)
        before = lax.ppermute(last, axis, up)
        after = lax.ppermute(initial, axis, down)
        array = jnp.concatenate([before, array, after], axis=dim)
    return array


def donor_sweep(padded, step_lon, step_lat):
    east_lon = jnp.maximum(step_lon, 0.0)
    west_lon = jnp.minimum(step_lon, 0.0)
    flux_lon = east_lon * padded[..., :-1] + west_lon * padded[..., 1:]
    swept_lon = padded[..., 1:-1] - (flux_lon[..., 1:] - flux_lon[..., :-1])
    east_lat = jnp.maximum(step_lat, 0.0)
    west_lat = jnp.minimum(step_lat, 0.0)
    flux_lat = east_lat * swept_lon[..., :-1, :] + west_lat * swept_lon[..., 1:, :]
    return swept_lon[..., 1:-1, :] - (flux_lat[..., 1:, :] - flux_lat[..., :-1, :])


def running_rank(marker):
    return jnp.cumsum(marker.astype(jnp.int32)) - 1


def pick_rows(marker, slot_count):
    ranking = running_rank(marker)
    matched = marker[None, :] & (
        ranking[None, :] == jnp.arange(slot_count, dtype=jnp.int32)[:, None]
    )
    positions = jnp.arange(marker.shape[0], dtype=jnp.int32)[None, :]
    return jnp.sum(jnp.where(matched, positions, 0), axis=1)


def hidden_layers(hidden, w_mid):
    for layer in range(w_mid.shape[0]):
        hidden = jax.nn.silu(
            jnp.dot(w_mid[layer], hidden, preferred_element_type=jnp.float32)
        ).astype(jnp.bfloat16)
    return hidden


def on_device(
    fields, in_scale, out_scale, w_in, w_mid, w_out, storm_mask, balance, substeps, courant
):
    lev_index = lax.axis_index("lev")
    lon_index = lax.axis_index("lon")
    lon_count = lax.axis_size("lon")
    tracers, levels, row_count, columns = fields.shape
    width_in = tracers * levels
    features = (fields * in_scale[:, :, None, None]).astype(jnp.bfloat16)
    blocks = jnp.arange(lon_count, dtype=jnp.int32)

    def column_of(position):
        return jnp.sum(jnp.where(blocks[None, :] == position, balance, 0), axis=1)

    own_targets = column_of(lon_index)
    slot_cap = row_count // 4
    work_cap = row_count // 2
    right_id = (lon_index + 1) % lon_count
    left_id = (lon_index - 1 + lon_count) % lon_count
    kept_rows = own_targets == lon_index
    to_right = own_targets == right_id
    to_left = own_targets == left_id
    from_left = column_of(left_id) == lon_index
    from_right = column_of(right_id) == lon_index
    candidates = [features]
    for offset, marker in ((1, to_right), (-1, to_left)):
        outgoing = jnp.take(features, pick_rows(marker, slot_cap), axis=2)
        candidates.append(shifted(outgoing, "lon", offset))
    candidates = jnp.concatenate(candidates, axis=2)
    slot_ids = jnp.arange(slot_cap, dtype=jnp.int32)
    occupied = jnp.concatenate(
        [
            kept_rows,
            slot_ids < jnp.sum(from_left.astype(jnp.int32)),
            slot_ids < jnp.sum(from_right.astype(jnp.int32)),
        ]
    )
    work = jnp.take(candidates, pick_rows(occupied, work_cap), axis=2)
    slot_count = work.shape[2]
    stacked = work.reshape(width_in, slot_count * columns)
    w_first = lax.dynamic_slice_in_dim(w_in, lev_index * width_in, width_in, 1)
    partial_sum = jnp.dot(w_first, stacked, preferred_element_type=jnp.float32)
    pre_act = lax.psum(partial_sum.astype(jnp.bfloat16), "lev").astype(jnp.float32)
    hidden = hidden_layers(jax.nn.silu(pre_act).astype(jnp.bfloat16), w_mid)
    w_last = lax.dynamic_slice_in_dim(w_out, lev_index * width_in, width_in, 0)
    outputs = jnp.dot(w_last, hidden, preferred_element_type=jnp.float32).astype(jnp.bfloat16)
    results = outputs.reshape(tracers, levels, slot_count, columns)
    work_slot = running_rank(occupied)
    returned = [results]
    for offset, first_slot in ((-1, row_count), (1, row_count + slot_cap)):
        picked = jnp.clip(work_slot[first_slot : first_slot + slot_cap], 0, work_cap - 1)
        answer = jnp.take(results, picked, axis=2)
        returned.append(shifted(answer, "lon", offset))
    returned = jnp.concatenate(returned, axis=2)
    anchor = jnp.where(
        kept_rows,
        work_slot[:row_count],
        jnp.where(
            to_right,
            work_cap + running_rank(to_right),
            jnp.where(to_left, work_cap + slot_cap + running_rank(to_left), 0),
        ),
    )
    tendency = jnp.take(returned, jnp.clip(anchor, 0, work_cap + 2 * slot_cap - 1), axis=2)
    convecting = (own_targets >= 0).astype(jnp.float32)
    active = storm_mask.astype(jnp.float32) * convecting[:, None]
    tracer_state = (
        fields + out_scale[:, :, None, None] * tendency.astype(jnp.float32) * active[None, None]
    )
    counts = substeps.astype(jnp.float32)
    for substep in range(SUBS):
        padded = with_halo(tracer_state, (("lon", 3),), 1, True)
        padded = with_halo(padded, (("lat", 2),), 1, False)
        running = substeps > substep
        step_lon = jnp.where(running, courant[0] / counts, 0.0).reshape(1, -1, 1, 1)
        step_lat = jnp.where(running, courant[1] / counts, 0.0).reshape(1, -1, 1, 1)
        step_lon, step_lat = (step_lon, step_lat)
        tracer_state = donor_sweep(padded, step_lon, step_lat)
    return tracer_state


def solution(mesh):
    in_specs = (
        P("lev", None, ("group", "lat"), "lon"),
        P("lev", None),
        P("lev", None),
        P(),
        P(),
        P(),
        P(("group", "lat"), "lon"),
        P(("group", "lat"), None),
        P(),
        P(),
    )
    out_specs = P("lev", None, ("group", "lat"), "lon")
    return jax.shard_map(
        on_device, mesh=mesh, in_specs=in_specs, out_specs=out_specs, check_vma=False
    )
```

profile of v0, /device:TPU:0, one launch (start us, length us, event | category | flops | bytes accessed | tf_op | source)
XLA Modules:
  0.0 121.3 jit_solution(15492676471551638229)
XLA Ops:
  6.6 0.8 select_reduce_fusion.2
  8.1 1.4 %fusion.12 = bf16[3,64,8,128]{3,1,2,0:T(8,128)(2,1)S(1)} fusion(f32[3,64,8,128]{3,2,1,0:T(8,128)} %param.14, f32[3,64]{1,0:T(4,128)} %param.15), kind=kLoop, calls=%fused_computation.46 | loop fusion | flops 393216 | bytes 1180416 | tf_op jit(solution)/shard_map/convert_element_type | solution.py:68
  9.5 0.6 gather_fusion.2
  10.1 3.1 %collective-permute-start = (bf16[3,64,2,128]{3,1,0,2:T(8,128)(2,1)S(1)}, bf16[3,64,2,128]{3,1,0,2:T(8,128)(2,1)S(1)}, u32[]{:S(2)}, u32[]{:S(2)}) collective-permute-start(bf16[3,64,2,128]{3,1,0,2:T(8,128)(2,1)S(1)} %select_bitcast_fusion.2), channel_id=1, source_target_pairs={{12,0},{0,4},{4,8},{8,12},{13,1},{1,5},{5,9},{9,13},{14,2},{2,6},{... | collective-permute-start | bytes 294920 | tf_op jit(solution)/shard_map/ppermute | solution.py:12
  13.2 0.6 gather_fusion.3
  13.8 2.1 %collective-permute-start.1 = (bf16[3,64,2,128]{3,1,2,0:T(8,128)(2,1)S(1)}, bf16[3,64,2,128]{3,1,2,0:T(8,128)(2,1)S(1)}, u32[]{:S(2)}, u32[]{:S(2)}) collective-permute-start(bf16[3,64,2,128]{3,1,2,0:T(8,128)(2,1)S(1)} %fusion.35), channel_id=1, source_target_pairs={{4,0},{8,4},{12,8},{0,12},{5,1},{9,5},{13,9},{1,13},{6,2},{10,6},{... | collective-permute-start | bytes 294920 | tf_op jit(solution)/shard_map/ppermute | solution.py:12
  15.9 0.6 fusion.41
  16.6 0.6 fusion.53
  17.2 0.7 iota_compare_fusion.4
  17.9 0.6 fusion.54
  18.5 0.6 iota_compare_fusion.2
  19.7 0.4 collective-permute-done.1
  20.2 0.6 gather_fusion
  20.9 1.0 convolution_convert_fusion
  22.0 18.4 %all-reduce.2.cloned.1.call-done = bf16[256,512]{1,0:T(8,128)(2,1)} async-done(((bf16[256,512]{1,0:T(8,128)(2,1)}), bf16[256,512]{1,0:T(8,128)(2,1)}) %all-reduce.2.cloned.1.call-update) | async-done | bytes 262160 | tf_op jit(solution)/shard_map/psum | solution.py:102
  40.4 1.6 %multiply_convert_fusion.1 = bf16[256,512]{1,0:T(8,128)(2,1)S(1)} fusion(bf16[256,512]{1,0:T(8,128)(2,1)} %all-reduce.2.cloned.1.call-done, bf16[3,256,256]{2,1,0:T(8,128)(2,1)S(1)} %copy-done.6), kind=kOutput, calls=%fused_computation.55 | convolution fusion | flops 136314880 | bytes 786432 | tf_op jit(solution)/shard_map/dot_general | solution.py:55
  42.1 0.5 convolution_convert_fusion.1
  42.7 0.6 gather_fusion.5
  43.3 0.6 gather_fusion.4
  43.9 3.6 %collective-permute-start.2 = (bf16[3,64,2,128]{3,1,0,2:T(8,128)(2,1)S(1)}, bf16[3,64,2,128]{3,1,0,2:T(8,128)(2,1)S(1)}, u32[]{:S(2)}, u32[]{:S(2)}) collective-permute-start(bf16[3,64,2,128]{3,1,0,2:T(8,128)(2,1)S(1)} %select_bitcast_fusion.1), channel_id=1, source_target_pairs={{4,0},{8,4},{12,8},{0,12},{5,1},{9,5},{13,9},{1,13},{6,2},{10,6},{... | collective-permute-start | bytes 294920 | tf_op jit(solution)/shard_map/ppermute | solution.py:12
  47.7 3.0 %collective-permute-done.2 = bf16[3,64,2,128]{3,1,0,2:T(8,128)(2,1)S(1)} collective-permute-done((bf16[3,64,2,128]{3,1,0,2:T(8,128)(2,1)S(1)}, bf16[3,64,2,128]{3,1,0,2:T(8,128)(2,1)S(1)}, u32[]{:S(2)}, u32[]{:S(2)}) %collective-permute-start.2) | collective-permute-done | bytes 98336 | tf_op jit(solution)/shard_map/ppermute | solution.py:12
  50.8 3.5 %collective-permute-done.3 = bf16[3,64,2,128]{3,1,0,2:T(8,128)(2,1)S(1)} collective-permute-done((bf16[3,64,2,128]{3,1,0,2:T(8,128)(2,1)S(1)}, bf16[3,64,2,128]{3,1,0,2:T(8,128)(2,1)S(1)}, u32[]{:S(2)}, u32[]{:S(2)}) %collective-permute-start.3) | collective-permute-done | bytes 98336 | tf_op jit(solution)/shard_map/ppermute | solution.py:12
  54.2 0.6 gather_fusion.1
  54.9 0.3 bitcast_add_fusion
  55.2 0.3 fusion.57
  55.5 0.3 copy.80
  55.8 0.3 copy.81
  56.1 0.9 collective-permute-start.5
  57.0 1.2 collective-permute-start.4
  58.2 4.3 %collective-permute-done.4 = f32[3,64,8,1]{1,2,3,0:T(8,128)S(1)} collective-permute-done((f32[3,64,8,1]{1,2,3,0:T(8,128)S(1)}, f32[3,64,8,1]{1,2,3,0:T(8,128)S(1)}, u32[]{:S(2)}, u32[]{:S(2)}) %collective-permute-start.4) | collective-permute-done | bytes 6176 | tf_op jit(solution)/shard_map/ppermute | solution.py:22
  62.5 0.3 copy.82
  62.8 0.3 copy.83
  63.4 3.4 %collective-permute-start.6 = (f32[3,64,1,130]{3,1,0,2:T(8,128)S(1)}, f32[3,64,1,130]{3,1,0,2:T(8,128)S(1)}, u32[]{:S(2)}, u32[]{:S(2)}) collective-permute-start(f32[3,64,1,130]{3,1,0,2:T(8,128)S(1)} %get-tuple-element.28), channel_id=1, source_target_pairs={{0,2},{1,3},{4,6},{5,7},{8,10},{9,11},{12,14},{13,15},{16,18},{17,... | collective-permute-start | bytes 299528 | tf_op jit(solution)/shard_map/ppermute | solution.py:22
  66.8 1.3 %collective-permute-start.7 = (f32[3,64,1,130]{3,1,0,2:T(8,128)S(1)}, f32[3,64,1,130]{3,1,0,2:T(8,128)S(1)}, u32[]{:S(2)}, u32[]{:S(2)}) collective-permute-start(f32[3,64,1,130]{3,1,0,2:T(8,128)S(1)} %get-tuple-element.29), channel_id=1, source_target_pairs={{2,0},{3,1},{6,4},{7,5},{10,8},{11,9},{14,12},{15,13},{18,16},{19,... | collective-permute-start | bytes 299528 | tf_op jit(solution)/shard_map/ppermute | solution.py:23
  68.1 1.8 %collective-permute-done.6 = f32[3,64,1,130]{3,1,0,2:T(8,128)S(1)} collective-permute-done((f32[3,64,1,130]{3,1,0,2:T(8,128)S(1)}, f32[3,64,1,130]{3,1,0,2:T(8,128)S(1)}, u32[]{:S(2)}, u32[]{:S(2)}) %collective-permute-start.6) | collective-permute-done | bytes 99872 | tf_op jit(solution)/shard_map/ppermute | solution.py:22
  69.9 4.4 %collective-permute-done.7 = f32[3,64,1,130]{3,1,0,2:T(8,128)S(1)} collective-permute-done((f32[3,64,1,130]{3,1,0,2:T(8,128)S(1)}, f32[3,64,1,130]{3,1,0,2:T(8,128)S(1)}, u32[]{:S(2)}, u32[]{:S(2)}) %collective-permute-start.7) | collective-permute-done | bytes 99872 | tf_op jit(solution)/shard_map/ppermute | solution.py:23
  74.3 0.7 pad_maximum_fusion
  75.0 0.6 fusion.2
  75.7 0.6 fusion.5
  76.9 0.3 copy.84
  77.5 3.8 %collective-permute-start.9 = (f32[3,64,8,1]{1,2,3,0:T(8,128)S(1)}, f32[3,64,8,1]{1,2,3,0:T(8,128)S(1)}, u32[]{:S(2)}, u32[]{:S(2)}) collective-permute-start(f32[3,64,8,1]{1,2,3,0:T(8,128)S(1)} %copy.85), channel_id=1, source_target_pairs={{4,0},{8,4},{12,8},{0,12},{5,1},{9,5},{13,9},{1,13},{6,2},{10,6},{... | collective-permute-start | bytes 18440 | tf_op jit(solution)/shard_map/ppermute | solution.py:23
  81.3 1.4 %collective-permute-done.8 = f32[3,64,8,1]{1,2,3,0:T(8,128)S(1)} collective-permute-done((f32[3,64,8,1]{1,2,3,0:T(8,128)S(1)}, f32[3,64,8,1]{1,2,3,0:T(8,128)S(1)}, u32[]{:S(2)}, u32[]{:S(2)}) %collective-permute-start.8) | collective-permute-done | bytes 6176 | tf_op jit(solution)/shard_map/ppermute | solution.py:22
  82.7 0.3 copy.86
  83.0 0.3 copy.87
  83.6 1.5 %collective-permute-start.10 = (f32[3,64,1,130]{3,1,0,2:T(8,128)S(1)}, f32[3,64,1,130]{3,1,0,2:T(8,128)S(1)}, u32[]{:S(2)}, u32[]{:S(2)}) collective-permute-start(f32[3,64,1,130]{3,1,0,2:T(8,128)S(1)} %get-tuple-element.26), channel_id=1, source_target_pairs={{0,2},{1,3},{4,6},{5,7},{8,10},{9,11},{12,14},{13,15},{16,18},{17,... | collective-permute-start | bytes 299528 | tf_op jit(solution)/shard_map/ppermute | solution.py:22
  85.0 1.3 %collective-permute-start.11 = (f32[3,64,1,130]{3,1,0,2:T(8,128)S(1)}, f32[3,64,1,130]{3,1,0,2:T(8,128)S(1)}, u32[]{:S(2)}, u32[]{:S(2)}) collective-permute-start(f32[3,64,1,130]{3,1,0,2:T(8,128)S(1)} %get-tuple-element.27), channel_id=1, source_target_pairs={{2,0},{3,1},{6,4},{7,5},{10,8},{11,9},{14,12},{15,13},{18,16},{19,... | collective-permute-start | bytes 299528 | tf_op jit(solution)/shard_map/ppermute | solution.py:23
  86.3 1.9 %collective-permute-done.10 = f32[3,64,1,130]{3,1,0,2:T(8,128)S(1)} collective-permute-done((f32[3,64,1,130]{3,1,0,2:T(8,128)S(1)}, f32[3,64,1,130]{3,1,0,2:T(8,128)S(1)}, u32[]{:S(2)}, u32[]{:S(2)}) %collective-permute-start.10) | collective-permute-done | bytes 99872 | tf_op jit(solution)/shard_map/ppermute | solution.py:22
  88.2 4.4 %collective-permute-done.11 = f32[3,64,1,130]{3,1,0,2:T(8,128)S(1)} collective-permute-done((f32[3,64,1,130]{3,1,0,2:T(8,128)S(1)}, f32[3,64,1,130]{3,1,0,2:T(8,128)S(1)}, u32[]{:S(2)}, u32[]{:S(2)}) %collective-permute-start.11) | collective-permute-done | bytes 99872 | tf_op jit(solution)/shard_map/ppermute | solution.py:23
  92.6 0.7 pad_maximum_fusion.1
  93.3 0.6 fusion.1
  93.9 0.6 fusion.4
  95.1 0.3 copy.88
  95.7 3.8 %collective-permute-start.13 = (f32[3,64,8,1]{1,2,3,0:T(8,128)S(1)}, f32[3,64,8,1]{1,2,3,0:T(8,128)S(1)}, u32[]{:S(2)}, u32[]{:S(2)}) collective-permute-start(f32[3,64,8,1]{1,2,3,0:T(8,128)S(1)} %copy.89), channel_id=1, source_target_pairs={{4,0},{8,4},{12,8},{0,12},{5,1},{9,5},{13,9},{1,13},{6,2},{10,6},{... | collective-permute-start | bytes 18440 | tf_op jit(solution)/shard_map/ppermute | solution.py:23
  99.6 1.4 %collective-permute-done.12 = f32[3,64,8,1]{1,2,3,0:T(8,128)S(1)} collective-permute-done((f32[3,64,8,1]{1,2,3,0:T(8,128)S(1)}, f32[3,64,8,1]{1,2,3,0:T(8,128)S(1)}, u32[]{:S(2)}, u32[]{:S(2)}) %collective-permute-start.12) | collective-permute-done | bytes 6176 | tf_op jit(solution)/shard_map/ppermute | solution.py:22
  100.9 0.3 copy.90
  101.3 0.3 copy.91
  101.8 1.5 %collective-permute-start.14 = (f32[3,64,1,130]{3,1,0,2:T(8,128)S(1)}, f32[3,64,1,130]{3,1,0,2:T(8,128)S(1)}, u32[]{:S(2)}, u32[]{:S(2)}) collective-permute-start(f32[3,64,1,130]{3,1,0,2:T(8,128)S(1)} %get-tuple-element.24), channel_id=1, source_target_pairs={{0,2},{1,3},{4,6},{5,7},{8,10},{9,11},{12,14},{13,15},{16,18},{17,... | collective-permute-start | bytes 299528 | tf_op jit(solution)/shard_map/ppermute | solution.py:22
  103.3 1.5 %collective-permute-start.15 = (f32[3,64,1,130]{3,1,0,2:T(8,128)S(1)}, f32[3,64,1,130]{3,1,0,2:T(8,128)S(1)}, u32[]{:S(2)}, u32[]{:S(2)}) collective-permute-start(f32[3,64,1,130]{3,1,0,2:T(8,128)S(1)} %get-tuple-element.25), channel_id=1, source_target_pairs={{2,0},{3,1},{6,4},{7,5},{10,8},{11,9},{14,12},{15,13},{18,16},{19,... | collective-permute-start | bytes 299528 | tf_op jit(solution)/shard_map/ppermute | solution.py:23
  104.8 1.7 %collective-permute-done.14 = f32[3,64,1,130]{3,1,0,2:T(8,128)S(1)} collective-permute-done((f32[3,64,1,130]{3,1,0,2:T(8,128)S(1)}, f32[3,64,1,130]{3,1,0,2:T(8,128)S(1)}, u32[]{:S(2)}, u32[]{:S(2)}) %collective-permute-start.14) | collective-permute-done | bytes 99872 | tf_op jit(solution)/shard_map/ppermute | solution.py:22
  106.4 4.4 %collective-permute-done.15 = f32[3,64,1,130]{3,1,0,2:T(8,128)S(1)} collective-permute-done((f32[3,64,1,130]{3,1,0,2:T(8,128)S(1)}, f32[3,64,1,130]{3,1,0,2:T(8,128)S(1)}, u32[]{:S(2)}, u32[]{:S(2)}) %collective-permute-start.15) | collective-permute-done | bytes 99872 | tf_op jit(solution)/shard_map/ppermute | solution.py:23
  110.9 0.7 pad_maximum_fusion.2
  111.5 0.6 fusion
  112.2 0.6 fusion.3
  113.1 1.3 %copy.92 = f32[3,64,8,128]{3,2,1,0:T(8,128)} copy(f32[3,64,8,128]{3,1,0,2:T(8,128)S(1)} %fusion.9) | data formatting | bytes 1572864 | tf_op jit(solution)/shard_map/sub | solution.py:36
  (78 shorter events, 5.0 us)
Async XLA Ops:
  6.5 14.4 %copy-start = (bf16[256,384]{1,0:T(8,128)(2,1)S(1)}, bf16[256,384]{1,0:T(8,128)(2,1)}, u32[]{:S(2)}) copy-start(bf16[256,384]{1,0:T(8,128)(2,1)} %param.17) | copy-start | bytes 589828
  6.5 33.9 %all-reduce.2.cloned.1.call-start = ((), (), s32[]{:S(2)}) async-start(), calls=%async_computation | async-start | bytes 524288 | tf_op jit(solution)/shard_map/psum | solution.py:102
  9.4 12.5 %copy-start.2 = (s32[8,128]{1,0:T(8,128)S(1)}, s32[8,128]{1,0:T(8,128)}, u32[]{:S(2)}) copy-start(s32[8,128]{1,0:T(8,128)} %param.20) | copy-start | bytes 12292
  9.4 31.0 %copy-start.6 = (bf16[3,256,256]{2,1,0:T(8,128)(2,1)S(1)}, bf16[3,256,256]{2,1,0:T(8,128)(2,1)}, u32[]{:S(2)}) copy-start(bf16[3,256,256]{2,1,0:T(8,128)(2,1)} %param.18) | copy-start | bytes 1179652
  10.1 9.6 %collective-permute-start = (bf16[3,64,2,128]{3,1,0,2:T(8,128)(2,1)S(1)}, bf16[3,64,2,128]{3,1,0,2:T(8,128)(2,1)S(1)}, u32[]{:S(2)}, u32[]{:S(2)}) collective-permute-start(bf16[3,64,2,128]{3,1,0,2:T(8,128)(2,1)S(1)} %select_bitcast_fusion.2), channel_id=1, source_target_pairs={{12,0},{0,4},{4,8},{8,12},{13,1},{1,5},{5,9},{9,13},{14,2},{2,6},{... | collective-permute-start | bytes 294920 | tf_op jit(solution)/shard_map/ppermute | solution.py:12
  13.8 6.3 %collective-permute-start.1 = (bf16[3,64,2,128]{3,1,2,0:T(8,128)(2,1)S(1)}, bf16[3,64,2,128]{3,1,2,0:T(8,128)(2,1)S(1)}, u32[]{:S(2)}, u32[]{:S(2)}) collective-permute-start(bf16[3,64,2,128]{3,1,2,0:T(8,128)(2,1)S(1)} %fusion.35), channel_id=1, source_target_pairs={{4,0},{8,4},{12,8},{0,12},{5,1},{9,5},{13,9},{1,13},{6,2},{10,6},{... | collective-permute-start | bytes 294920 | tf_op jit(solution)/shard_map/ppermute | solution.py:12
  22.0 20.1 %copy-start.7 = (bf16[384,256]{1,0:T(8,128)(2,1)S(1)}, bf16[384,256]{1,0:T(8,128)(2,1)}, u32[]{:S(2)}) copy-start(bf16[384,256]{1,0:T(8,128)(2,1)} %param.19) | copy-start | bytes 589828
  42.6 12.3 %copy-start.1 = (f32[3,64,8,128]{3,2,1,0:T(8,128)S(1)}, f32[3,64,8,128]{3,2,1,0:T(8,128)}, u32[]{:S(2)}) copy-start(f32[3,64,8,128]{3,2,1,0:T(8,128)} %param.14) | copy-start | bytes 2359300
  42.6 12.3 %copy-start.3 = (f32[3,64]{1,0:T(4,128)S(1)}, f32[3,64]{1,0:T(4,128)}, u32[]{:S(2)}) copy-start(f32[3,64]{1,0:T(4,128)} %param.16) | copy-start | bytes 2308
  43.9 6.8 %collective-permute-start.2 = (bf16[3,64,2,128]{3,1,0,2:T(8,128)(2,1)S(1)}, bf16[3,64,2,128]{3,1,0,2:T(8,128)(2,1)S(1)}, u32[]{:S(2)}, u32[]{:S(2)}) collective-permute-start(bf16[3,64,2,128]{3,1,0,2:T(8,128)(2,1)S(1)} %select_bitcast_fusion.1), channel_id=1, source_target_pairs={{4,0},{8,4},{12,8},{0,12},{5,1},{9,5},{13,9},{1,13},{6,2},{10,6},{... | collective-permute-start | bytes 294920 | tf_op jit(solution)/shard_map/ppermute | solution.py:12
  47.6 6.6 %collective-permute-start.3 = (bf16[3,64,2,128]{3,1,0,2:T(8,128)(2,1)S(1)}, bf16[3,64,2,128]{3,1,0,2:T(8,128)(2,1)S(1)}, u32[]{:S(2)}, u32[]{:S(2)}) collective-permute-start(bf16[3,64,2,128]{3,1,0,2:T(8,128)(2,1)S(1)} %select_bitcast_fusion), channel_id=1, source_target_pairs={{12,0},{0,4},{4,8},{8,12},{13,1},{1,5},{5,9},{9,13},{14,2},{2,6},{... | collective-permute-start | bytes 294920 | tf_op jit(solution)/shard_map/ppermute | solution.py:12
  55.2 3.0 %copy-start.4 = (s32[64]{0:T(128)S(1)}, s32[64]{0:T(128)}, u32[]{:S(2)}) copy-start(s32[64]{0:T(128)} %param.22) | copy-start | bytes 772
  55.2 3.0 %copy-start.5 = (f32[2,64]{1,0:T(2,128)S(1)}, f32[2,64]{1,0:T(2,128)}, u32[]{:S(2)}) copy-start(f32[2,64]{1,0:T(2,128)} %param.23) | copy-start | bytes 1540
  56.1 6.7 %collective-permute-start.5 = (f32[3,64,8,1]{1,2,3,0:T(8,128)S(1)}, f32[3,64,8,1]{1,2,3,0:T(8,128)S(1)}, u32[]{:S(2)}, u32[]{:S(2)}) collective-permute-start(f32[3,64,8,1]{1,2,3,0:T(8,128)S(1)} %copy.81), channel_id=1, source_target_pairs={{4,0},{8,4},{12,8},{0,12},{5,1},{9,5},{13,9},{1,13},{6,2},{10,6},{... | collective-permute-start | bytes 18440 | tf_op jit(solution)/shard_map/ppermute | solution.py:23
  57.0 5.5 %collective-permute-start.4 = (f32[3,64,8,1]{1,2,3,0:T(8,128)S(1)}, f32[3,64,8,1]{1,2,3,0:T(8,128)S(1)}, u32[]{:S(2)}, u32[]{:S(2)}) collective-permute-start(f32[3,64,8,1]{1,2,3,0:T(8,128)S(1)} %copy.80), channel_id=1, source_target_pairs={{0,4},{4,8},{8,12},{12,0},{1,5},{5,9},{9,13},{13,1},{2,6},{6,10},{... | collective-permute-start | bytes 18440 | tf_op jit(solution)/shard_map/ppermute | solution.py:22
  63.4 6.5 %collective-permute-start.6 = (f32[3,64,1,130]{3,1,0,2:T(8,128)S(1)}, f32[3,64,1,130]{3,1,0,2:T(8,128)S(1)}, u32[]{:S(2)}, u32[]{:S(2)}) collective-permute-start(f32[3,64,1,130]{3,1,0,2:T(8,128)S(1)} %get-tuple-element.28), channel_id=1, source_target_pairs={{0,2},{1,3},{4,6},{5,7},{8,10},{9,11},{12,14},{13,15},{16,18},{17,... | collective-permute-start | bytes 299528 | tf_op jit(solution)/shard_map/ppermute | solution.py:22
  66.8 7.6 %collective-permute-start.7 = (f32[3,64,1,130]{3,1,0,2:T(8,128)S(1)}, f32[3,64,1,130]{3,1,0,2:T(8,128)S(1)}, u32[]{:S(2)}, u32[]{:S(2)}) collective-permute-start(f32[3,64,1,130]{3,1,0,2:T(8,128)S(1)} %get-tuple-element.29), channel_id=1, source_target_pairs={{2,0},{3,1},{6,4},{7,5},{10,8},{11,9},{14,12},{15,13},{18,16},{19,... | collective-permute-start | bytes 299528 | tf_op jit(solution)/shard_map/ppermute | solution.py:23
  77.1 5.5 %collective-permute-start.8 = (f32[3,64,8,1]{1,2,3,0:T(8,128)S(1)}, f32[3,64,8,1]{1,2,3,0:T(8,128)S(1)}, u32[]{:S(2)}, u32[]{:S(2)}) collective-permute-start(f32[3,64,8,1]{1,2,3,0:T(8,128)S(1)} %copy.84), channel_id=1, source_target_pairs={{0,4},{4,8},{8,12},{12,0},{1,5},{5,9},{9,13},{13,1},{2,6},{6,10},{... | collective-permute-start | bytes 18440 | tf_op jit(solution)/shard_map/ppermute | solution.py:22
  77.5 5.5 %collective-permute-start.9 = (f32[3,64,8,1]{1,2,3,0:T(8,128)S(1)}, f32[3,64,8,1]{1,2,3,0:T(8,128)S(1)}, u32[]{:S(2)}, u32[]{:S(2)}) collective-permute-start(f32[3,64,8,1]{1,2,3,0:T(8,128)S(1)} %copy.85), channel_id=1, source_target_pairs={{4,0},{8,4},{12,8},{0,12},{5,1},{9,5},{13,9},{1,13},{6,2},{10,6},{... | collective-permute-start | bytes 18440 | tf_op jit(solution)/shard_map/ppermute | solution.py:23
  83.6 4.6 %collective-permute-start.10 = (f32[3,64,1,130]{3,1,0,2:T(8,128)S(1)}, f32[3,64,1,130]{3,1,0,2:T(8,128)S(1)}, u32[]{:S(2)}, u32[]{:S(2)}) collective-permute-start(f32[3,64,1,130]{3,1,0,2:T(8,128)S(1)} %get-tuple-element.26), channel_id=1, source_target_pairs={{0,2},{1,3},{4,6},{5,7},{8,10},{9,11},{12,14},{13,15},{16,18},{17,... | collective-permute-start | bytes 299528 | tf_op jit(solution)/shard_map/ppermute | solution.py:22
  85.0 7.6 %collective-permute-start.11 = (f32[3,64,1,130]{3,1,0,2:T(8,128)S(1)}, f32[3,64,1,130]{3,1,0,2:T(8,128)S(1)}, u32[]{:S(2)}, u32[]{:S(2)}) collective-permute-start(f32[3,64,1,130]{3,1,0,2:T(8,128)S(1)} %get-tuple-element.27), channel_id=1, source_target_pairs={{2,0},{3,1},{6,4},{7,5},{10,8},{11,9},{14,12},{15,13},{18,16},{19,... | collective-permute-start | bytes 299528 | tf_op jit(solution)/shard_map/ppermute | solution.py:23
  95.4 5.5 %collective-permute-start.12 = (f32[3,64,8,1]{1,2,3,0:T(8,128)S(1)}, f32[3,64,8,1]{1,2,3,0:T(8,128)S(1)}, u32[]{:S(2)}, u32[]{:S(2)}) collective-permute-start(f32[3,64,8,1]{1,2,3,0:T(8,128)S(1)} %copy.88), channel_id=1, source_target_pairs={{0,4},{4,8},{8,12},{12,0},{1,5},{5,9},{9,13},{13,1},{2,6},{6,10},{... | collective-permute-start | bytes 18440 | tf_op jit(solution)/shard_map/ppermute | solution.py:22
  95.7 5.5 %collective-permute-start.13 = (f32[3,64,8,1]{1,2,3,0:T(8,128)S(1)}, f32[3,64,8,1]{1,2,3,0:T(8,128)S(1)}, u32[]{:S(2)}, u32[]{:S(2)}) collective-permute-start(f32[3,64,8,1]{1,2,3,0:T(8,128)S(1)} %copy.89), channel_id=1, source_target_pairs={{4,0},{8,4},{12,8},{0,12},{5,1},{9,5},{13,9},{1,13},{6,2},{10,6},{... | collective-permute-start | bytes 18440 | tf_op jit(solution)/shard_map/ppermute | solution.py:23
  101.8 4.6 %collective-permute-start.14 = (f32[3,64,1,130]{3,1,0,2:T(8,128)S(1)}, f32[3,64,1,130]{3,1,0,2:T(8,128)S(1)}, u32[]{:S(2)}, u32[]{:S(2)}) collective-permute-start(f32[3,64,1,130]{3,1,0,2:T(8,128)S(1)} %get-tuple-element.24), channel_id=1, source_target_pairs={{0,2},{1,3},{4,6},{5,7},{8,10},{9,11},{12,14},{13,15},{16,18},{17,... | collective-permute-start | bytes 299528 | tf_op jit(solution)/shard_map/ppermute | solution.py:22
  103.3 7.6 %collective-permute-start.15 = (f32[3,64,1,130]{3,1,0,2:T(8,128)S(1)}, f32[3,64,1,130]{3,1,0,2:T(8,128)S(1)}, u32[]{:S(2)}, u32[]{:S(2)}) collective-permute-start(f32[3,64,1,130]{3,1,0,2:T(8,128)S(1)} %get-tuple-element.25), channel_id=1, source_target_pairs={{2,0},{3,1},{6,4},{7,5},{10,8},{11,9},{14,12},{15,13},{18,16},{19,... | collective-permute-start | bytes 299528 | tf_op jit(solution)/shard_map/ppermute | solution.py:23
Sparse Core Ops, SparseCore 0:
  22.1 18.3 all-reduce.1
where the time goes:
time: 122 us; the launch traced here: 121 us
  waiting for transfers between devices  50.9 us (42%)
  starting transfers between devices  29 us (24%)
  other arithmetic  14.6 us (12%)
  between operations  14 us (11%)
  local copies, waits for them, and re-layouts  9.68 us (8%)
  matrix products  3.11 us (3%)
    psum x1, waiting for transfers between devices, on_device(): lax.psum(partial_sum.astype(jnp.bfloat16), 'lev').astype(jnp.float32)  18.4 us
    ppermute x6, waiting for transfers between devices, with_halo(): after = lax.ppermute(initial, axis, down)  13.2 us
    ppermute x6, starting transfers between devices, with_halo(): after = lax.ppermute(initial, axis, down)  12.6 us
    ppermute x6, waiting for transfers between devices, with_halo(): before = lax.ppermute(last, axis, up)  12.4 us
    ppermute x4, starting transfers between devices, shifted(): return lax.ppermute(block, axis, route)  8.86 us
    ppermute x6, starting transfers between devices, with_halo(): before = lax.ppermute(last, axis, up)  7.54 us
    ppermute x4, waiting for transfers between devices, shifted(): return lax.ppermute(block, axis, route)  6.88 us
  transfers between devices with their start and end apart: 17, of which 13 were waited for; matrix products, arithmetic and copies ran while one was open for 5% of the time, Pallas kernels for 0%

commit v1 on v0

v1 whole, which is shorter than its diff:
```python
import functools

import jax
import jax.numpy as jnp
from jax import lax
from jax.experimental import pallas as pl
from jax.experimental.pallas import tpu as pltpu
from jax.sharding import PartitionSpec as P

W = 3
LANES = 128
EXTRA = 8
F32 = jnp.float32
BF16 = jnp.bfloat16
VMEM_LIMIT = 40 * 1024 * 1024


def lane_ids(rows):
    return lax.broadcasted_iota(jnp.int32, (rows, LANES), 1)


def turned(x, shift):
    if isinstance(shift, int):
        shift %= LANES
        if shift == 0:
            return x
    return pltpu.roll(x, shift, 1)


def silu(v):
    half = 0.5 * v
    return half + half * jnp.tanh(half)


def as_columns(scratch, parts):
    scratch[...] = jnp.zeros_like(scratch)
    at = 0
    for part in parts:
        scratch[at : at + part.shape[0], : part.shape[1]] = part
        at += part.shape[0]
    return scratch[...].T


def column(turned_rows, index, levels):
    return jnp.broadcast_to(turned_rows[:levels, index : index + 1], (levels, LANES))


def side_packs(edges):
    lane = lane_ids(edges[0].shape[0])
    east = lane % 6 < 3
    last = [jnp.where(east, e, 0.0) for e in edges]
    first = [jnp.where(east, 0.0, e) for e in edges]
    east_pack = last[0] + turned(last[1], 3) + turned(last[2], 48)
    west_pack = turned(first[0], -3) + first[1] + turned(first[2], 45)
    return east_pack, west_pack


def prepare_kernel(tracers, levels, rows, moves, fields, in_scale, storm, balance, features, keep, give, active, *rest):
    edge_rows, (scratch,) = rest[: len(moves)], rest[len(moves) :]
    lon, lat, lev = (lax.axis_index(name) for name in ("lon", "lat", "lev"))
    position = lax.broadcasted_iota(jnp.int32, balance.shape, 1)
    target = jnp.max(jnp.where(position == lon, balance[...], -1).astype(F32), axis=1, keepdims=True)
    mask = jnp.where(target >= 0.0, storm[...].astype(F32), 0.0)
    active[...] = mask
    scales = as_columns(scratch, [in_scale[...]])
    lane = lane_ids(levels)
    edges = []
    scale_lanes = jnp.zeros((levels, LANES), F32)
    for t in range(tracers):
        scale = column(scales, t, levels)
        scale_lanes = jnp.where(lane == 96 + t, scale, scale_lanes)
        pack = jnp.zeros((levels, LANES), F32)
        for i in range(rows):
            x = fields[pl.ds(t * levels * rows + i, levels, stride=rows), :]
            features[i, t * levels : (t + 1) * levels, :] = (x * scale).astype(BF16)
            pack = jnp.where((lane >= 6 * i) & (lane < 6 * i + 6), turned(x, 6 * i + W), pack)
        edges.append(pack)
    lane = lane_ids(1)
    mask_pack = jnp.zeros((1, LANES), F32)
    for i in range(rows):
        mask_pack = jnp.where((lane >= 6 * i) & (lane < 6 * i + 6), turned(active[i : i + 1, :], 6 * i + W), mask_pack)
    mask_pack = jnp.broadcast_to(mask_pack, (EXTRA, LANES))
    none = jnp.zeros_like(mask_pack)
    last_pack, first_pack = side_packs(edges)
    last_mask, first_mask = side_packs([mask_pack, none, none])
    head = lev == 0
    keep[:levels] = jnp.where(head, last_pack, first_pack) + scale_lanes
    give[:levels] = jnp.where(head, first_pack, last_pack) + scale_lanes
    keep[levels:] = jnp.where(head, last_mask, first_mask)
    give[levels:] = jnp.where(head, first_mask, last_mask)
    for move, out in zip(moves, edge_rows):
        start = first_row_sent(move, lat, rows)
        for r in range(W):
            for t in range(tracers):
                x = fields[pl.ds(t * levels * rows + start + r, levels, stride=rows), :]
                out[(r * tracers + t) * levels : (r * tracers + t + 1) * levels, :] = x
        tail = W * tracers * levels
        for r in range(W):
            out[tail + r : tail + r + 1, :] = active[pl.ds(start + r, 1), :]
        out[tail + W :, :] = jnp.zeros((EXTRA - W, LANES), F32)


def first_row_sent(move, lat, rows):
    if move == 0:
        return jnp.where(lat == 0, rows - W, 0)
    return rows - W if move > 0 else 0


def first_row_received(move, lat, rows):
    if move == 0:
        return jnp.where(lat == 0, 0, rows - W)
    return rows - W if move > 0 else 0


def network(x, w_in, w_mid, w_last):
    hidden = silu(jnp.dot(w_in, x, preferred_element_type=F32)).astype(BF16)
    for layer in range(len(w_mid)):
        hidden = silu(jnp.dot(w_mid[layer], hidden, preferred_element_type=F32)).astype(BF16)
    return jnp.dot(w_last, hidden, preferred_element_type=F32).astype(BF16)


def taps(step, count):
    first = jnp.abs(step)
    second = jnp.where(count > 1.5, first, 0.0)
    third = jnp.where(count > 2.5, first, 0.0)
    rest = [1.0 - a for a in (first, second, third)]
    return (
        rest[0] * rest[1] * rest[2],
        first * rest[1] * rest[2] + rest[0] * second * rest[2] + rest[0] * rest[1] * third,
        first * second * rest[2] + first * rest[1] * third + rest[0] * second * third,
        first * second * third,
    )


OUT_SCALE, LON, LON_SIGN, LAT, LAT_SIGN, EDGE, PLANES = 0, 3, 7, 8, 12, 13, 18


def write_weights(weights, scratch, out_scale, courant, substeps, levels):
    columns = as_columns(scratch, [out_scale[...], courant[...], substeps[...].astype(F32)])
    tracers = out_scale.shape[0]
    for t in range(tracers):
        weights[OUT_SCALE + t] = column(columns, t, levels)
    count = column(columns, tracers + 2, levels)
    lane = lane_ids(levels)
    place = lane % 6
    step = column(columns, tracers, levels) / count
    up = step > 0.0
    w = taps(step, count)
    weights[LON_SIGN] = jnp.where(up, 1.0, 0.0)
    for k in range(4):
        weights[LON + k] = jnp.where(
            up, jnp.where(lane >= k, w[k], 0.0), jnp.where(lane < LANES - (W - k), w[W - k], 0.0)
        )
    east = [jnp.where(up | (place > 2) | (place < d), 0.0, w[W - d]) for d in range(3)]
    west = [jnp.where(up & (place > 2) & (place + d < 6), w[W - d], 0.0) for d in range(3)]
    weights[EDGE] = east[0] + west[0]
    weights[EDGE + 1] = east[1]
    weights[EDGE + 2] = west[1]
    weights[EDGE + 3] = east[2]
    weights[EDGE + 4] = west[2]
    step = column(columns, tracers + 1, levels) / count
    up = step > 0.0
    w = taps(step, count)
    weights[LAT_SIGN] = jnp.where(up, 1.0, 0.0)
    for k in range(4):
        weights[LAT + k] = jnp.where(up, w[W - k], w[k])


def sweep_lon(q, weights, span):
    up = weights[LON_SIGN, span, :] > 0.5
    q = jnp.where(up, q, turned(q, -W))
    total = weights[LON, span, :] * q
    for k in range(1, 4):
        total += weights[LON + k, span, :] * turned(q, k)
    return total


def own_kernel(
    tracers, levels, rows, fields, mine, other, w_in, w_mid, w_out, out_scale, courant, substeps, active,
    swept, weights, x, tendency, scratch,
):
    lev = lax.axis_index("lev")
    width = tracers * levels
    write_weights(weights, scratch, out_scale, courant, substeps, levels)
    near = pl.ds(pl.multiple_of(lev * width, width), width)
    far = pl.ds(pl.multiple_of((1 - lev) * width, width), width)
    w_last = w_out[near, :]
    for i in range(rows):
        x[near, i * LANES : (i + 1) * LANES] = mine[i]
        x[far, i * LANES : (i + 1) * LANES] = other[i]
    step = 2 * LANES
    for j in range(0, rows * LANES, step):
        tendency[:, j : j + step] = network(x[:, j : j + step], w_in[...], w_mid, w_last)
    for t in range(tracers):
        for i in range(rows):
            for g in range(0, levels, 16):
                span = slice(g, g + 16)
                at = t * levels + g
                q = fields[pl.ds(at * rows + i, 16, stride=rows), :]
                moist = tendency[at : at + 16, i * LANES : (i + 1) * LANES].astype(F32)
                q = q + weights[OUT_SCALE + t, span, :] * moist * active[i : i + 1, :]
                swept[i, at : at + 16, :] = sweep_lon(q, weights, span)


def finish_kernel(tracers, levels, rows, moves, *refs):
    count = len(moves)
    swept, weights, w_in, w_mid, w_out, packs, ring, ring_other = refs[:8]
    corner, corner_other, edge, edge_other = (refs[8 + n * count : 8 + (n + 1) * count] for n in range(4))
    out, x, tendency, halo, mask_rows = refs[8 + 4 * count :]
    lat, lev = lax.axis_index("lat"), lax.axis_index("lev")
    width = tracers * levels
    block = levels + EXTRA
    head = lev == 0
    near = pl.ds(pl.multiple_of(lev * width, width), width)
    far = pl.ds(pl.multiple_of((1 - lev) * width, width), width)
    w_last = w_out[near, :]

    def sides(received, forwarded):
        own_r, other_r = received[:block], received[block:]
        other_f, own_f = forwarded[:block], forwarded[block:]
        return (
            (jnp.where(head, own_r, own_f), jnp.where(head, own_f, own_r)),
            (jnp.where(head, other_r, other_f), jnp.where(head, other_f, other_r)),
        )

    ring_sides = sides(ring, ring_other)
    corner_sides = [sides(c, f) for c, f in zip(corner, corner_other)]
    lane = lane_ids(levels)
    east = lane % 6 < 3

    def unpack(which, t, part):
        shift_east = (0, -3, -48)[t]
        shift_west = (3, 0, -45)[t]
        west_pack, east_pack = ring_sides[which]
        picked = east[: part.stop - part.start]
        value = jnp.where(picked, turned(east_pack[part], shift_east), turned(west_pack[part], shift_west))
        lane_part = lane[: part.stop - part.start]
        for n, move in enumerate(moves):
            west_pack, east_pack = corner_sides[n][which]
            base = 48 + 18 * n
            shift = base - 6 * first_row_received(move, lat, rows) + 2 * LANES
            far_value = jnp.where(
                picked, turned(east_pack[part], (shift + shift_east) % LANES), turned(west_pack[part], (shift + shift_west) % LANES)
            )
            value = jnp.where((lane_part >= base) & (lane_part < base + 18), far_value, value)
        return jnp.where(lane_part < 48 + 18 * count, value, 0.0)

    for which, place in ((0, near), (1, far)):
        start = lev * width if which == 0 else (1 - lev) * width
        source = edge if which == 0 else edge_other
        for t in range(tracers):
            scale = jnp.broadcast_to(packs[which * block : which * block + levels, 96 + t : 97 + t], (levels, LANES))
            to = pl.ds(pl.multiple_of(start + t * levels, levels), levels)
            value = unpack(which, t, slice(0, levels))
            if which == 0:
                halo[t] = value
            x[to, :LANES] = (value * scale).astype(BF16)
            for n in range(count):
                for r in range(W):
                    column_at = (1 + n * W + r) * LANES
                    value = source[n][(r * tracers + t) * levels : (r * tracers + t + 1) * levels, :]
                    x[to, column_at : column_at + LANES] = (value * scale).astype(BF16)
    mask_rows[...] = unpack(0, 0, slice(levels, block))
    total = (1 + W * count) * LANES
    step = 2 * LANES
    for j in range(0, total, step):
        stop = min(j + step, total)
        tendency[:, j:stop] = network(x[:, j:stop], w_in[...], w_mid, w_last)

    tail = W * tracers * levels
    lane = lane_ids(8)
    at_edge = (lane < W) | (lane >= LANES - W)
    southward = jnp.where(lat == 0, 0.0, 1.0)
    for t in range(tracers):
        for g in range(0, levels, 16):
            span = slice(g, g + 16)
            at = t * levels + g
            lane = lane_ids(16)
            at_edge = (lane < W) | (lane >= LANES - W)
            scale = weights[OUT_SCALE + t, span, :]
            up = weights[LAT_SIGN, span, :] > 0.5

            def physics(value, column_at, mask):
                return value + scale * tendency[at : at + 16, column_at : column_at + LANES].astype(F32) * mask

            sides_q = physics(halo[t, span, :], 0, mask_rows[0:1, :])
            if count == 2:
                sides_q = jnp.where(up | (lane < 48), sides_q, turned(sides_q, -18))
            fix = weights[EDGE, span, :] * sides_q
            for k, shift in ((1, 1), (2, -1), (3, 2), (4, -2)):
                fix += weights[EDGE + k, span, :] * turned(sides_q, shift)

            def fixed(value, first):
                return value + jnp.where(at_edge, turned(fix, LANES - W - first), 0.0)

            beyond = []
            for r in range(W):
                rows_q = [
                    physics(
                        edge[n][(r * tracers + t) * levels + g : (r * tracers + t) * levels + g + 16, :],
                        (1 + n * W + r) * LANES,
                        edge[n][tail + r : tail + r + 1, :],
                    )
                    for n in range(count)
                ]
                q = jnp.where(up, rows_q[0], rows_q[-1])
                q = fixed(sweep_lon(q, weights, span), 48 + 6 * r)
                if count == 1:
                    q = jnp.where(weights[LAT_SIGN, span, :] == southward, q, 0.0)
                beyond.append(q)
            inner = [fixed(swept[i, at : at + 16, :], 6 * i) for i in range(rows)]
            line = []
            for i in range(rows + W):
                above = beyond[i] if i < W else inner[i - W]
                below = inner[i] if i < rows else beyond[i - rows]
                line.append(jnp.where(up, above, below))
            for i in range(rows):
                value = weights[LAT, span, :] * line[i]
                for k in range(1, 4):
                    value += weights[LAT + k, span, :] * line[i + k]
                out[pl.ds(at * rows + i, 16, stride=rows), :] = value


def call(kernel, out_shape, scratch, flops, moved, name):
    return pl.pallas_call(
        kernel,
        out_shape=out_shape,
        scratch_shapes=scratch,
        compiler_params=pltpu.CompilerParams(vmem_limit_bytes=VMEM_LIMIT),
        cost_estimate=pl.CostEstimate(flops=flops, bytes_accessed=moved, transcendentals=0),
        name=name,
    )


def swap_cores(x):
    return lax.ppermute(x, "lev", [(0, 1), (1, 0)])


def routes(lon_count, lat_count, move, along_lon):
    pairs = []
    for i in range(lon_count):
        for j in range(lat_count):
            to_lat = 1 - j if move == 0 else j + (move or 0)
            if not 0 <= to_lat < lat_count:
                continue
            for k in range(2):
                to_lon = (i + (1 - 2 * k)) % lon_count if along_lon else i
                pairs.append((((i * lat_count) + j) * 2 + k, ((to_lon * lat_count) + to_lat) * 2 + k))
    return pairs


def send(x, move, along_lon):
    axes = ("lon", "lat", "lev")
    lon_count, lat_count = lax.axis_size("lon"), lax.axis_size("lat")
    if move is None:
        pairs = []
        for i in range(lon_count):
            for j in range(lat_count):
                for k in range(2):
                    to_lon = (i + (1 - 2 * k)) % lon_count
                    pairs.append(((i * lat_count + j) * 2 + k, (to_lon * lat_count + j) * 2 + k))
    else:
        pairs = routes(lon_count, lat_count, move, along_lon)
    return lax.ppermute(x, axes, pairs)


def on_device(fields, in_scale, out_scale, w_in, w_mid, w_out, storm_mask, balance, substeps, courant):
    tracers, levels, rows, columns = fields.shape
    width = tracers * levels
    moves = (0,) if lax.axis_size("lat") == 2 else (1, -1)
    count = len(moves)
    flat = fields.reshape(width * rows, columns)
    block = levels + EXTRA
    edge_shape = jax.ShapeDtypeStruct((W * width + EXTRA, columns), F32)
    pack_shape = jax.ShapeDtypeStruct((block, LANES), F32)
    features, keep, give, active, *edge_rows = call(
        functools.partial(prepare_kernel, tracers, levels, rows, moves),
        [jax.ShapeDtypeStruct((rows, width, columns), BF16), pack_shape, pack_shape,
         jax.ShapeDtypeStruct((rows, columns), F32)] + [edge_shape] * count,
        [pltpu.VMEM((8, LANES), F32)],
        10**6, 2 * 10**6, "prepare",
    )(flat, in_scale, storm_mask, balance)

    given = swap_cores(give)
    features_other = swap_cores(features)
    edge = [send(e, move, False) for e, move in zip(edge_rows, moves)]
    packs = jnp.concatenate([keep, given], axis=0)
    corner = [send(packs, move, True) for move in moves]
    ring = send(packs, None, True)

    swept, weights = call(
        functools.partial(own_kernel, tracers, levels, rows),
        [jax.ShapeDtypeStruct((rows, width, columns), F32), jax.ShapeDtypeStruct((PLANES, levels, LANES), F32)],
        [pltpu.VMEM((2 * width, rows * columns), BF16), pltpu.VMEM((width, rows * columns), BF16),
         pltpu.VMEM((8, LANES), F32)],
        10**9, 4 * 10**6, "own_columns",
    )(flat, features, features_other, w_in, w_mid, w_out, out_scale, courant, substeps.reshape(1, levels), active)

    ring_other = swap_cores(ring)
    corner_other = [swap_cores(c) for c in corner]
    edge_other = [swap_cores(e) for e in edge]
    total = (1 + W * count) * LANES
    out = call(
        functools.partial(finish_kernel, tracers, levels, rows, moves),
        jax.ShapeDtypeStruct((width * rows, columns), F32),
        [pltpu.VMEM((2 * width, total), BF16), pltpu.VMEM((width, total), BF16),
         pltpu.VMEM((tracers, levels, LANES), F32), pltpu.VMEM((EXTRA, LANES), F32)],
        10**9, 4 * 10**6, "finish",
    )(swept, weights, w_in, w_mid, w_out, packs, ring, ring_other, *corner, *corner_other, *edge, *edge_other)
    return out.reshape(fields.shape)


def solution(mesh):
    in_specs = (
        P("lev", None, ("group", "lat"), "lon"),
        P("lev", None),
        P("lev", None),
        P(),
        P(),
        P(),
        P(("group", "lat"), "lon"),
        P(("group", "lat"), None),
        P(),
        P(),
    )
    out_specs = P("lev", None, ("group", "lat"), "lon")
    return jax.shard_map(
        on_device, mesh=mesh, in_specs=in_specs, out_specs=out_specs, check_vma=False
    )
```

time: 122 us -> 30.6 us (0.25)
  waiting for transfers between devices: 50.9 us -> 11.7 us
  starting transfers between devices: 29 us -> 7.9 us
  other arithmetic: 14.6 us -> 0 us
  between operations: 14 us -> 0.11 us
  Pallas kernels: 0 us -> 8.08 us
  local copies, waits for them, and re-layouts: 9.68 us -> 2.58 us
  matrix products: 3.11 us -> 0 us
    ppermute x16 -> x8, starting transfers between devices: 29 us -> 7.9 us  [the longest x3 7.39 us: send(): return lax.ppermute(x, axes, pairs)]
    ppermute x16 -> x8, waiting for transfers between devices: 32.5 us -> 11.7 us  [the longest x3 11.7 us: send(): return lax.ppermute(x, axes, pairs)]
    psum x1 -> x0, waiting for transfers between devices: 18.4 us -> none  [on_device(): lax.psum(partial_sum.astype(jnp.bfloat16), 'lev').astype(jnp.float32)]
    pallas_call x0 -> x3, Pallas kernels: none -> 8.08 us  [the longest x1 4.12 us: on_device(): call(functools.partial(own_kernel, tracers, levels, rows), [jax.ShapeDtyp...]
    gather x7 -> x0, local copies, waits for them, and re-layouts: 3.63 us -> none  [the longest x2 1.13 us: on_device(): answer = jnp.take(results, picked, axis=2)]
    concatenate x8 -> x0, other arithmetic: 3.38 us -> none  [the longest x3 2.03 us: with_halo(): array = jnp.concatenate([before, array, after], axis=dim)]
    dot_general x3 -> x0, matrix products: 3.11 us -> none  [the longest x1 1.64 us: hidden_layers(): jnp.dot(w_mid[layer], hidden, preferred_element_type=jnp.float32)]
    add x7 -> x0, other arithmetic: 2.8 us -> none  [the longest x3 1.95 us: donor_sweep(): flux_lon = east_lon * padded[..., :-1] + west_lon * padded[..., 1:]]
  transfers between devices with their start and end apart: 17 -> 8, of which waited for: 13 -> 3; matrix products, arithmetic and copies ran while one was open for 5% -> 0% of each run, Pallas kernels for 0% -> 14%
where the time goes in v1:
time: 30.6 us; the launch traced here: 30.4 us
  waiting for transfers between devices  11.7 us (38%)
  Pallas kernels  8.08 us (26%)
  starting transfers between devices  7.9 us (26%)
  local copies, waits for them, and re-layouts  2.58 us (8%)
    ppermute x3, waiting for transfers between devices, send(): return lax.ppermute(x, axes, pairs)  11.7 us
    ppermute x3, starting transfers between devices, send(): return lax.ppermute(x, axes, pairs)  7.39 us
    pallas_call x1, Pallas kernels, on_device(): call(functools.partial(own_kernel, tracers, levels, rows), [jax.ShapeDtyp...  4.12 us
    pallas_call x1, Pallas kernels, on_device(): call(functools.partial(finish_kernel, tracers, levels, rows, moves), jax....  3.49 us
    unnamed x20, local copies, waits for them, and re-layouts  2.58 us
  transfers between devices with their start and end apart: 8, of which 3 were waited for; matrix products, arithmetic and copies ran while one was open for 0% of the time, Pallas kernels for 14%

profile of v1, /device:TPU:0, one launch (start us, length us, event | category | flops | bytes accessed | tf_op | source)
XLA Modules:
  0.0 30.4 jit_solution(12040680496071070359)
XLA Ops:
  0.0 0.0 copy-start.4
  0.0 0.0 copy-start.5
  0.0 0.8 %copy.11.balance = s32[8,4]{1,0:T(8,128)S(1)} copy(s32[8,4]{0,1:T(4,128)} %param.17) | data formatting | bytes 256 | tf_op args[7]
  0.8 0.0 copy-done.4
  0.8 0.0 copy-done.5
  0.8 0.0 copy-start
  0.8 1.1 %copy-done = f32[3,64,8,128]{3,2,1,0:T(8,128)S(1)} copy-done((f32[3,64,8,128]{3,2,1,0:T(8,128)S(1)}, f32[3,64,8,128]{3,2,1,0:T(8,128)}, u32[]{:S(2)}) %copy-start) | copy-done | bytes 786456
  1.9 0.0 copy-start.1
  1.9 0.0 copy-start.2
  1.9 0.0 copy-start.3
  1.9 0.5 %prepare.1 = (bf16[8,192,128]{2,1,0:T(8,128)(2,1)S(1)}, f32[72,128]{1,0:T(8,128)S(1)}, f32[72,128]{1,0:T(8,128)S(1)}, f32[8,128]{1,0:T(8,128)S(1)}, f32[584,128]{1,0:T(8,128)S(1)}) custom-call(f32[1536,128]{1,0:T(8,128)S(1)} %bitcast.3, f32[3,64]{1,0:T(4,128)S(1)} %copy-done.5, s32[8,128]{1,0:T(8,128)S(1)} %copy-done.4, s32[8,4]{1,0:T(8,128)S(1)} %copy.11.balance), custom_call_target="tpu_custom_call" | custom-call | flops 1000000 | bytes 2000000 | tf_op jit(solution)/shard_map/prepare/pallas_call | solution.py:376
  2.4 3.0 %collective-permute-start.6 = (f32[584,128]{1,0:T(8,128)S(1)}, f32[584,128]{1,0:T(8,128)S(1)}, u32[]{:S(2)}, u32[]{:S(2)}) collective-permute-start(f32[584,128]{1,0:T(8,128)S(1)} %get-tuple-element.18), channel_id=1, source_target_pairs={{0,2},{1,3},{2,0},{3,1},{4,6},{5,7},{6,4},{7,5},{8,10},{9,11},{10,... | collective-permute-start | bytes 897032 | tf_op jit(solution)/shard_map/ppermute | solution.py:364
  5.4 0.0 collective-permute-start
  5.4 0.5 %collective-permute-start.1 = (f32[72,128]{1,0:T(8,128)S(1)}, f32[72,128]{1,0:T(8,128)S(1)}, u32[]{:S(2)}, u32[]{:S(2)}) collective-permute-start(f32[72,128]{1,0:T(8,128)S(1)} %get-tuple-element.17), channel_id=1, source_target_pairs={{0,1},{1,0},{2,3},{3,2},{4,5},{5,4},{6,7},{7,6},{8,9},{9,8},{10,11... | collective-permute-start | bytes 110600 | tf_op jit(solution)/shard_map/ppermute | solution.py:336
  5.9 6.6 %collective-permute-done.6.refs_10_ = f32[584,128]{1,0:T(8,128)S(1)} collective-permute-done((f32[584,128]{1,0:T(8,128)S(1)}, f32[584,128]{1,0:T(8,128)S(1)}, u32[]{:S(2)}, u32[]{:S(2)}) %collective-permute-start.6) | collective-permute-done | bytes 299040 | tf_op jit(solution)/shard_map/ppermute | solution.py:364
  12.5 0.0 collective-permute-start.7
  12.5 0.0 collective-permute-done.1
  12.5 0.0 copy-start.6
  12.5 1.9 %collective-permute-start.2 = (f32[144,128]{1,0:T(8,128)S(1)}, f32[144,128]{1,0:T(8,128)S(1)}, u32[]{:S(2)}, u32[]{:S(2)}) collective-permute-start(f32[144,128]{1,0:T(8,128)S(1)} %constant_dynamic-update-slice_fusion.refs_5_), channel_id=1, source_target_pairs={{0,4},{1,13},{2,6},{3,15},{4,8},{5,1},{6,10},{7,3},{8,12},{9,5},{1... | collective-permute-start | bytes 221192 | tf_op jit(solution)/shard_map/ppermute | solution.py:364
  14.4 2.5 %collective-permute-start.4 = (f32[144,128]{1,0:T(8,128)S(1)}, f32[144,128]{1,0:T(8,128)S(1)}, u32[]{:S(2)}, u32[]{:S(2)}) collective-permute-start(f32[144,128]{1,0:T(8,128)S(1)} %constant_dynamic-update-slice_fusion.refs_5_), channel_id=1, source_target_pairs={{0,6},{1,15},{2,4},{3,13},{4,10},{5,3},{6,8},{7,1},{8,14},{9,7},{1... | collective-permute-start | bytes 221192 | tf_op jit(solution)/shard_map/ppermute | solution.py:364
  16.9 2.6 %collective-permute-done.2.refs_6_ = f32[144,128]{1,0:T(8,128)S(1)} collective-permute-done((f32[144,128]{1,0:T(8,128)S(1)}, f32[144,128]{1,0:T(8,128)S(1)}, u32[]{:S(2)}, u32[]{:S(2)}) %collective-permute-start.2) | collective-permute-done | bytes 73760 | tf_op jit(solution)/shard_map/ppermute | solution.py:364
  19.6 0.0 collective-permute-start.3
  19.6 2.5 %collective-permute-done.4.refs_8_ = f32[144,128]{1,0:T(8,128)S(1)} collective-permute-done((f32[144,128]{1,0:T(8,128)S(1)}, f32[144,128]{1,0:T(8,128)S(1)}, u32[]{:S(2)}, u32[]{:S(2)}) %collective-permute-start.4) | collective-permute-done | bytes 73760 | tf_op jit(solution)/shard_map/ppermute | solution.py:364
  22.1 0.0 collective-permute-start.5
  22.1 0.0 collective-permute-done.other
  22.1 0.0 copy-start.7
  22.1 0.0 copy-start.8
  22.1 0.0 copy-done.1
  22.1 0.0 copy-done.2
  22.1 0.0 copy-done.3
  22.1 0.0 copy-done.6
  22.1 0.6 %copy-done.7 = f32[2,64]{1,0:T(2,128)S(1)} copy-done((f32[2,64]{1,0:T(2,128)S(1)}, f32[2,64]{1,0:T(2,128)}, u32[]{:S(2)}) %copy-start.7) | copy-done | bytes 536
  22.7 0.0 copy-done.8
  22.7 4.1 %own_columns.1 = (f32[8,192,128]{2,1,0:T(8,128)S(1)}, f32[18,64,128]{2,1,0:T(8,128)S(1)}) custom-call(f32[1536,128]{1,0:T(8,128)S(1)} %bitcast.4, bf16[8,192,128]{2,1,0:T(8,128)(2,1)S(1)} %get-tuple-element.12.mine, bf16[8,192,128]{2,1,0:T(8,128)(2,1)S(1)} %collective-permute-done.other, bf16[256,384]{1,0:T(8,128)(2,1)S(1)} %copy-done.2, ...), custom_call_target="tpu_custom_call" | custom-call | flops 1000000000 | bytes 4000000 | tf_op jit(solution)/shard_map/own_columns/pallas_call | solution.py:391
  26.9 0.0 collective-permute-done.3.refs_7_
  26.9 0.0 collective-permute-done.5.refs_9_
  26.9 0.0 collective-permute-done.7.refs_11_
  26.9 3.5 %finish.1 = f32[1536,128]{1,0:T(8,128)} custom-call(f32[8,192,128]{2,1,0:T(8,128)S(1)} %get-tuple-element.14.refs_0_, f32[18,64,128]{2,1,0:T(8,128)S(1)} %get-tuple-element.15.refs_1_, bf16[256,384]{1,0:T(8,128)(2,1)S(1)} %copy-done.2, bf16[3,256,256]{2,1,0:T(8,128)(2,1)S(1)} %copy-done.1, bf16[384,256]{1,0:T(8,128)(2,1)S(1)} %copy-done.3, ...), custom_call_target="tpu_custom_call" | custom-call | flops 1000000000 | bytes 4000000 | tf_op jit(solution)/shard_map/finish/pallas_call | solution.py:403
  (2 shorter events, 0.0 us)
Async XLA Ops:
  0.0 0.8 %copy-start.4 = (s32[8,128]{1,0:T(8,128)S(1)}, s32[8,128]{1,0:T(8,128)}, u32[]{:S(2)}) copy-start(s32[8,128]{1,0:T(8,128)} %storm.1) | copy-start | bytes 12292
  0.0 0.8 %copy-start.5 = (f32[3,64]{1,0:T(4,128)S(1)}, f32[3,64]{1,0:T(4,128)}, u32[]{:S(2)}) copy-start(f32[3,64]{1,0:T(4,128)} %in_scale.1) | copy-start | bytes 2308
  0.8 1.1 %copy-start = (f32[3,64,8,128]{3,2,1,0:T(8,128)S(1)}, f32[3,64,8,128]{3,2,1,0:T(8,128)}, u32[]{:S(2)}) copy-start(f32[3,64,8,128]{3,2,1,0:T(8,128)} %param.10) | copy-start | bytes 2359300
  1.9 20.2 %copy-start.1 = (bf16[3,256,256]{2,1,0:T(8,128)(2,1)S(1)}, bf16[3,256,256]{2,1,0:T(8,128)(2,1)}, u32[]{:S(2)}) copy-start(bf16[3,256,256]{2,1,0:T(8,128)(2,1)} %refs_3_.1) | copy-start | bytes 1179652
  1.9 20.2 %copy-start.2 = (bf16[256,384]{1,0:T(8,128)(2,1)S(1)}, bf16[256,384]{1,0:T(8,128)(2,1)}, u32[]{:S(2)}) copy-start(bf16[256,384]{1,0:T(8,128)(2,1)} %refs_2_.1) | copy-start | bytes 589828
  1.9 20.2 %copy-start.3 = (bf16[384,256]{1,0:T(8,128)(2,1)S(1)}, bf16[384,256]{1,0:T(8,128)(2,1)}, u32[]{:S(2)}) copy-start(bf16[384,256]{1,0:T(8,128)(2,1)} %refs_4_.1) | copy-start | bytes 589828
  2.4 10.1 %collective-permute-start.6 = (f32[584,128]{1,0:T(8,128)S(1)}, f32[584,128]{1,0:T(8,128)S(1)}, u32[]{:S(2)}, u32[]{:S(2)}) collective-permute-start(f32[584,128]{1,0:T(8,128)S(1)} %get-tuple-element.18), channel_id=1, source_target_pairs={{0,2},{1,3},{2,0},{3,1},{4,6},{5,7},{6,4},{7,5},{8,10},{9,11},{10,... | collective-permute-start | bytes 897032 | tf_op jit(solution)/shard_map/ppermute | solution.py:364
  5.4 16.6 %collective-permute-start = (bf16[8,192,128]{2,1,0:T(8,128)(2,1)S(1)}, bf16[8,192,128]{2,1,0:T(8,128)(2,1)S(1)}, u32[]{:S(2)}, u32[]{:S(2)}) collective-permute-start(bf16[8,192,128]{2,1,0:T(8,128)(2,1)S(1)} %get-tuple-element.12.mine), channel_id=1, source_target_pairs={{0,1},{1,0},{2,3},{3,2},{4,5},{5,4},{6,7},{7,6},{8,9},{9,8},{10,11... | collective-permute-start | bytes 1179656 | tf_op jit(solution)/shard_map/ppermute | solution.py:336
  5.4 7.1 %collective-permute-start.1 = (f32[72,128]{1,0:T(8,128)S(1)}, f32[72,128]{1,0:T(8,128)S(1)}, u32[]{:S(2)}, u32[]{:S(2)}) collective-permute-start(f32[72,128]{1,0:T(8,128)S(1)} %get-tuple-element.17), channel_id=1, source_target_pairs={{0,1},{1,0},{2,3},{3,2},{4,5},{5,4},{6,7},{7,6},{8,9},{9,8},{10,11... | collective-permute-start | bytes 110600 | tf_op jit(solution)/shard_map/ppermute | solution.py:336
  12.5 14.4 %collective-permute-start.7 = (f32[584,128]{1,0:T(8,128)S(1)}, f32[584,128]{1,0:T(8,128)S(1)}, u32[]{:S(2)}, u32[]{:S(2)}) collective-permute-start(f32[584,128]{1,0:T(8,128)S(1)} %collective-permute-done.6.refs_10_), channel_id=1, source_target_pairs={{0,1},{1,0},{2,3},{3,2},{4,5},{5,4},{6,7},{7,6},{8,9},{9,8},{10,11... | collective-permute-start | bytes 897032 | tf_op jit(solution)/shard_map/ppermute | solution.py:336
  12.5 9.6 %copy-start.6 = (f32[3,64]{1,0:T(4,128)S(1)}, f32[3,64]{1,0:T(4,128)}, u32[]{:S(2)}) copy-start(f32[3,64]{1,0:T(4,128)} %out_scale.1) | copy-start | bytes 2308
  12.5 7.0 %collective-permute-start.2 = (f32[144,128]{1,0:T(8,128)S(1)}, f32[144,128]{1,0:T(8,128)S(1)}, u32[]{:S(2)}, u32[]{:S(2)}) collective-permute-start(f32[144,128]{1,0:T(8,128)S(1)} %constant_dynamic-update-slice_fusion.refs_5_), channel_id=1, source_target_pairs={{0,4},{1,13},{2,6},{3,15},{4,8},{5,1},{6,10},{7,3},{8,12},{9,5},{1... | collective-permute-start | bytes 221192 | tf_op jit(solution)/shard_map/ppermute | solution.py:364
  14.4 7.6 %collective-permute-start.4 = (f32[144,128]{1,0:T(8,128)S(1)}, f32[144,128]{1,0:T(8,128)S(1)}, u32[]{:S(2)}, u32[]{:S(2)}) collective-permute-start(f32[144,128]{1,0:T(8,128)S(1)} %constant_dynamic-update-slice_fusion.refs_5_), channel_id=1, source_target_pairs={{0,6},{1,15},{2,4},{3,13},{4,10},{5,3},{6,8},{7,1},{8,14},{9,7},{1... | collective-permute-start | bytes 221192 | tf_op jit(solution)/shard_map/ppermute | solution.py:364
  19.6 7.3 %collective-permute-start.3 = (f32[144,128]{1,0:T(8,128)S(1)}, f32[144,128]{1,0:T(8,128)S(1)}, u32[]{:S(2)}, u32[]{:S(2)}) collective-permute-start(f32[144,128]{1,0:T(8,128)S(1)} %collective-permute-done.2.refs_6_), channel_id=1, source_target_pairs={{0,1},{1,0},{2,3},{3,2},{4,5},{5,4},{6,7},{7,6},{8,9},{9,8},{10,11... | collective-permute-start | bytes 221192 | tf_op jit(solution)/shard_map/ppermute | solution.py:336
  22.1 4.8 %collective-permute-start.5 = (f32[144,128]{1,0:T(8,128)S(1)}, f32[144,128]{1,0:T(8,128)S(1)}, u32[]{:S(2)}, u32[]{:S(2)}) collective-permute-start(f32[144,128]{1,0:T(8,128)S(1)} %collective-permute-done.4.refs_8_), channel_id=1, source_target_pairs={{0,1},{1,0},{2,3},{3,2},{4,5},{5,4},{6,7},{7,6},{8,9},{9,8},{10,11... | collective-permute-start | bytes 221192 | tf_op jit(solution)/shard_map/ppermute | solution.py:336
  22.1 0.7 %copy-start.7 = (f32[2,64]{1,0:T(2,128)S(1)}, f32[2,64]{1,0:T(2,128)}, u32[]{:S(2)}) copy-start(f32[2,64]{1,0:T(2,128)} %courant.1) | copy-start | bytes 1540
  22.1 0.7 %copy-start.8 = (s32[64]{0:T(128)S(1)}, s32[64]{0:T(128)}, u32[]{:S(2)}) copy-start(s32[64]{0:T(128)} %param.18) | copy-start | bytes 772

commit v2 on v1

--- a/solution.py
+++ b/solution.py
@@ -12,6 +12,8 @@
 EXTRA = 8
 F32 = jnp.float32
 BF16 = jnp.bfloat16
+GROUP = 32
+HALF_GROUP = 16
 VMEM_LIMIT = 40 * 1024 * 1024
 
 
@@ -55,18 +57,42 @@
     return east_pack, west_pack
 
 
-def prepare_kernel(tracers, levels, rows, moves, fields, in_scale, storm, balance, features, keep, give, active, *rest):
-    edge_rows, (scratch,) = rest[: len(moves)], rest[len(moves) :]
+def prepare_kernel(tracers, levels, rows, moves, *refs):
+    sources, refs = refs[:7], refs[7:]
+    features, keep, give, active, small = refs[:5]
+    edge_rows, refs = refs[5 : 5 + len(moves)], refs[5 + len(moves) :]
+    (fields, in_scale, storm, balance, *loads), scratch, sems = refs[:7], refs[7], refs[8]
+    part = levels * rows
+    copies = [
+        pltpu.make_async_copy(source, into, sems.at[n])
+        for n, (source, into) in enumerate(zip(sources[1:], (in_scale, storm, balance, *loads)))
+    ]
+    chunks = [
+        pltpu.make_async_copy(
+            sources[0].at[pl.ds(t * part, part)], fields.at[pl.ds(t * part, part)], sems.at[len(copies) + t]
+        )
+        for t in range(tracers)
+    ]
+    for copy in copies + chunks:
+        copy.start()
+    for copy in copies:
+        copy.wait()
+    small[...] = jnp.zeros_like(small)
+    at = 0
+    for load in loads:
+        small[at : at + load.shape[0], : load.shape[1]] = load[...].astype(F32)
+        at += load.shape[0]
     lon, lat, lev = (lax.axis_index(name) for name in ("lon", "lat", "lev"))
-    position = lax.broadcasted_iota(jnp.int32, balance.shape, 1)
-    target = jnp.max(jnp.where(position == lon, balance[...], -1).astype(F32), axis=1, keepdims=True)
-    mask = jnp.where(target >= 0.0, storm[...].astype(F32), 0.0)
+    position = lax.broadcasted_iota(jnp.int32, balance.shape, 0)
+    target = jnp.max(jnp.where(position == lon, balance[...], -1).astype(F32), axis=0, keepdims=True)
+    scales = as_columns(scratch, [in_scale[...], target])
+    mask = jnp.where(column(scales, tracers, rows) >= 0.0, storm[...].astype(F32), 0.0)
     active[...] = mask
-    scales = as_columns(scratch, [in_scale[...]])
     lane = lane_ids(levels)
     edges = []
     scale_lanes = jnp.zeros((levels, LANES), F32)
     for t in range(tracers):
+        chunks[t].wait()
         scale = column(scales, t, levels)
         scale_lanes = jnp.where(lane == 96 + t, scale, scale_lanes)
         pack = jnp.zeros((levels, LANES), F32)
@@ -135,9 +161,8 @@
 OUT_SCALE, LON, LON_SIGN, LAT, LAT_SIGN, EDGE, PLANES = 0, 3, 7, 8, 12, 13, 18
 
 
-def write_weights(weights, scratch, out_scale, courant, substeps, levels):
-    columns = as_columns(scratch, [out_scale[...], courant[...], substeps[...].astype(F32)])
-    tracers = out_scale.shape[0]
+def write_weights(weights, small, tracers, levels):
+    columns = small[...].T
     for t in range(tracers):
         weights[OUT_SCALE + t] = column(columns, t, levels)
     count = column(columns, tracers + 2, levels)
@@ -166,47 +191,47 @@
         weights[LAT + k] = jnp.where(up, w[W - k], w[k])
 
 
-def sweep_lon(q, weights, span):
+def sweep_lon(values, weights, span):
     up = weights[LON_SIGN, span, :] > 0.5
-    q = jnp.where(up, q, turned(q, -W))
-    total = weights[LON, span, :] * q
-    for k in range(1, 4):
-        total += weights[LON + k, span, :] * turned(q, k)
-    return total
-
-
-def own_kernel(
-    tracers, levels, rows, fields, mine, other, w_in, w_mid, w_out, out_scale, courant, substeps, active,
-    swept, weights, x, tendency, scratch,
-):
+    values = [jnp.where(up, q, turned(q, -W)) for q in values]
+    w = [weights[LON + k, span, :] for k in range(4)]
+    return [w[0] * q + w[1] * turned(q, 1) + w[2] * turned(q, 2) + w[3] * turned(q, 3) for q in values]
+
+
+def own_network_kernel(tracers, levels, rows, mine, other, w_in, w_mid, w_out, tendency, token, x):
     lev = lax.axis_index("lev")
     width = tracers * levels
-    write_weights(weights, scratch, out_scale, courant, substeps, levels)
+    token[...] = jnp.zeros_like(token)
     near = pl.ds(pl.multiple_of(lev * width, width), width)
     far = pl.ds(pl.multiple_of((1 - lev) * width, width), width)
     w_last = w_out[near, :]
     for i in range(rows):
         x[near, i * LANES : (i + 1) * LANES] = mine[i]
         x[far, i * LANES : (i + 1) * LANES] = other[i]
-    step = 2 * LANES
-    for j in range(0, rows * LANES, step):
-        tendency[:, j : j + step] = network(x[:, j : j + step], w_in[...], w_mid, w_last)
-    for t in range(tracers):
-        for i in range(rows):
-            for g in range(0, levels, 16):
-                span = slice(g, g + 16)
-                at = t * levels + g
-                q = fields[pl.ds(at * rows + i, 16, stride=rows), :]
-                moist = tendency[at : at + 16, i * LANES : (i + 1) * LANES].astype(F32)
-                q = q + weights[OUT_SCALE + t, span, :] * moist * active[i : i + 1, :]
-                swept[i, at : at + 16, :] = sweep_lon(q, weights, span)
+    tendency[...] = network(x[...], w_in[...], w_mid, w_last)
+
+
+def own_sweep_kernel(tracers, levels, rows, fields, tendency, small, active, swept, weights):
+    write_weights(weights, small, tracers, levels)
+    for g in range(0, levels, GROUP):
+        span = slice(g, g + GROUP)
+        for t in range(tracers):
+            at = t * levels + g
+            scale = weights[OUT_SCALE + t, span, :]
+            values = []
+            for i in range(rows):
+                moist = tendency[at : at + GROUP, i * LANES : (i + 1) * LANES].astype(F32)
+                q = fields[pl.ds(at * rows + i, GROUP, stride=rows), :]
+                values.append(q + scale * moist * active[i : i + 1, :])
+            for i, q in enumerate(sweep_lon(values, weights, span)):
+                swept[i, at : at + GROUP, :] = q
 
 
 def finish_kernel(tracers, levels, rows, moves, *refs):
     count = len(moves)
     swept, weights, w_in, w_mid, w_out, packs, ring, ring_other = refs[:8]
     corner, corner_other, edge, edge_other = (refs[8 + n * count : 8 + (n + 1) * count] for n in range(4))
-    out, x, tendency, halo, mask_rows = refs[8 + 4 * count :]
+    out, x, tendency, halo, mask_rows, fixes, beyond = refs[8 + 4 * count :]
     lat, lev = lax.axis_index("lat"), lax.axis_index("lev")
     width = tracers * levels
     block = levels + EXTRA
@@ -261,70 +286,75 @@
                     value = source[n][(r * tracers + t) * levels : (r * tracers + t + 1) * levels, :]
                     x[to, column_at : column_at + LANES] = (value * scale).astype(BF16)
     mask_rows[...] = unpack(0, 0, slice(levels, block))
-    total = (1 + W * count) * LANES
-    step = 2 * LANES
-    for j in range(0, total, step):
-        stop = min(j + step, total)
-        tendency[:, j:stop] = network(x[:, j:stop], w_in[...], w_mid, w_last)
+    tendency[...] = network(x[...], w_in[...], w_mid, w_last)
 
     tail = W * tracers * levels
-    lane = lane_ids(8)
+    lane = lane_ids(levels)
+    southward = jnp.where(lat == 0, 0.0, 1.0)
+    everything = slice(0, levels)
+    for t in range(tracers):
+        at = t * levels
+        scale = weights[OUT_SCALE + t]
+        up = weights[LAT_SIGN] > 0.5
+
+        def physics(value, column_at, mask):
+            return value + scale * tendency[at : at + levels, column_at : column_at + LANES].astype(F32) * mask
+
+        sides_q = physics(halo[t], 0, mask_rows[0:1, :])
+        if count == 2:
+            sides_q = jnp.where(up | (lane < 48), sides_q, turned(sides_q, -18))
+        fix = weights[EDGE] * sides_q
+        for k, shift in ((1, 1), (2, -1), (3, 2), (4, -2)):
+            fix += weights[EDGE + k] * turned(sides_q, shift)
+        values = []
+        for r in range(W):
+            rows_q = [
+                physics(
+                    edge[n][(r * tracers + t) * levels : (r * tracers + t + 1) * levels, :],
+                    (1 + n * W + r) * LANES,
+                    edge[n][tail + r : tail + r + 1, :],
+                )
+                for n in range(count)
+            ]
+            values.append(jnp.where(up, rows_q[0], rows_q[-1]))
+        values = sweep_lon(values, weights, everything)
+        at_edge = (lane < W) | (lane >= LANES - W)
+        values = [q + jnp.where(at_edge, turned(fix, LANES - W - 48 - 6 * r), 0.0) for r, q in enumerate(values)]
+        if count == 1:
+            values = [jnp.where(weights[LAT_SIGN] == southward, q, 0.0) for q in values]
+        fixes[t] = fix
+        for r, q in enumerate(values):
+            beyond[t * W + r] = q
+
+    lane = lane_ids(HALF_GROUP)
     at_edge = (lane < W) | (lane >= LANES - W)
-    southward = jnp.where(lat == 0, 0.0, 1.0)
-    for t in range(tracers):
-        for g in range(0, levels, 16):
-            span = slice(g, g + 16)
+    for g in range(0, levels, HALF_GROUP):
+        span = slice(g, g + HALF_GROUP)
+        up = weights[LAT_SIGN, span, :] > 0.5
+        w = [weights[LAT + k, span, :] for k in range(4)]
+        for t in range(tracers):
             at = t * levels + g
-            lane = lane_ids(16)
-            at_edge = (lane < W) | (lane >= LANES - W)
-            scale = weights[OUT_SCALE + t, span, :]
-            up = weights[LAT_SIGN, span, :] > 0.5
-
-            def physics(value, column_at, mask):
-                return value + scale * tendency[at : at + 16, column_at : column_at + LANES].astype(F32) * mask
-
-            sides_q = physics(halo[t, span, :], 0, mask_rows[0:1, :])
-            if count == 2:
-                sides_q = jnp.where(up | (lane < 48), sides_q, turned(sides_q, -18))
-            fix = weights[EDGE, span, :] * sides_q
-            for k, shift in ((1, 1), (2, -1), (3, 2), (4, -2)):
-                fix += weights[EDGE + k, span, :] * turned(sides_q, shift)
-
-            def fixed(value, first):
-                return value + jnp.where(at_edge, turned(fix, LANES - W - first), 0.0)
-
-            beyond = []
-            for r in range(W):
-                rows_q = [
-                    physics(
-                        edge[n][(r * tracers + t) * levels + g : (r * tracers + t) * levels + g + 16, :],
-                        (1 + n * W + r) * LANES,
-                        edge[n][tail + r : tail + r + 1, :],
-                    )
-                    for n in range(count)
-                ]
-                q = jnp.where(up, rows_q[0], rows_q[-1])
-                q = fixed(sweep_lon(q, weights, span), 48 + 6 * r)
-                if count == 1:
-                    q = jnp.where(weights[LAT_SIGN, span, :] == southward, q, 0.0)
-                beyond.append(q)
-            inner = [fixed(swept[i, at : at + 16, :], 6 * i) for i in range(rows)]
+            fix = fixes[t, span, :]
+            inner = [
+                swept[i, at : at + HALF_GROUP, :] + jnp.where(at_edge, turned(fix, LANES - W - 6 * i), 0.0)
+                for i in range(rows)
+            ]
+            outer = [beyond[t * W + r, span, :] for r in range(W)]
             line = []
             for i in range(rows + W):
-                above = beyond[i] if i < W else inner[i - W]
-                below = inner[i] if i < rows else beyond[i - rows]
+                above = outer[i] if i < W else inner[i - W]
+                below = inner[i] if i < rows else outer[i - rows]
                 line.append(jnp.where(up, above, below))
-            for i in range(rows):
-                value = weights[LAT, span, :] * line[i]
-                for k in range(1, 4):
-                    value += weights[LAT + k, span, :] * line[i + k]
-                out[pl.ds(at * rows + i, 16, stride=rows), :] = value
-
-
-def call(kernel, out_shape, scratch, flops, moved, name):
+            results = [w[0] * line[i] + w[1] * line[i + 1] + w[2] * line[i + 2] + w[3] * line[i + 3] for i in range(rows)]
+            for i, value in enumerate(results):
+                out[pl.ds(at * rows + i, HALF_GROUP, stride=rows), :] = value
+
+
+def call(kernel, out_shape, scratch, flops, moved, name, **specs):
     return pl.pallas_call(
         kernel,
         out_shape=out_shape,
+        **specs,
         scratch_shapes=scratch,
         compiler_params=pltpu.CompilerParams(vmem_limit_bytes=VMEM_LIMIT),
         cost_estimate=pl.CostEstimate(flops=flops, bytes_accessed=moved, transcendentals=0),
@@ -373,13 +403,17 @@
     block = levels + EXTRA
     edge_shape = jax.ShapeDtypeStruct((W * width + EXTRA, columns), F32)
     pack_shape = jax.ShapeDtypeStruct((block, LANES), F32)
-    features, keep, give, active, *edge_rows = call(
+    inputs = (flat, in_scale, storm_mask, balance.T, out_scale, courant, substeps.reshape(1, levels))
+    inputs = [pltpu.with_memory_space_constraint(x, pltpu.HBM) for x in inputs]
+    features, keep, give, active, small, *edge_rows = call(
         functools.partial(prepare_kernel, tracers, levels, rows, moves),
         [jax.ShapeDtypeStruct((rows, width, columns), BF16), pack_shape, pack_shape,
-         jax.ShapeDtypeStruct((rows, columns), F32)] + [edge_shape] * count,
-        [pltpu.VMEM((8, LANES), F32)],
+         jax.ShapeDtypeStruct((rows, columns), F32), jax.ShapeDtypeStruct((8, LANES), F32)] + [edge_shape] * count,
+        [pltpu.VMEM(x.shape, x.dtype) for x in inputs]
+        + [pltpu.VMEM((8, LANES), F32), pltpu.SemaphoreType.DMA((len(inputs) - 1 + tracers,))],
         10**6, 2 * 10**6, "prepare",
-    )(flat, in_scale, storm_mask, balance)
+        in_specs=[pl.BlockSpec(memory_space=pltpu.HBM)] * len(inputs),
+    )(*inputs)
 
     given = swap_cores(give)
     features_other = swap_cores(features)
@@ -388,23 +422,29 @@
     corner = [send(packs, move, True) for move in moves]
     ring = send(packs, None, True)
 
+    tendency, token = call(
+        functools.partial(own_network_kernel, tracers, levels, rows),
+        [jax.ShapeDtypeStruct((width, rows * columns), BF16), jax.ShapeDtypeStruct((8, LANES), F32)],
+        [pltpu.VMEM((2 * width, rows * columns), BF16)],
+        2 * 10**9, 8 * 10**6, "own_network",
+    )(features, features_other, w_in, w_mid, w_out)
     swept, weights = call(
-        functools.partial(own_kernel, tracers, levels, rows),
+        functools.partial(own_sweep_kernel, tracers, levels, rows),
         [jax.ShapeDtypeStruct((rows, width, columns), F32), jax.ShapeDtypeStruct((PLANES, levels, LANES), F32)],
-        [pltpu.VMEM((2 * width, rows * columns), BF16), pltpu.VMEM((width, rows * columns), BF16),
-         pltpu.VMEM((8, LANES), F32)],
-        10**9, 4 * 10**6, "own_columns",
-    )(flat, features, features_other, w_in, w_mid, w_out, out_scale, courant, substeps.reshape(1, levels), active)
-
-    ring_other = swap_cores(ring)
-    corner_other = [swap_cores(c) for c in corner]
+        [],
+        10**9, 4 * 10**6, "own_sweep",
+    )(flat, tendency, small, active)
+
+    forwarded = swap_cores(jnp.concatenate([ring, *corner], axis=0) + token[:1])
+    ring_other, *corner_other = jnp.split(forwarded, count + 1, axis=0)
     edge_other = [swap_cores(e) for e in edge]
     total = (1 + W * count) * LANES
     out = call(
         functools.partial(finish_kernel, tracers, levels, rows, moves),
         jax.ShapeDtypeStruct((width * rows, columns), F32),
         [pltpu.VMEM((2 * width, total), BF16), pltpu.VMEM((width, total), BF16),
-         pltpu.VMEM((tracers, levels, LANES), F32), pltpu.VMEM((EXTRA, LANES), F32)],
+         pltpu.VMEM((tracers, levels, LANES), F32), pltpu.VMEM((EXTRA, LANES), F32),
+         pltpu.VMEM((tracers, levels, LANES), F32), pltpu.VMEM((tracers * W, levels, LANES), F32)],
         10**9, 4 * 10**6, "finish",
     )(swept, weights, w_in, w_mid, w_out, packs, ring, ring_other, *corner, *corner_other, *edge, *edge_other)
     return out.reshape(fields.shape)

time: 30.6 us -> 19.3 us (0.63)
  waiting for transfers between devices: 11.7 us -> 3.34 us
  local copies, waits for them, and re-layouts: 2.58 us -> 0.04 us
  Pallas kernels: 8.08 us -> 7.74 us
    ppermute x3, waiting for transfers between devices: 11.7 us -> 3.33 us  [send(): return lax.ppermute(x, axes, pairs)]
    unnamed x20 -> x9, local copies, waits for them, and re-layouts: 2.58 us -> 0.02 us
    pallas_call x1 -> x2, Pallas kernels: 4.12 us -> 2.79 us  [the longest x1 1.51 us: on_device(): call(functools.partial(own_network_kernel, tracers, levels, rows), [jax.S...]
    pallas_call x1, Pallas kernels: 0.47 us -> 1.77 us  [on_device(): call(functools.partial(prepare_kernel, tracers, levels, rows, moves), [ja...]
    ppermute x5 -> x4, starting transfers between devices: 0.52 us -> 1.18 us  [swap_cores(): return lax.ppermute(x, 'lev', [(0, 1), (1, 0)])]
    ppermute x3, starting transfers between devices: 7.39 us -> 6.75 us  [send(): return lax.ppermute(x, axes, pairs)]
  transfers between devices with their start and end apart: 8 -> 7, of which waited for: 3 -> 2; matrix products, arithmetic and copies ran while one was open for 0% -> 0% of each run, Pallas kernels for 14% -> 15%
where the time goes in v2:
time: 19.3 us; the launch traced here: 19.1 us
  starting transfers between devices  7.93 us (41%)
  Pallas kernels  7.74 us (40%)
  waiting for transfers between devices  3.34 us (17%)
    ppermute x3, starting transfers between devices, send(): return lax.ppermute(x, axes, pairs)  6.75 us
    ppermute x3, waiting for transfers between devices, send(): return lax.ppermute(x, axes, pairs)  3.33 us
    pallas_call x1, Pallas kernels, on_device(): call(functools.partial(finish_kernel, tracers, levels, rows, moves), jax....  3.19 us
    pallas_call x1, Pallas kernels, on_device(): call(functools.partial(prepare_kernel, tracers, levels, rows, moves), [ja...  1.77 us
    pallas_call x1, Pallas kernels, on_device(): call(functools.partial(own_network_kernel, tracers, levels, rows), [jax.S...  1.51 us
    pallas_call x1, Pallas kernels, on_device(): call(functools.partial(own_sweep_kernel, tracers, levels, rows), [jax.Sha...  1.28 us
    ppermute x4, starting transfers between devices, swap_cores(): return lax.ppermute(x, 'lev', [(0, 1), (1, 0)])  1.18 us
  transfers between devices with their start and end apart: 7, of which 2 were waited for; matrix products, arithmetic and copies ran while one was open for 0% of the time, Pallas kernels for 15%

profile of v2, /device:TPU:0, one launch (start us, length us, event | category | flops | bytes accessed | tf_op | source)
XLA Modules:
  0.0 19.1 jit_solution(5777282493134843917)
XLA Ops:
  0.0 0.0 copy-start.1
  0.0 0.0 copy-start.2
  0.0 0.0 copy-start.3
  0.0 1.8 %prepare.1 = (bf16[8,192,128]{2,1,0:T(8,128)(2,1)S(1)}, f32[72,128]{1,0:T(8,128)S(1)}, f32[72,128]{1,0:T(8,128)S(1)}, f32[8,128]{1,0:T(8,128)S(1)}, f32[8,128]{1,0:T(8,128)S(1)}, /*index=5*/f32[584,128]{1,0:T(8,128)S(1)}) custom-call(f32[1536,128]{1,0:T(8,128)} %bitcast.6, f32[3,64]{1,0:T(4,128)} %refs_1_.1, s32[8,128]{1,0:T(8,128)} %refs_2_.2, ...), custom_call_target="tpu_custom_call" | custom-call | flops 1000000 | bytes 2000000 | tf_op jit(solution)/shard_map/prepare/pallas_call | solution.py:408
  1.8 0.5 %collective-permute-start = (bf16[8,192,128]{2,1,0:T(8,128)(2,1)S(1)}, bf16[8,192,128]{2,1,0:T(8,128)(2,1)S(1)}, u32[]{:S(2)}, u32[]{:S(2)}) collective-permute-start(bf16[8,192,128]{2,1,0:T(8,128)(2,1)S(1)} %get-tuple-element.15.mine), channel_id=1, source_target_pairs={{0,1},{1,0},{2,3},{3,2},{4,5},{5,4},{6,7},{7,6},{8,9},{9,8},{10,11... | collective-permute-start | bytes 1179656 | tf_op jit(solution)/shard_map/ppermute | solution.py:366
  2.3 0.1 collective-permute-start.1
  2.4 2.9 %collective-permute-start.5 = (f32[584,128]{1,0:T(8,128)S(1)}, f32[584,128]{1,0:T(8,128)S(1)}, u32[]{:S(2)}, u32[]{:S(2)}) collective-permute-start(f32[584,128]{1,0:T(8,128)S(1)} %get-tuple-element.24), channel_id=1, source_target_pairs={{0,2},{1,3},{2,0},{3,1},{4,6},{5,7},{6,4},{7,5},{8,10},{9,11},{10,... | collective-permute-start | bytes 897032 | tf_op jit(solution)/shard_map/ppermute | solution.py:394
  5.3 0.0 collective-permute-done.1
  5.3 0.0 copy-start
  5.3 2.3 %collective-permute-start.3 = (f32[144,128]{1,0:T(8,128)S(1)}, f32[144,128]{1,0:T(8,128)S(1)}, u32[]{:S(2)}, u32[]{:S(2)}) collective-permute-start(f32[144,128]{1,0:T(8,128)S(1)} %constant_dynamic-update-slice_fusion.refs_5_), channel_id=1, source_target_pairs={{0,6},{1,15},{2,4},{3,13},{4,10},{5,3},{6,8},{7,1},{8,14},{9,7},{1... | collective-permute-start | bytes 221192 | tf_op jit(solution)/shard_map/ppermute | solution.py:394
  7.6 1.6 %collective-permute-start.2 = (f32[144,128]{1,0:T(8,128)S(1)}, f32[144,128]{1,0:T(8,128)S(1)}, u32[]{:S(2)}, u32[]{:S(2)}) collective-permute-start(f32[144,128]{1,0:T(8,128)S(1)} %constant_dynamic-update-slice_fusion.refs_5_), channel_id=1, source_target_pairs={{0,4},{1,13},{2,6},{3,15},{4,8},{5,1},{6,10},{7,3},{8,12},{9,5},{1... | collective-permute-start | bytes 221192 | tf_op jit(solution)/shard_map/ppermute | solution.py:394
  9.2 0.0 collective-permute-done.other
  9.2 0.0 copy-done.1
  9.2 0.0 copy-done.2
  9.2 0.0 copy-done.3
  9.2 1.5 %own_network.1 = (bf16[192,1024]{1,0:T(8,128)(2,1)S(1)}, f32[8,128]{1,0:T(8,128)S(1)}) custom-call(bf16[8,192,128]{2,1,0:T(8,128)(2,1)S(1)} %get-tuple-element.15.mine, bf16[8,192,128]{2,1,0:T(8,128)(2,1)S(1)} %collective-permute-done.other, bf16[256,384]{1,0:T(8,128)(2,1)S(1)} %copy-done.2, bf16[3,256,256]{2,1,0:T(8,128)(2,1)S(1)} %copy-done.1, ...), custom_call_target="tpu_custom_call" | custom-call | flops 2000000000 | bytes 8000000 | tf_op jit(solution)/shard_map/own_network/pallas_call | solution.py:425
  10.7 2.5 %collective-permute-done.3.refs_8_ = f32[144,128]{1,0:T(8,128)S(1)} collective-permute-done((f32[144,128]{1,0:T(8,128)S(1)}, f32[144,128]{1,0:T(8,128)S(1)}, u32[]{:S(2)}, u32[]{:S(2)}) %collective-permute-start.3) | collective-permute-done | bytes 73760 | tf_op jit(solution)/shard_map/ppermute | solution.py:394
  13.2 0.8 %collective-permute-done.2.refs_6_ = f32[144,128]{1,0:T(8,128)S(1)} collective-permute-done((f32[144,128]{1,0:T(8,128)S(1)}, f32[144,128]{1,0:T(8,128)S(1)}, u32[]{:S(2)}, u32[]{:S(2)}) %collective-permute-start.2) | collective-permute-done | bytes 73760 | tf_op jit(solution)/shard_map/ppermute | solution.py:394
  14.0 0.2 %collective-permute-start.4 = (f32[288,128]{1,0:T(8,128)S(1)}, f32[288,128]{1,0:T(8,128)S(1)}, u32[]{:S(2)}, u32[]{:S(2)}) collective-permute-start(f32[288,128]{1,0:T(8,128)S(1)} %maximum_add_fusion), channel_id=1, source_target_pairs={{0,1},{1,0},{2,3},{3,2},{4,5},{5,4},{6,7},{7,6},{8,9},{9,8},{10,11... | collective-permute-start | bytes 442376 | tf_op jit(solution)/shard_map/ppermute | solution.py:366
  14.3 0.0 collective-permute-done.5.refs_10_
  14.3 0.4 %collective-permute-start.6 = (f32[584,128]{1,0:T(8,128)S(1)}, f32[584,128]{1,0:T(8,128)S(1)}, u32[]{:S(2)}, u32[]{:S(2)}) collective-permute-start(f32[584,128]{1,0:T(8,128)S(1)} %collective-permute-done.5.refs_10_), channel_id=1, source_target_pairs={{0,1},{1,0},{2,3},{3,2},{4,5},{5,4},{6,7},{7,6},{8,9},{9,8},{10,11... | collective-permute-start | bytes 897032 | tf_op jit(solution)/shard_map/ppermute | solution.py:366
  14.6 0.0 copy-done
  14.6 1.3 %own_sweep.1 = (f32[8,192,128]{2,1,0:T(8,128)S(1)}, f32[18,64,128]{2,1,0:T(8,128)S(1)}) custom-call(f32[1536,128]{1,0:T(8,128)S(1)} %bitcast.7, bf16[192,1024]{1,0:T(8,128)(2,1)S(1)} %get-tuple-element.16.tendency, f32[8,128]{1,0:T(8,128)S(1)} %get-tuple-element.17.small, f32[8,128]{1,0:T(8,128)S(1)} %get-tuple-element.18.active), custom_call_target="tpu_custom_call" | custom-call | flops 1000000000 | bytes 4000000 | tf_op jit(solution)/shard_map/own_sweep/pallas_call | solution.py:431
  15.9 0.0 collective-permute-done.4
  15.9 0.0 collective-permute-done.6.refs_11_
  16.0 3.2 %finish.1 = f32[1536,128]{1,0:T(8,128)} custom-call(f32[8,192,128]{2,1,0:T(8,128)S(1)} %get-tuple-element.19.refs_0_, f32[18,64,128]{2,1,0:T(8,128)S(1)} %get-tuple-element.20.refs_1_, bf16[256,384]{1,0:T(8,128)(2,1)S(1)} %copy-done.2, bf16[3,256,256]{2,1,0:T(8,128)(2,1)S(1)} %copy-done.1, bf16[384,256]{1,0:T(8,128)(2,1)S(1)} %copy-done.3, ...), custom_call_target="tpu_custom_call" | custom-call | flops 1000000000 | bytes 4000000 | tf_op jit(solution)/shard_map/finish/pallas_call | solution.py:442
  (5 shorter events, 0.0 us)
Async XLA Ops:
  0.0 9.2 %copy-start.1 = (bf16[3,256,256]{2,1,0:T(8,128)(2,1)S(1)}, bf16[3,256,256]{2,1,0:T(8,128)(2,1)}, u32[]{:S(2)}) copy-start(bf16[3,256,256]{2,1,0:T(8,128)(2,1)} %refs_3_.1) | copy-start | bytes 1179652
  0.0 9.2 %copy-start.2 = (bf16[256,384]{1,0:T(8,128)(2,1)S(1)}, bf16[256,384]{1,0:T(8,128)(2,1)}, u32[]{:S(2)}) copy-start(bf16[256,384]{1,0:T(8,128)(2,1)} %refs_2_.3) | copy-start | bytes 589828
  0.0 9.2 %copy-start.3 = (bf16[384,256]{1,0:T(8,128)(2,1)S(1)}, bf16[384,256]{1,0:T(8,128)(2,1)}, u32[]{:S(2)}) copy-start(bf16[384,256]{1,0:T(8,128)(2,1)} %refs_4_.3) | copy-start | bytes 589828
  1.8 7.4 %collective-permute-start = (bf16[8,192,128]{2,1,0:T(8,128)(2,1)S(1)}, bf16[8,192,128]{2,1,0:T(8,128)(2,1)S(1)}, u32[]{:S(2)}, u32[]{:S(2)}) collective-permute-start(bf16[8,192,128]{2,1,0:T(8,128)(2,1)S(1)} %get-tuple-element.15.mine), channel_id=1, source_target_pairs={{0,1},{1,0},{2,3},{3,2},{4,5},{5,4},{6,7},{7,6},{8,9},{9,8},{10,11... | collective-permute-start | bytes 1179656 | tf_op jit(solution)/shard_map/ppermute | solution.py:366
  2.3 3.0 %collective-permute-start.1 = (f32[72,128]{1,0:T(8,128)S(1)}, f32[72,128]{1,0:T(8,128)S(1)}, u32[]{:S(2)}, u32[]{:S(2)}) collective-permute-start(f32[72,128]{1,0:T(8,128)S(1)} %get-tuple-element.22), channel_id=1, source_target_pairs={{0,1},{1,0},{2,3},{3,2},{4,5},{5,4},{6,7},{7,6},{8,9},{9,8},{10,11... | collective-permute-start | bytes 110600 | tf_op jit(solution)/shard_map/ppermute | solution.py:366
  2.4 11.9 %collective-permute-start.5 = (f32[584,128]{1,0:T(8,128)S(1)}, f32[584,128]{1,0:T(8,128)S(1)}, u32[]{:S(2)}, u32[]{:S(2)}) collective-permute-start(f32[584,128]{1,0:T(8,128)S(1)} %get-tuple-element.24), channel_id=1, source_target_pairs={{0,2},{1,3},{2,0},{3,1},{4,6},{5,7},{6,4},{7,5},{8,10},{9,11},{10,... | collective-permute-start | bytes 897032 | tf_op jit(solution)/shard_map/ppermute | solution.py:394
  5.3 9.3 %copy-start = (f32[3,64,8,128]{3,2,1,0:T(8,128)S(1)}, f32[3,64,8,128]{3,2,1,0:T(8,128)}, u32[]{:S(2)}) copy-start(f32[3,64,8,128]{3,2,1,0:T(8,128)} %param.10) | copy-start | bytes 2359300
  5.3 7.9 %collective-permute-start.3 = (f32[144,128]{1,0:T(8,128)S(1)}, f32[144,128]{1,0:T(8,128)S(1)}, u32[]{:S(2)}, u32[]{:S(2)}) collective-permute-start(f32[144,128]{1,0:T(8,128)S(1)} %constant_dynamic-update-slice_fusion.refs_5_), channel_id=1, source_target_pairs={{0,6},{1,15},{2,4},{3,13},{4,10},{5,3},{6,8},{7,1},{8,14},{9,7},{1... | collective-permute-start | bytes 221192 | tf_op jit(solution)/shard_map/ppermute | solution.py:394
  7.6 6.4 %collective-permute-start.2 = (f32[144,128]{1,0:T(8,128)S(1)}, f32[144,128]{1,0:T(8,128)S(1)}, u32[]{:S(2)}, u32[]{:S(2)}) collective-permute-start(f32[144,128]{1,0:T(8,128)S(1)} %constant_dynamic-update-slice_fusion.refs_5_), channel_id=1, source_target_pairs={{0,4},{1,13},{2,6},{3,15},{4,8},{5,1},{6,10},{7,3},{8,12},{9,5},{1... | collective-permute-start | bytes 221192 | tf_op jit(solution)/shard_map/ppermute | solution.py:394
  14.0 1.9 %collective-permute-start.4 = (f32[288,128]{1,0:T(8,128)S(1)}, f32[288,128]{1,0:T(8,128)S(1)}, u32[]{:S(2)}, u32[]{:S(2)}) collective-permute-start(f32[288,128]{1,0:T(8,128)S(1)} %maximum_add_fusion), channel_id=1, source_target_pairs={{0,1},{1,0},{2,3},{3,2},{4,5},{5,4},{6,7},{7,6},{8,9},{9,8},{10,11... | collective-permute-start | bytes 442376 | tf_op jit(solution)/shard_map/ppermute | solution.py:366
  14.3 1.7 %collective-permute-start.6 = (f32[584,128]{1,0:T(8,128)S(1)}, f32[584,128]{1,0:T(8,128)S(1)}, u32[]{:S(2)}, u32[]{:S(2)}) collective-permute-start(f32[584,128]{1,0:T(8,128)S(1)} %collective-permute-done.5.refs_10_), channel_id=1, source_target_pairs={{0,1},{1,0},{2,3},{3,2},{4,5},{5,4},{6,7},{7,6},{8,9},{9,8},{10,11... | collective-permute-start | bytes 897032 | tf_op jit(solution)/shard_map/ppermute | solution.py:366

commit v3 on v2

v3 whole, which is shorter than its diff:
```python
import functools

import jax
import jax.numpy as jnp
from jax import lax
from jax.experimental import pallas as pl
from jax.experimental.pallas import tpu as pltpu
from jax.sharding import PartitionSpec as P

W = 3
LANES = 128
SCALE_LANE = 96
FIELD_BOUND = 8.0
FIXED_ONE = 32768.0 / FIELD_BOUND
FIXED_MOST = 32767.0
EXTRA = 8
F32 = jnp.float32
BF16 = jnp.bfloat16
GROUP = 32
HALF_GROUP = 16
VMEM_LIMIT = 40 * 1024 * 1024


def lane_ids(rows):
    return lax.broadcasted_iota(jnp.int32, (rows, LANES), 1)


def turned(x, shift):
    if isinstance(shift, int):
        shift %= LANES
        if shift == 0:
            return x
    return pltpu.roll(x, shift, 1)


def silu(v):
    half = 0.5 * v
    return half + half * jnp.tanh(half)


def as_columns(scratch, parts):
    scratch[...] = jnp.zeros_like(scratch)
    at = 0
    for part in parts:
        scratch[at : at + part.shape[0], : part.shape[1]] = part
        at += part.shape[0]
    return scratch[...].T


def column(turned_rows, index, levels):
    return jnp.broadcast_to(turned_rows[:levels, index : index + 1], (levels, LANES))


def side_packs(edges):
    lane = lane_ids(edges[0].shape[0])
    east = lane % 6 < 3
    last = [jnp.where(east, e, 0.0) for e in edges]
    first = [jnp.where(east, 0.0, e) for e in edges]
    east_pack = last[0] + turned(last[1], 3) + turned(last[2], 48)
    west_pack = turned(first[0], -3) + first[1] + turned(first[2], 45)
    return east_pack, west_pack


def edge_kernel(tracers, levels, rows, *refs):
    sources, (keep, give, active, small, features), refs = refs[:7], refs[7:12], refs[12:]
    (fields, in_scale, storm, balance, *loads), scratch, sems = refs[:7], refs[7], refs[8]
    part = levels * rows
    chunks = [
        pltpu.make_async_copy(sources[0].at[pl.ds(t * part, part)], fields.at[pl.ds(t * part, part)], sems.at[t])
        for t in range(tracers)
    ]
    copies = [
        pltpu.make_async_copy(source, into, sems.at[tracers + n])
        for n, (source, into) in enumerate(zip(sources[1:], (in_scale, storm, balance, *loads)))
    ]
    for copy in copies + chunks:
        copy.start()
    for copy in copies:
        copy.wait()
    small[...] = jnp.zeros_like(small)
    at = 0
    for load in loads:
        small[at : at + load.shape[0], : load.shape[1]] = load[...].astype(F32)
        at += load.shape[0]
    lon, lev = lax.axis_index("lon"), lax.axis_index("lev")
    position = lax.broadcasted_iota(jnp.int32, balance.shape, 0)
    target = jnp.max(jnp.where(position == lon, balance[...], -1).astype(F32), axis=0, keepdims=True)
    scales = as_columns(scratch, [in_scale[...], loads[0][...], target])
    mask = jnp.where(column(scales, 2 * tracers, rows) >= 0.0, storm[...].astype(F32), 0.0)
    active[...] = mask
    lane = lane_ids(levels)
    scale_lanes = jnp.zeros((levels, LANES), F32)
    for n in range(2 * tracers):
        scale_lanes = jnp.where(lane == SCALE_LANE + n, column(scales, n, levels), scale_lanes)
    lane = lane_ids(1)
    mask_pack = jnp.zeros((1, LANES), F32)
    for i in range(rows):
        mask_pack = jnp.where((lane >= 6 * i) & (lane < 6 * i + 6), turned(active[i : i + 1, :], 6 * i + W), mask_pack)
    mask_pack = jnp.broadcast_to(mask_pack, (EXTRA, LANES))
    none = jnp.zeros_like(mask_pack)
    last_mask, first_mask = side_packs([mask_pack, none, none])
    lane = lane_ids(levels)
    edges = []
    for t in range(tracers):
        chunks[t].wait()
        scale = column(scales, t, levels)
        pack = jnp.zeros((levels, LANES), F32)
        for i in range(rows):
            x = fields[pl.ds(t * part + i, levels, stride=rows), :]
            features[i, t * levels : (t + 1) * levels, :] = (x * scale).astype(BF16)
            pack = jnp.where((lane >= 6 * i) & (lane < 6 * i + 6), turned(x, 6 * i + W), pack)
        edges.append(pack)
    last_pack, first_pack = side_packs(edges)
    head = lev == 0
    keep[:levels] = jnp.where(head, last_pack, first_pack) + scale_lanes
    give[:levels] = jnp.where(head, first_pack, last_pack) + scale_lanes
    keep[levels:] = jnp.where(head, last_mask, first_mask)
    give[levels:] = jnp.where(head, first_mask, last_mask)


def binary_scale(largest):
    largest = largest * (1.0 / FIELD_BOUND)
    power, scale = jnp.zeros_like(largest), jnp.ones_like(largest)
    for bits in (64, 32, 16, 8, 4, 2, 1):
        small = largest < 2.0**-bits
        largest = jnp.where(small, largest * 2.0**bits, largest)
        scale = jnp.where(small, scale * 2.0**bits, scale)
        power = jnp.where(small, power + float(bits), power)
    return scale, power


def inverse_scale(power):
    scale = jnp.ones_like(power)
    for bits in (64, 32, 16, 8, 4, 2, 1):
        large = power > bits - 0.5
        scale = jnp.where(large, scale * 2.0**-bits, scale)
        power = jnp.where(large, power - float(bits), power)
    return scale


def to_fixed(x):
    return jnp.round(x).astype(jnp.int32).astype(jnp.int16)


def from_fixed(x):
    return x.astype(jnp.int32).astype(F32)


def row_message_kernel(tracers, levels, rows, moves, fields, active, *edge_rows):
    lat = lax.axis_index("lat")
    lane = lane_ids(levels)
    row = lax.broadcasted_iota(jnp.int32, (2 * EXTRA, LANES), 0)
    tail = W * tracers * levels
    for move, out in zip(moves, edge_rows):
        start = first_row_sent(move, lat, rows)
        values = [
            [fields[pl.ds((t * levels) * rows + start + r, levels, stride=rows), :] for r in range(W)]
            for t in range(tracers)
        ]
        largest = [jnp.max(jnp.maximum(jnp.maximum(jnp.abs(a), jnp.abs(b)), jnp.abs(c)), axis=1, keepdims=True) for a, b, c in values]
        bound = jnp.zeros((levels, LANES), F32)
        for t in range(tracers):
            bound = jnp.where(lane == t, largest[t], bound)
        scale, power = binary_scale(bound)
        for t in range(tracers):
            to_one = jnp.broadcast_to(scale[:, t : t + 1], (levels, LANES))
            for r, x in enumerate(values[t]):
                x = jnp.clip(x * to_one * FIXED_ONE, -FIXED_MOST, FIXED_MOST)
                out[(r * tracers + t) * levels : (r * tracers + t + 1) * levels, :] = to_fixed(x)
        out[tail : tail + levels, :] = to_fixed(power)
        mask = jnp.zeros(row.shape, F32)
        for r in range(W):
            mask = jnp.where(row == r, active[pl.ds(start + r, 1), :], mask)
        out[tail + levels :, :] = to_fixed(mask)


def first_row_sent(move, lat, rows):
    if move == 0:
        return jnp.where(lat == 0, rows - W, 0)
    return rows - W if move > 0 else 0


def first_row_received(move, lat, rows):
    if move == 0:
        return jnp.where(lat == 0, 0, rows - W)
    return rows - W if move > 0 else 0


def network(x, w_in, w_mid, w_last):
    hidden = silu(jnp.dot(w_in, x, preferred_element_type=F32)).astype(BF16)
    for layer in range(len(w_mid)):
        hidden = silu(jnp.dot(w_mid[layer], hidden, preferred_element_type=F32)).astype(BF16)
    return jnp.dot(w_last, hidden, preferred_element_type=F32).astype(BF16)


def taps(step, count):
    first = jnp.abs(step)
    second = jnp.where(count > 1.5, first, 0.0)
    third = jnp.where(count > 2.5, first, 0.0)
    rest = [1.0 - a for a in (first, second, third)]
    return (
        rest[0] * rest[1] * rest[2],
        first * rest[1] * rest[2] + rest[0] * second * rest[2] + rest[0] * rest[1] * third,
        first * second * rest[2] + first * rest[1] * third + rest[0] * second * third,
        first * second * third,
    )


def narrow_network(x, w_in, w_mid, w_last):
    def layer(hidden, w):
        return lax.dot_general(hidden, w, (((1,), (1,)), ((), ())), preferred_element_type=F32)

    hidden = silu(lax.dot_general(x, w_in, (((0,), (1,)), ((), ())), preferred_element_type=F32)).astype(BF16)
    for k in range(len(w_mid)):
        hidden = silu(layer(hidden, w_mid[k])).astype(BF16)
    return layer(w_last, hidden).astype(BF16)


OUT_SCALE, LON, LON_SIGN, LAT, LAT_SIGN, EDGE, PLANES = 0, 3, 7, 8, 12, 13, 18


def write_weights(weights, small, tracers, levels):
    columns = small[...].T
    for t in range(tracers):
        weights[OUT_SCALE + t] = column(columns, t, levels)
    count = column(columns, tracers + 2, levels)
    lane = lane_ids(levels)
    place = lane % 6
    step = column(columns, tracers, levels) / count
    up = step > 0.0
    w = taps(step, count)
    weights[LON_SIGN] = jnp.where(up, 1.0, 0.0)
    for k in range(4):
        weights[LON + k] = jnp.where(
            up, jnp.where(lane >= k, w[k], 0.0), jnp.where(lane < LANES - (W - k), w[W - k], 0.0)
        )
    east = [jnp.where(up | (place > 2) | (place < d), 0.0, w[W - d]) for d in range(3)]
    west = [jnp.where(up & (place > 2) & (place + d < 6), w[W - d], 0.0) for d in range(3)]
    weights[EDGE] = east[0] + west[0]
    weights[EDGE + 1] = east[1]
    weights[EDGE + 2] = west[1]
    weights[EDGE + 3] = east[2]
    weights[EDGE + 4] = west[2]
    step = column(columns, tracers + 1, levels) / count
    up = step > 0.0
    w = taps(step, count)
    weights[LAT_SIGN] = jnp.where(up, 1.0, 0.0)
    for k in range(4):
        weights[LAT + k] = jnp.where(up, w[W - k], w[k])


def sweep_lon(values, weights, span):
    up = weights[LON_SIGN, span, :] > 0.5
    values = [jnp.where(up, q, turned(q, -W)) for q in values]
    w = [weights[LON + k, span, :] for k in range(4)]
    return [w[0] * q + w[1] * turned(q, 1) + w[2] * turned(q, 2) + w[3] * turned(q, 3) for q in values]


def own_network_kernel(tracers, levels, rows, mine, other, w_in, w_mid, w_out, tendency, x):
    lev = lax.axis_index("lev")
    width = tracers * levels
    near = pl.ds(pl.multiple_of(lev * width, width), width)
    far = pl.ds(pl.multiple_of((1 - lev) * width, width), width)
    w_last = w_out[near, :]
    for i in range(rows):
        x[near, i * LANES : (i + 1) * LANES] = mine[i]
        x[far, i * LANES : (i + 1) * LANES] = other[i]
    tendency[...] = network(x[...], w_in[...], w_mid, w_last)


def own_sweep_kernel(tracers, levels, rows, fields, tendency, small, active, swept, weights, token):
    token[...] = jnp.zeros_like(token)
    write_weights(weights, small, tracers, levels)
    for g in range(0, levels, GROUP):
        span = slice(g, g + GROUP)
        for t in range(tracers):
            at = t * levels + g
            scale = weights[OUT_SCALE + t, span, :]
            values = []
            for i in range(rows):
                moist = tendency[at : at + GROUP, i * LANES : (i + 1) * LANES].astype(F32)
                q = fields[pl.ds(at * rows + i, GROUP, stride=rows), :]
                values.append(q + scale * moist * active[i : i + 1, :])
            for i, q in enumerate(sweep_lon(values, weights, span)):
                swept[i, at : at + GROUP, :] = q


def edge_network_kernel(tracers, levels, rows, moves, ring, *refs):
    count = len(moves)
    corner, (weights, w_in, w_mid, w_out, mine, other, x) = refs[:count], refs[count:]
    lat, lev = lax.axis_index("lat"), lax.axis_index("lev")
    width = tracers * levels
    block = levels + EXTRA
    head = lev == 0
    lane = lane_ids(levels)
    west = (lane % 6 >= 3) == head
    shifts = [jnp.where(head, a, b) for a, b in ((W, 0), (0, LANES - W), (LANES - 48 + W, LANES - 48))]

    def unpack(t, part):
        value = turned(ring[part, :], shifts[t])
        lane_part = lane[: value.shape[0]]
        used = lane_part < 48
        for n, move in enumerate(moves):
            base = 48 + 18 * n
            shift = shifts[t] + (base - 6 * first_row_received(move, lat, rows))
            shift = jnp.where(shift < 0, shift + LANES, jnp.where(shift >= LANES, shift - LANES, shift))
            here = (lane_part >= base) & (lane_part < base + 18)
            value = jnp.where(here, turned(corner[n][part, :], shift), value)
            used = used | here
        return jnp.where(used & west[: value.shape[0]], value, 0.0)

    mask = unpack(0, slice(levels, block))[:1]
    halos, scales = [], []
    for which in range(2):
        start = lev * width if which == 0 else (1 - lev) * width
        part = slice(which * block, which * block + levels)
        for t in range(tracers):
            in_scale, out_scale = (
                jnp.broadcast_to(ring[part, at : at + 1], (levels, LANES))
                for at in (SCALE_LANE + t, SCALE_LANE + tracers + t)
            )
            value = unpack(t, part)
            halos.append(value)
            scales.append(out_scale)
            x[pl.ds(pl.multiple_of(start + t * levels, levels), levels), :] = (value * in_scale).astype(BF16)
    tendency = narrow_network(x[...], w_in[...], w_mid, w_out[...]).astype(F32)
    x_tendency = [tendency[n * levels : (n + 1) * levels] for n in range(2 * tracers)]
    x_tendency = [
        jnp.where(head, x_tendency[n], x_tendency[(n + tracers) % (2 * tracers)]) for n in range(2 * tracers)
    ]
    values = [halo + scale * moist * mask for halo, scale, moist in zip(halos, scales, x_tendency)]
    if count == 2:
        up = weights[LAT_SIGN] > 0.5
        values = [jnp.where(up | (lane < 48), q, turned(q, -18)) for q in values]
    fix = [weights[EDGE] * q for q in values]
    for k, shift in ((1, 1), (2, -1), (3, 2), (4, -2)):
        fix = [f + weights[EDGE + k] * turned(q, shift) for f, q in zip(fix, values)]
    for t in range(tracers):
        mine[t] = fix[t]
        other[t] = fix[tracers + t]


def row_kernel(tracers, levels, moves, packs, *refs):
    count = len(moves)
    edge, edge_other, (weights, w_in, w_mid, w_out, beyond, x, tendency, fields) = refs[:count], refs[count : 2 * count], refs[2 * count :]
    lev = lax.axis_index("lev")
    width = tracers * levels
    block = levels + EXTRA
    near = pl.ds(pl.multiple_of(lev * width, width), width)
    tail = W * tracers * levels
    for which, source in ((0, edge), (1, edge_other)):
        start = lev * width if which == 0 else (1 - lev) * width
        unscale = [inverse_scale(from_fixed(source[n][tail : tail + levels, :])) * (1.0 / FIXED_ONE) for n in range(count)]
        for t in range(tracers):
            in_scale = jnp.broadcast_to(
                packs[which * block : which * block + levels, SCALE_LANE + t : SCALE_LANE + t + 1], (levels, LANES)
            )
            to = pl.ds(pl.multiple_of(start + t * levels, levels), levels)
            for n in range(count):
                scale = jnp.broadcast_to(unscale[n][:, t : t + 1], (levels, LANES))
                for r in range(W):
                    column_at = (n * W + r) * LANES
                    part = (r * tracers + t) * levels
                    value = from_fixed(source[n][part : part + levels, :]) * scale
                    x[to, column_at : column_at + LANES] = (value * in_scale).astype(BF16)
                    if which == 0:
                        fields[n, part : part + levels, :] = value
    masks = [from_fixed(e[tail + levels :, :]) for e in edge]
    tendency[...] = narrow_network(x[...], w_in[...], w_mid, w_out[near, :])
    up = weights[LAT_SIGN] > 0.5
    values = []
    for t in range(tracers):
        for r in range(W):
            rows_q = []
            for n in range(count):
                column_at = (n * W + r) * LANES
                moist = tendency[t * levels : (t + 1) * levels, column_at : column_at + LANES].astype(F32)
                value = fields[n, (r * tracers + t) * levels : (r * tracers + t + 1) * levels, :]
                rows_q.append(value + weights[OUT_SCALE + t] * moist * masks[n][r : r + 1, :])
            values.append(jnp.where(up, rows_q[0], rows_q[1]) if count > 1 else rows_q[0])
    for n, q in enumerate(sweep_lon(values, weights, slice(0, levels))):
        beyond[n] = q


def finish_kernel(tracers, levels, rows, moves, swept, weights, fix_mine, fix_other, beyond, out, result, sems):
    lat = lax.axis_index("lat")
    southward = jnp.where(lat == 0, 0.0, 1.0)
    copies = []
    lane = lane_ids(HALF_GROUP)
    at_edge = (lane < W) | (lane >= LANES - W)
    for g in range(0, levels, HALF_GROUP):
        span = slice(g, g + HALF_GROUP)
        sign = weights[LAT_SIGN, span, :]
        up = sign > 0.5
        w = [weights[LAT + k, span, :] for k in range(4)]
        for t in range(tracers):
            at = t * levels + g
            fix = fix_mine[t, span, :] + fix_other[t, span, :]

            def fixed(value, first):
                return value + jnp.where(at_edge, turned(fix, LANES - W - first), 0.0)

            inner = [fixed(swept[i, at : at + HALF_GROUP, :], 6 * i) for i in range(rows)]
            outer = [fixed(beyond[t * W + r, span, :], 48 + 6 * r) for r in range(W)]
            if len(moves) == 1:
                outer = [jnp.where(sign == southward, q, 0.0) for q in outer]
            line = []
            for i in range(rows + W):
                above = outer[i] if i < W else inner[i - W]
                below = inner[i] if i < rows else outer[i - rows]
                line.append(jnp.where(up, above, below))
            results = [w[0] * line[i] + w[1] * line[i + 1] + w[2] * line[i + 2] + w[3] * line[i + 3] for i in range(rows)]
            for i, value in enumerate(results):
                result[pl.ds(at * rows + i, HALF_GROUP, stride=rows), :] = value
            part = pl.ds(at * rows, HALF_GROUP * rows)
            copies.append(pltpu.make_async_copy(result.at[part], out.at[part], sems.at[len(copies)]))
            copies[-1].start()
    for copy in copies:
        copy.wait()


def call(kernel, out_shape, scratch, flops, moved, name, **specs):
    return pl.pallas_call(
        kernel,
        out_shape=out_shape,
        **specs,
        scratch_shapes=scratch,
        compiler_params=pltpu.CompilerParams(vmem_limit_bytes=VMEM_LIMIT),
        cost_estimate=pl.CostEstimate(flops=flops, bytes_accessed=moved, transcendentals=0),
        name=name,
    )


def swap_cores(x):
    return lax.ppermute(x, "lev", [(0, 1), (1, 0)])


def routes(lon_count, lat_count, move, along_lon):
    pairs = []
    for i in range(lon_count):
        for j in range(lat_count):
            to_lat = 1 - j if move == 0 else j + (move or 0)
            if not 0 <= to_lat < lat_count:
                continue
            for k in range(2):
                to_lon = (i + (1 - 2 * k)) % lon_count if along_lon else i
                pairs.append((((i * lat_count) + j) * 2 + k, ((to_lon * lat_count) + to_lat) * 2 + k))
    return pairs


def send(x, move, along_lon):
    axes = ("lon", "lat", "lev")
    lon_count, lat_count = lax.axis_size("lon"), lax.axis_size("lat")
    if move is None:
        pairs = []
        for i in range(lon_count):
            for j in range(lat_count):
                for k in range(2):
                    to_lon = (i + (1 - 2 * k)) % lon_count
                    pairs.append(((i * lat_count + j) * 2 + k, (to_lon * lat_count + j) * 2 + k))
    else:
        pairs = routes(lon_count, lat_count, move, along_lon)
    return lax.ppermute(x, axes, pairs)


def on_device(fields, in_scale, out_scale, w_in, w_mid, w_out, storm_mask, balance, substeps, courant):
    tracers, levels, rows, columns = fields.shape
    width = tracers * levels
    moves = (0,) if lax.axis_size("lat") == 2 else (1, -1)
    count = len(moves)
    flat = fields.reshape(width * rows, columns)
    block = levels + EXTRA
    edge_shape = jax.ShapeDtypeStruct((W * width + levels + 2 * EXTRA, columns), jnp.int16)
    pack_shape = jax.ShapeDtypeStruct((block, LANES), F32)
    inputs = (flat, in_scale, storm_mask, balance.T, out_scale, courant, substeps.reshape(1, levels))
    inputs = [pltpu.with_memory_space_constraint(x, pltpu.HBM) for x in inputs]
    small_shape = jax.ShapeDtypeStruct((EXTRA, LANES), F32)
    keep, give, active, small, features = call(
        functools.partial(edge_kernel, tracers, levels, rows),
        [pack_shape, pack_shape, jax.ShapeDtypeStruct((rows, columns), F32), small_shape,
         jax.ShapeDtypeStruct((rows, width, columns), BF16)],
        [pltpu.VMEM(x.shape, x.dtype) for x in inputs]
        + [pltpu.VMEM((EXTRA, LANES), F32), pltpu.SemaphoreType.DMA((len(inputs) - 1 + tracers,))],
        10**6, 2 * 10**6, "edges",
        in_specs=[pl.BlockSpec(memory_space=pltpu.HBM)] * len(inputs),
    )(*inputs)
    given = swap_cores(give)
    features_other = swap_cores(features)
    edge_rows = call(
        functools.partial(row_message_kernel, tracers, levels, rows, moves),
        [edge_shape] * count,
        [],
        10**6, 2 * 10**6, "row_messages",
    )(flat, active)
    packs = jnp.concatenate([keep, given], axis=0)
    corner = [send(packs, move, True) for move in moves]
    ring = send(packs, None, True)
    edge = [send(e, move, False) for e, move in zip(edge_rows, moves)]

    tendency = call(
        functools.partial(own_network_kernel, tracers, levels, rows),
        jax.ShapeDtypeStruct((width, rows * columns), BF16),
        [pltpu.VMEM((2 * width, rows * columns), BF16)],
        10**6, 10**6, "own_network",
    )(features, features_other, w_in, w_mid, w_out)
    swept, weights, token = call(
        functools.partial(own_sweep_kernel, tracers, levels, rows),
        [jax.ShapeDtypeStruct((rows, width, columns), F32), jax.ShapeDtypeStruct((PLANES, levels, LANES), F32),
         jax.ShapeDtypeStruct((2 * EXTRA, LANES), jnp.int16)],
        [],
        10**6, 10**6, "own_sweep",
    )(flat, tendency, small, active)

    fix_shape = jax.ShapeDtypeStruct((tracers, levels, LANES), F32)
    fix_mine, fix_given = call(
        functools.partial(edge_network_kernel, tracers, levels, rows, moves),
        [fix_shape, fix_shape],
        [pltpu.VMEM((2 * width, LANES), BF16)],
        10**9, 4 * 10**6, "edge_network",
    )(ring, *corner, weights, w_in, w_mid, w_out)
    fix_other = swap_cores(fix_given)
    edge_other = [swap_cores(e + token[:1]) for e in edge]
    total = W * count * LANES
    beyond = call(
        functools.partial(row_kernel, tracers, levels, moves),
        jax.ShapeDtypeStruct((tracers * W, levels, LANES), F32),
        [pltpu.VMEM((2 * width, total), BF16), pltpu.VMEM((width, total), BF16),
         pltpu.VMEM((count, W * width, LANES), F32)],
        10**9, 4 * 10**6, "row_network",
    )(packs, *edge, *edge_other, weights, w_in, w_mid, w_out)
    out = call(
        functools.partial(finish_kernel, tracers, levels, rows, moves),
        jax.ShapeDtypeStruct((width * rows, columns), F32),
        [pltpu.VMEM((width * rows, columns), F32), pltpu.SemaphoreType.DMA((width // HALF_GROUP,))],
        10**9, 4 * 10**6, "finish",
        out_specs=pl.BlockSpec(memory_space=pltpu.HBM),
    )(swept, weights, fix_mine, fix_other, beyond)
    return out.reshape(fields.shape)


def solution(mesh):
    in_specs = (
        P("lev", None, ("group", "lat"), "lon"),
        P("lev", None),
        P("lev", None),
        P(),
        P(),
        P(),
        P(("group", "lat"), "lon"),
        P(("group", "lat"), None),
        P(),
        P(),
    )
    out_specs = P("lev", None, ("group", "lat"), "lon")
    return jax.shard_map(
        on_device, mesh=mesh, in_specs=in_specs, out_specs=out_specs, check_vma=False
    )
```

time: 19.3 us -> 18.2 us (0.943)
  waiting for transfers between devices: 3.34 us -> 1.47 us
  Pallas kernels: 7.74 us -> 8.75 us
  starting transfers between devices: 7.93 us -> 7.65 us
    pallas_call x2 -> x5, Pallas kernels: 3.27 us -> 6.33 us  [the longest x1 1.7 us: on_device(): call(functools.partial(edge_kernel, tracers, levels, rows), [pack_shape,...]
    pallas_call x1, Pallas kernels: 3.19 us -> 1.15 us  [on_device(): call(functools.partial(finish_kernel, tracers, levels, rows, moves), jax....]
    ppermute x3, waiting for transfers between devices: 3.33 us -> 1.46 us  [send(): return lax.ppermute(x, axes, pairs)]
    ppermute x3, starting transfers between devices: 6.75 us -> 6.43 us  [send(): return lax.ppermute(x, axes, pairs)]
  transfers between devices with their start and end apart: 7 -> 7, of which waited for: 2 -> 2; matrix products, arithmetic and copies ran while one was open for 0% -> 0% of each run, Pallas kernels for 15% -> 33%
where the time goes in v3:
time: 18.2 us; the launch traced here: 18 us
  Pallas kernels  8.75 us (48%)
  starting transfers between devices  7.65 us (42%)
  waiting for transfers between devices  1.47 us (8%)
    ppermute x3, starting transfers between devices, send(): return lax.ppermute(x, axes, pairs)  6.43 us
    pallas_call x1, Pallas kernels, on_device(): call(functools.partial(edge_kernel, tracers, levels, rows), [pack_shape,...  1.7 us
    pallas_call x1, Pallas kernels, on_device(): call(functools.partial(row_kernel, tracers, levels, moves), jax.ShapeDtyp...  1.53 us
    pallas_call x1, Pallas kernels, on_device(): call(functools.partial(own_network_kernel, tracers, levels, rows), jax.Sh...  1.49 us
    ppermute x3, waiting for transfers between devices, send(): return lax.ppermute(x, axes, pairs)  1.46 us
    pallas_call x1, Pallas kernels, on_device(): call(functools.partial(edge_network_kernel, tracers, levels, rows, moves)...  1.29 us
    pallas_call x1, Pallas kernels, on_device(): call(functools.partial(own_sweep_kernel, tracers, levels, rows), [jax.Sha...  1.28 us
    ppermute x4, starting transfers between devices, swap_cores(): return lax.ppermute(x, 'lev', [(0, 1), (1, 0)])  1.22 us
  transfers between devices with their start and end apart: 7, of which 2 were waited for; matrix products, arithmetic and copies ran while one was open for 0% of the time, Pallas kernels for 33%

profile of v3, /device:TPU:0, one launch (start us, length us, event | category | flops | bytes accessed | tf_op | source)
XLA Modules:
  0.0 18.0 jit_solution(8505407977530921877)
XLA Ops:
  0.0 0.0 copy-start
  0.0 1.7 %edges.1 = (f32[72,128]{1,0:T(8,128)S(1)}, f32[72,128]{1,0:T(8,128)S(1)}, f32[8,128]{1,0:T(8,128)S(1)}, f32[8,128]{1,0:T(8,128)S(1)}, bf16[8,192,128]{2,1,0:T(8,128)(2,1)S(1)}) custom-call(f32[1536,128]{1,0:T(8,128)} %bitcast.6, f32[3,64]{1,0:T(4,128)} %refs_1_.1, s32[8,128]{1,0:T(8,128)} %refs_2_.2, s32[4,8]{1,0:T(4,128)} %bitcast.9, f32[3,64]{1,0:T(4,128)} %refs_4_.3, ...), custom_call_target="tpu_custom_call" | custom-call | flops 1000000 | bytes 2000000 | tf_op jit(solution)/shard_map/edges/pallas_call | solution.py:478
  1.7 0.5 %collective-permute-start = (bf16[8,192,128]{2,1,0:T(8,128)(2,1)S(1)}, bf16[8,192,128]{2,1,0:T(8,128)(2,1)S(1)}, u32[]{:S(2)}, u32[]{:S(2)}) collective-permute-start(bf16[8,192,128]{2,1,0:T(8,128)(2,1)S(1)} %get-tuple-element.15.mine), channel_id=1, source_target_pairs={{0,1},{1,0},{2,3},{3,2},{4,5},{5,4},{6,7},{7,6},{8,9},{9,8},{10,11... | collective-permute-start | bytes 1179656 | tf_op jit(solution)/shard_map/ppermute | solution.py:435
  2.2 0.1 collective-permute-start.1
  2.3 0.0 copy-done
  2.3 0.0 copy-start.1
  2.3 0.0 copy-start.2
  2.3 0.0 copy-start.3
  2.3 0.3 %row_messages.1 = s16[656,128]{1,0:T(8,128)(2,1)S(1)} custom-call(f32[1536,128]{1,0:T(8,128)S(1)} %bitcast.7, f32[8,128]{1,0:T(8,128)S(1)} %get-tuple-element.17.active), custom_call_target="tpu_custom_call" | custom-call | flops 1000000 | bytes 2000000 | tf_op jit(solution)/shard_map/row_messages/pallas_call | solution.py:489
  2.6 3.0 %collective-permute-start.5 = (s16[656,128]{1,0:T(8,128)(2,1)S(1)}, s16[656,128]{1,0:T(8,128)(2,1)S(1)}, u32[]{:S(2)}, u32[]{:S(2)}) collective-permute-start(s16[656,128]{1,0:T(8,128)(2,1)S(1)} %row_messages.1), channel_id=1, source_target_pairs={{0,2},{1,3},{2,0},{3,1},{4,6},{5,7},{6,4},{7,5},{8,10},{9,11},{10,... | collective-permute-start | bytes 503816 | tf_op jit(solution)/shard_map/ppermute | solution.py:463
  5.6 0.0 collective-permute-done.1
  5.6 1.9 %collective-permute-start.3 = (f32[144,128]{1,0:T(8,128)S(1)}, f32[144,128]{1,0:T(8,128)S(1)}, u32[]{:S(2)}, u32[]{:S(2)}) collective-permute-start(f32[144,128]{1,0:T(8,128)S(1)} %constant_dynamic-update-slice_fusion.packs), channel_id=1, source_target_pairs={{0,6},{1,15},{2,4},{3,13},{4,10},{5,3},{6,8},{7,1},{8,14},{9,7},{1... | collective-permute-start | bytes 221192 | tf_op jit(solution)/shard_map/ppermute | solution.py:463
  7.5 1.6 %collective-permute-start.2 = (f32[144,128]{1,0:T(8,128)S(1)}, f32[144,128]{1,0:T(8,128)S(1)}, u32[]{:S(2)}, u32[]{:S(2)}) collective-permute-start(f32[144,128]{1,0:T(8,128)S(1)} %constant_dynamic-update-slice_fusion.packs), channel_id=1, source_target_pairs={{0,4},{1,13},{2,6},{3,15},{4,8},{5,1},{6,10},{7,3},{8,12},{9,5},{1... | collective-permute-start | bytes 221192 | tf_op jit(solution)/shard_map/ppermute | solution.py:463
  9.1 0.0 collective-permute-done.other
  9.1 0.0 copy-done.1
  9.1 0.0 copy-done.2
  9.1 0.0 copy-done.3
  9.1 1.5 %own_network.1.tendency = bf16[192,1024]{1,0:T(8,128)(2,1)S(1)} custom-call(bf16[8,192,128]{2,1,0:T(8,128)(2,1)S(1)} %get-tuple-element.15.mine, bf16[8,192,128]{2,1,0:T(8,128)(2,1)S(1)} %collective-permute-done.other, bf16[256,384]{1,0:T(8,128)(2,1)S(1)} %copy-done.2, bf16[3,256,256]{2,1,0:T(8,128)(2,1)S(1)} %copy-done.1, bf16[384,256]{1,0:T(8,128)(2,1)S(1)} %copy-done.3), custom_call_target="tpu_custom_call" | custom-call | flops 1000000 | bytes 1000000 | tf_op jit(solution)/shard_map/own_network/pallas_call | solution.py:500
  10.6 1.3 %own_sweep.1 = (f32[8,192,128]{2,1,0:T(8,128)S(1)}, f32[18,64,128]{2,1,0:T(8,128)S(1)}, s16[16,128]{1,0:T(8,128)(2,1)S(1)}) custom-call(f32[1536,128]{1,0:T(8,128)S(1)} %bitcast.8, bf16[192,1024]{1,0:T(8,128)(2,1)S(1)} %own_network.1.tendency, f32[8,128]{1,0:T(8,128)S(1)} %get-tuple-element.16.small, f32[8,128]{1,0:T(8,128)S(1)} %get-tuple-element.17.active), custom_call_target="tpu_custom_call" | custom-call | flops 1000000 | bytes 1000000 | tf_op jit(solution)/shard_map/own_sweep/pallas_call | solution.py:506
  11.9 0.0 collective-permute-done.5.refs_0_
  12.0 0.5 %collective-permute-start.6 = (s16[656,128]{1,0:T(8,128)(2,1)S(1)}, s16[656,128]{1,0:T(8,128)(2,1)S(1)}, u32[]{:S(2)}, u32[]{:S(2)}) collective-permute-start(s16[656,128]{1,0:T(8,128)(2,1)S(1)} %broadcast_add_fusion), channel_id=1, source_target_pairs={{0,1},{1,0},{2,3},{3,2},{4,5},{5,4},{6,7},{7,6},{8,9},{9,8},{10,11... | collective-permute-start | bytes 503816 | tf_op jit(solution)/shard_map/ppermute | solution.py:435
  12.5 1.0 %collective-permute-done.3.refs_0_ = f32[144,128]{1,0:T(8,128)S(1)} collective-permute-done((f32[144,128]{1,0:T(8,128)S(1)}, f32[144,128]{1,0:T(8,128)S(1)}, u32[]{:S(2)}, u32[]{:S(2)}) %collective-permute-start.3) | collective-permute-done | bytes 73760 | tf_op jit(solution)/shard_map/ppermute | solution.py:463
  13.5 0.5 %collective-permute-done.2.ring = f32[144,128]{1,0:T(8,128)S(1)} collective-permute-done((f32[144,128]{1,0:T(8,128)S(1)}, f32[144,128]{1,0:T(8,128)S(1)}, u32[]{:S(2)}, u32[]{:S(2)}) %collective-permute-start.2) | collective-permute-done | bytes 73760 | tf_op jit(solution)/shard_map/ppermute | solution.py:463
  14.0 1.3 %edge_network.1 = (f32[3,64,128]{2,1,0:T(8,128)S(1)}, f32[3,64,128]{2,1,0:T(8,128)S(1)}) custom-call(f32[144,128]{1,0:T(8,128)S(1)} %collective-permute-done.2.ring, f32[144,128]{1,0:T(8,128)S(1)} %collective-permute-done.3.refs_0_, f32[18,64,128]{2,1,0:T(8,128)S(1)} %get-tuple-element.19.refs_1_.refs_2_.weights, bf16[256,384]{1,0:T(8,128)(2,1)S(1)} %copy-done.2, ...), custom_call_target="tpu_custom_call" | custom-call | flops 1000000000 | bytes 4000000 | tf_op jit(solution)/shard_map/edge_network/pallas_call | solution.py:515
  15.3 0.1 collective-permute-start.4
  15.3 0.0 collective-permute-done.6.refs_1_
  15.3 1.5 %row_network.1.beyond = f32[9,64,128]{2,1,0:T(8,128)S(1)} custom-call(f32[144,128]{1,0:T(8,128)S(1)} %constant_dynamic-update-slice_fusion.packs, s16[656,128]{1,0:T(8,128)(2,1)S(1)} %collective-permute-done.5.refs_0_, s16[656,128]{1,0:T(8,128)(2,1)S(1)} %collective-permute-done.6.refs_1_, f32[18,64,128]{2,1,0:T(8,128)S(1)} %get-tuple-element.19.refs_1_.refs_2_.weights, ...), custom_call_target="tpu_custom_call" | custom-call | flops 1000000000 | bytes 4000000 | tf_op jit(solution)/shard_map/row_network/pallas_call | solution.py:524
  16.9 0.0 collective-permute-done.4.fix_other
  16.9 1.1 %finish.1 = f32[1536,128]{1,0:T(8,128)} custom-call(f32[8,192,128]{2,1,0:T(8,128)S(1)} %get-tuple-element.18.swept, f32[18,64,128]{2,1,0:T(8,128)S(1)} %get-tuple-element.19.refs_1_.refs_2_.weights, f32[3,64,128]{2,1,0:T(8,128)S(1)} %get-tuple-element.22.fix_mine, f32[3,64,128]{2,1,0:T(8,128)S(1)} %collective-permute-done.4.fix_other, ...), custom_call_target="tpu_custom_call" | custom-call | flops 1000000000 | bytes 4000000 | tf_op jit(solution)/shard_map/finish/pallas_call | solution.py:531
  (4 shorter events, 0.0 us)
Async XLA Ops:
  0.0 2.3 %copy-start = (f32[3,64,8,128]{3,2,1,0:T(8,128)S(1)}, f32[3,64,8,128]{3,2,1,0:T(8,128)}, u32[]{:S(2)}) copy-start(f32[3,64,8,128]{3,2,1,0:T(8,128)} %param.10) | copy-start | bytes 2359300
  1.7 7.4 %collective-permute-start = (bf16[8,192,128]{2,1,0:T(8,128)(2,1)S(1)}, bf16[8,192,128]{2,1,0:T(8,128)(2,1)S(1)}, u32[]{:S(2)}, u32[]{:S(2)}) collective-permute-start(bf16[8,192,128]{2,1,0:T(8,128)(2,1)S(1)} %get-tuple-element.15.mine), channel_id=1, source_target_pairs={{0,1},{1,0},{2,3},{3,2},{4,5},{5,4},{6,7},{7,6},{8,9},{9,8},{10,11... | collective-permute-start | bytes 1179656 | tf_op jit(solution)/shard_map/ppermute | solution.py:435
  2.2 3.4 %collective-permute-start.1 = (f32[72,128]{1,0:T(8,128)S(1)}, f32[72,128]{1,0:T(8,128)S(1)}, u32[]{:S(2)}, u32[]{:S(2)}) collective-permute-start(f32[72,128]{1,0:T(8,128)S(1)} %get-tuple-element.21), channel_id=1, source_target_pairs={{0,1},{1,0},{2,3},{3,2},{4,5},{5,4},{6,7},{7,6},{8,9},{9,8},{10,11... | collective-permute-start | bytes 110600 | tf_op jit(solution)/shard_map/ppermute | solution.py:435
  2.3 6.8 %copy-start.1 = (bf16[3,256,256]{2,1,0:T(8,128)(2,1)S(1)}, bf16[3,256,256]{2,1,0:T(8,128)(2,1)}, u32[]{:S(2)}) copy-start(bf16[3,256,256]{2,1,0:T(8,128)(2,1)} %refs_4_.5) | copy-start | bytes 1179652
  2.3 6.8 %copy-start.2 = (bf16[256,384]{1,0:T(8,128)(2,1)S(1)}, bf16[256,384]{1,0:T(8,128)(2,1)}, u32[]{:S(2)}) copy-start(bf16[256,384]{1,0:T(8,128)(2,1)} %refs_3_.3) | copy-start | bytes 589828
  2.3 6.8 %copy-start.3 = (bf16[384,256]{1,0:T(8,128)(2,1)S(1)}, bf16[384,256]{1,0:T(8,128)(2,1)}, u32[]{:S(2)}) copy-start(bf16[384,256]{1,0:T(8,128)(2,1)} %refs_5_.3) | copy-start | bytes 589828
  2.6 9.3 %collective-permute-start.5 = (s16[656,128]{1,0:T(8,128)(2,1)S(1)}, s16[656,128]{1,0:T(8,128)(2,1)S(1)}, u32[]{:S(2)}, u32[]{:S(2)}) collective-permute-start(s16[656,128]{1,0:T(8,128)(2,1)S(1)} %row_messages.1), channel_id=1, source_target_pairs={{0,2},{1,3},{2,0},{3,1},{4,6},{5,7},{6,4},{7,5},{8,10},{9,11},{10,... | collective-permute-start | bytes 503816 | tf_op jit(solution)/shard_map/ppermute | solution.py:463
  5.6 7.8 %collective-permute-start.3 = (f32[144,128]{1,0:T(8,128)S(1)}, f32[144,128]{1,0:T(8,128)S(1)}, u32[]{:S(2)}, u32[]{:S(2)}) collective-permute-start(f32[144,128]{1,0:T(8,128)S(1)} %constant_dynamic-update-slice_fusion.packs), channel_id=1, source_target_pairs={{0,6},{1,15},{2,4},{3,13},{4,10},{5,3},{6,8},{7,1},{8,14},{9,7},{1... | collective-permute-start | bytes 221192 | tf_op jit(solution)/shard_map/ppermute | solution.py:463
  7.5 6.4 %collective-permute-start.2 = (f32[144,128]{1,0:T(8,128)S(1)}, f32[144,128]{1,0:T(8,128)S(1)}, u32[]{:S(2)}, u32[]{:S(2)}) collective-permute-start(f32[144,128]{1,0:T(8,128)S(1)} %constant_dynamic-update-slice_fusion.packs), channel_id=1, source_target_pairs={{0,4},{1,13},{2,6},{3,15},{4,8},{5,1},{6,10},{7,3},{8,12},{9,5},{1... | collective-permute-start | bytes 221192 | tf_op jit(solution)/shard_map/ppermute | solution.py:463
  12.0 3.4 %collective-permute-start.6 = (s16[656,128]{1,0:T(8,128)(2,1)S(1)}, s16[656,128]{1,0:T(8,128)(2,1)S(1)}, u32[]{:S(2)}, u32[]{:S(2)}) collective-permute-start(s16[656,128]{1,0:T(8,128)(2,1)S(1)} %broadcast_add_fusion), channel_id=1, source_target_pairs={{0,1},{1,0},{2,3},{3,2},{4,5},{5,4},{6,7},{7,6},{8,9},{9,8},{10,11... | collective-permute-start | bytes 503816 | tf_op jit(solution)/shard_map/ppermute | solution.py:435
  15.3 1.6 %collective-permute-start.4 = (f32[3,64,128]{2,1,0:T(8,128)S(1)}, f32[3,64,128]{2,1,0:T(8,128)S(1)}, u32[]{:S(2)}, u32[]{:S(2)}) collective-permute-start(f32[3,64,128]{2,1,0:T(8,128)S(1)} %get-tuple-element.23), channel_id=1, source_target_pairs={{0,1},{1,0},{2,3},{3,2},{4,5},{5,4},{6,7},{7,6},{8,9},{9,8},{10,11... | collective-permute-start | bytes 294920 | tf_op jit(solution)/shard_map/ppermute | solution.py:435

commit v4 on v3

--- a/solution.py
+++ b/solution.py
@@ -9,6 +9,7 @@
 
 W = 3
 LANES = 128
+HALF_LANES = 48
 SCALE_LANE = 96
 FIELD_BOUND = 8.0
 FIXED_ONE = 32768.0 / FIELD_BOUND
@@ -51,14 +52,15 @@
     return jnp.broadcast_to(turned_rows[:levels, index : index + 1], (levels, LANES))
 
 
-def side_packs(edges):
-    lane = lane_ids(edges[0].shape[0])
+def side_messages(edges):
+    lane = lane_ids(1)
     east = lane % 6 < 3
-    last = [jnp.where(east, e, 0.0) for e in edges]
-    first = [jnp.where(east, 0.0, e) for e in edges]
-    east_pack = last[0] + turned(last[1], 3) + turned(last[2], 48)
-    west_pack = turned(first[0], -3) + first[1] + turned(first[2], 45)
-    return east_pack, west_pack
+    used = lane < HALF_LANES
+    half = edges[2].shape[0] // 2
+    pairs = ((edges[0], edges[1]), (edges[2][:half], edges[2][half:]))
+    last = [jnp.where(east, p, turned(q, W)) for p, q in pairs]
+    first = [jnp.where(used, jnp.where(east, turned(p, -W), q), 0.0) for p, q in pairs]
+    return last, first
 
 
 def edge_kernel(tracers, levels, rows, *refs):
@@ -89,16 +91,23 @@
     mask = jnp.where(column(scales, 2 * tracers, rows) >= 0.0, storm[...].astype(F32), 0.0)
     active[...] = mask
     lane = lane_ids(levels)
-    scale_lanes = jnp.zeros((levels, LANES), F32)
+    own_scales, given_scales = jnp.zeros((levels, LANES), F32), jnp.zeros((levels, LANES), F32)
     for n in range(2 * tracers):
-        scale_lanes = jnp.where(lane == SCALE_LANE + n, column(scales, n, levels), scale_lanes)
+        scale = column(scales, n, levels)
+        own_scales = jnp.where(lane == SCALE_LANE + n, scale, own_scales)
+        given_scales = jnp.where(lane == SCALE_LANE + 2 * tracers + n, scale, given_scales)
     lane = lane_ids(1)
     mask_pack = jnp.zeros((1, LANES), F32)
     for i in range(rows):
-        mask_pack = jnp.where((lane >= 6 * i) & (lane < 6 * i + 6), turned(active[i : i + 1, :], 6 * i + W), mask_pack)
+        mask_pack = jnp.where((lane >= 6 * i) & (lane < 6 * i + 6), turned(mask[i : i + 1, :], 6 * i + W), mask_pack)
     mask_pack = jnp.broadcast_to(mask_pack, (EXTRA, LANES))
-    none = jnp.zeros_like(mask_pack)
-    last_mask, first_mask = side_packs([mask_pack, none, none])
+    east = lane % 6 < 3
+    last_mask = jnp.where(east, mask_pack, 0.0)
+    first_mask = turned(jnp.where(east, 0.0, mask_pack), -W)
+    half = levels // 2
+    head = lev == 0
+    keep[levels + half :] = jnp.where(head, last_mask, first_mask)
+    give[levels + half :] = turned(jnp.where(head, first_mask, last_mask), HALF_LANES)
     lane = lane_ids(levels)
     edges = []
     for t in range(tracers):
@@ -110,12 +119,11 @@
             features[i, t * levels : (t + 1) * levels, :] = (x * scale).astype(BF16)
             pack = jnp.where((lane >= 6 * i) & (lane < 6 * i + 6), turned(x, 6 * i + W), pack)
         edges.append(pack)
-    last_pack, first_pack = side_packs(edges)
-    head = lev == 0
-    keep[:levels] = jnp.where(head, last_pack, first_pack) + scale_lanes
-    give[:levels] = jnp.where(head, first_pack, last_pack) + scale_lanes
-    keep[levels:] = jnp.where(head, last_mask, first_mask)
-    give[levels:] = jnp.where(head, first_mask, last_mask)
+    last, first = side_messages(edges)
+    keep[:levels] = jnp.where(head, last[0], first[0]) + own_scales
+    give[:levels] = turned(jnp.where(head, first[0], last[0]), HALF_LANES) + given_scales
+    keep[levels : levels + half] = jnp.where(head, last[1], first[1])
+    give[levels : levels + half] = turned(jnp.where(head, first[1], last[1]), HALF_LANES)
 
 
 def binary_scale(largest):
@@ -285,41 +293,51 @@
                 swept[i, at : at + GROUP, :] = q
 
 
+def read_scale(message, which, n, tracers, levels):
+    at = SCALE_LANE + 2 * tracers * which + n
+    return jnp.broadcast_to(message[:levels, at : at + 1], (levels, LANES))
+
+
 def edge_network_kernel(tracers, levels, rows, moves, ring, *refs):
     count = len(moves)
     corner, (weights, w_in, w_mid, w_out, mine, other, x) = refs[:count], refs[count:]
     lat, lev = lax.axis_index("lat"), lax.axis_index("lev")
     width = tracers * levels
-    block = levels + EXTRA
     head = lev == 0
     lane = lane_ids(levels)
     west = (lane % 6 >= 3) == head
-    shifts = [jnp.where(head, a, b) for a, b in ((W, 0), (0, LANES - W), (LANES - 48 + W, LANES - 48))]
-
-    def unpack(t, part):
-        value = turned(ring[part, :], shifts[t])
-        lane_part = lane[: value.shape[0]]
+    shifts = [jnp.where(head, a, b) for a, b in ((W, 0), (0, LANES - W))]
+    half = levels // 2
+
+    def place(message, part, which, extra):
+        moved = []
+        for shift in shifts:
+            shift = shift + (extra + LANES - HALF_LANES * which)
+            shift = jnp.where(shift >= 2 * LANES, shift - 2 * LANES, jnp.where(shift >= LANES, shift - LANES, shift))
+            moved.append(turned(message[part, :], shift))
+        return moved
+
+    def unpack(part, which):
+        lane_part = lane[: part.stop - part.start]
+        values = place(ring, part, which, 0)
         used = lane_part < 48
         for n, move in enumerate(moves):
             base = 48 + 18 * n
-            shift = shifts[t] + (base - 6 * first_row_received(move, lat, rows))
-            shift = jnp.where(shift < 0, shift + LANES, jnp.where(shift >= LANES, shift - LANES, shift))
             here = (lane_part >= base) & (lane_part < base + 18)
-            value = jnp.where(here, turned(corner[n][part, :], shift), value)
+            far = place(corner[n], part, which, base - 6 * first_row_received(move, lat, rows))
+            values = [jnp.where(here, q, value) for q, value in zip(far, values)]
             used = used | here
-        return jnp.where(used & west[: value.shape[0]], value, 0.0)
-
-    mask = unpack(0, slice(levels, block))[:1]
+        used = used & west[: lane_part.shape[0]]
+        return [jnp.where(used, value, 0.0) for value in values]
+
+    mask = unpack(slice(levels + half, levels + half + EXTRA), 0)[0][:1]
     halos, scales = [], []
     for which in range(2):
         start = lev * width if which == 0 else (1 - lev) * width
-        part = slice(which * block, which * block + levels)
-        for t in range(tracers):
-            in_scale, out_scale = (
-                jnp.broadcast_to(ring[part, at : at + 1], (levels, LANES))
-                for at in (SCALE_LANE + t, SCALE_LANE + tracers + t)
-            )
-            value = unpack(t, part)
+        values = unpack(slice(0, levels), which)
+        values.append(jnp.concatenate(unpack(slice(levels, levels + half), which), axis=0))
+        for t, value in enumerate(values):
+            in_scale, out_scale = (read_scale(ring, which, n, tracers, levels) for n in (t, tracers + t))
             halos.append(value)
             scales.append(out_scale)
             x[pl.ds(pl.multiple_of(start + t * levels, levels), levels), :] = (value * in_scale).astype(BF16)
@@ -345,16 +363,13 @@
     edge, edge_other, (weights, w_in, w_mid, w_out, beyond, x, tendency, fields) = refs[:count], refs[count : 2 * count], refs[2 * count :]
     lev = lax.axis_index("lev")
     width = tracers * levels
-    block = levels + EXTRA
     near = pl.ds(pl.multiple_of(lev * width, width), width)
     tail = W * tracers * levels
     for which, source in ((0, edge), (1, edge_other)):
         start = lev * width if which == 0 else (1 - lev) * width
         unscale = [inverse_scale(from_fixed(source[n][tail : tail + levels, :])) * (1.0 / FIXED_ONE) for n in range(count)]
         for t in range(tracers):
-            in_scale = jnp.broadcast_to(
-                packs[which * block : which * block + levels, SCALE_LANE + t : SCALE_LANE + t + 1], (levels, LANES)
-            )
+            in_scale = read_scale(packs, which, t, tracers, levels)
             to = pl.ds(pl.multiple_of(start + t * levels, levels), levels)
             for n in range(count):
                 scale = jnp.broadcast_to(unscale[n][:, t : t + 1], (levels, LANES))
@@ -469,9 +484,8 @@
     moves = (0,) if lax.axis_size("lat") == 2 else (1, -1)
     count = len(moves)
     flat = fields.reshape(width * rows, columns)
-    block = levels + EXTRA
     edge_shape = jax.ShapeDtypeStruct((W * width + levels + 2 * EXTRA, columns), jnp.int16)
-    pack_shape = jax.ShapeDtypeStruct((block, LANES), F32)
+    pack_shape = jax.ShapeDtypeStruct((levels + levels // 2 + EXTRA, LANES), F32)
     inputs = (flat, in_scale, storm_mask, balance.T, out_scale, courant, substeps.reshape(1, levels))
     inputs = [pltpu.with_memory_space_constraint(x, pltpu.HBM) for x in inputs]
     small_shape = jax.ShapeDtypeStruct((EXTRA, LANES), F32)
@@ -481,7 +495,7 @@
          jax.ShapeDtypeStruct((rows, width, columns), BF16)],
         [pltpu.VMEM(x.shape, x.dtype) for x in inputs]
         + [pltpu.VMEM((EXTRA, LANES), F32), pltpu.SemaphoreType.DMA((len(inputs) - 1 + tracers,))],
-        10**6, 2 * 10**6, "edges",
+        10000000000, 0, "edges",
         in_specs=[pl.BlockSpec(memory_space=pltpu.HBM)] * len(inputs),
     )(*inputs)
     given = swap_cores(give)
@@ -490,9 +504,9 @@
         functools.partial(row_message_kernel, tracers, levels, rows, moves),
         [edge_shape] * count,
         [],
-        10**6, 2 * 10**6, "row_messages",
+        10000000000, 0, "row_messages",
     )(flat, active)
-    packs = jnp.concatenate([keep, given], axis=0)
+    packs = keep + given
     corner = [send(packs, move, True) for move in moves]
     ring = send(packs, None, True)
     edge = [send(e, move, False) for e, move in zip(edge_rows, moves)]
@@ -501,14 +515,14 @@
         functools.partial(own_network_kernel, tracers, levels, rows),
         jax.ShapeDtypeStruct((width, rows * columns), BF16),
         [pltpu.VMEM((2 * width, rows * columns), BF16)],
-        10**6, 10**6, "own_network",
+        10000000000, 0, "own_network",
     )(features, features_other, w_in, w_mid, w_out)
     swept, weights, token = call(
         functools.partial(own_sweep_kernel, tracers, levels, rows),
         [jax.ShapeDtypeStruct((rows, width, columns), F32), jax.ShapeDtypeStruct((PLANES, levels, LANES), F32),
          jax.ShapeDtypeStruct((2 * EXTRA, LANES), jnp.int16)],
         [],
-        10**6, 10**6, "own_sweep",
+        10000000000, 0, "own_sweep",
     )(flat, tendency, small, active)
 
     fix_shape = jax.ShapeDtypeStruct((tracers, levels, LANES), F32)
@@ -516,7 +530,7 @@
         functools.partial(edge_network_kernel, tracers, levels, rows, moves),
         [fix_shape, fix_shape],
         [pltpu.VMEM((2 * width, LANES), BF16)],
-        10**9, 4 * 10**6, "edge_network",
+        10000000000, 0, "edge_network",
     )(ring, *corner, weights, w_in, w_mid, w_out)
     fix_other = swap_cores(fix_given)
     edge_other = [swap_cores(e + token[:1]) for e in edge]
@@ -526,13 +540,13 @@
         jax.ShapeDtypeStruct((tracers * W, levels, LANES), F32),
         [pltpu.VMEM((2 * width, total), BF16), pltpu.VMEM((width, total), BF16),
          pltpu.VMEM((count, W * width, LANES), F32)],
-        10**9, 4 * 10**6, "row_network",
+        10000000000, 0, "row_network",
     )(packs, *edge, *edge_other, weights, w_in, w_mid, w_out)
     out = call(
         functools.partial(finish_kernel, tracers, levels, rows, moves),
         jax.ShapeDtypeStruct((width * rows, columns), F32),
         [pltpu.VMEM((width * rows, columns), F32), pltpu.SemaphoreType.DMA((width // HALF_GROUP,))],
-        10**9, 4 * 10**6, "finish",
+        10000000000, 0, "finish",
         out_specs=pl.BlockSpec(memory_space=pltpu.HBM),
     )(swept, weights, fix_mine, fix_other, beyond)
     return out.reshape(fields.shape)

time: 18.2 us -> 17.6 us (0.967)
  starting transfers between devices: 7.65 us -> 7.13 us
  waiting for transfers between devices: 1.47 us -> 1.19 us
    ppermute x3, waiting for transfers between devices: 1.46 us -> 1.18 us  [send(): return lax.ppermute(x, axes, pairs)]
    ppermute x3, starting transfers between devices: 6.43 us -> 6.16 us  [send(): return lax.ppermute(x, axes, pairs)]
    ppermute x4, starting transfers between devices: 1.22 us -> 0.97 us  [swap_cores(): return lax.ppermute(x, 'lev', [(0, 1), (1, 0)])]
  transfers between devices with their start and end apart: 7 -> 7, of which waited for: 2 -> 2; matrix products, arithmetic and copies ran while one was open for 0% -> 0% of each run, Pallas kernels for 33% -> 34%
where the time goes in v4:
time: 17.6 us; the launch traced here: 17.4 us
  Pallas kernels  8.9 us (51%)
  starting transfers between devices  7.13 us (41%)
  waiting for transfers between devices  1.19 us (7%)
    ppermute x3, starting transfers between devices, send(): return lax.ppermute(x, axes, pairs)  6.16 us
    pallas_call x1, Pallas kernels, on_device(): call(functools.partial(edge_kernel, tracers, levels, rows), [pack_shape,...  1.83 us
    pallas_call x1, Pallas kernels, on_device(): call(functools.partial(row_kernel, tracers, levels, moves), jax.ShapeDtyp...  1.51 us
    pallas_call x1, Pallas kernels, on_device(): call(functools.partial(own_network_kernel, tracers, levels, rows), jax.Sh...  1.5 us
    pallas_call x1, Pallas kernels, on_device(): call(functools.partial(edge_network_kernel, tracers, levels, rows, moves)...  1.32 us
    pallas_call x1, Pallas kernels, on_device(): call(functools.partial(own_sweep_kernel, tracers, levels, rows), [jax.Sha...  1.28 us
    ppermute x3, waiting for transfers between devices, send(): return lax.ppermute(x, axes, pairs)  1.18 us
    pallas_call x1, Pallas kernels, on_device(): call(functools.partial(finish_kernel, tracers, levels, rows, moves), jax....  1.15 us
  transfers between devices with their start and end apart: 7, of which 2 were waited for; matrix products, arithmetic and copies ran while one was open for 0% of the time, Pallas kernels for 34%

profile of v4, /device:TPU:0, one launch (start us, length us, event | category | flops | bytes accessed | tf_op | source)
XLA Modules:
  0.0 17.4 jit_solution(13229484998577649800)
XLA Ops:
  0.0 0.0 copy-start
  0.0 1.8 %edges.1 = (f32[104,128]{1,0:T(8,128)S(1)}, f32[104,128]{1,0:T(8,128)S(1)}, f32[8,128]{1,0:T(8,128)S(1)}, f32[8,128]{1,0:T(8,128)S(1)}, bf16[8,192,128]{2,1,0:T(8,128)(2,1)S(1)}) custom-call(f32[1536,128]{1,0:T(8,128)} %bitcast.6, f32[3,64]{1,0:T(4,128)} %refs_1_.1, s32[8,128]{1,0:T(8,128)} %refs_2_.2, s32[4,8]{1,0:T(4,128)} %bitcast.9, f32[3,64]{1,0:T(4,128)} %refs_4_.3, ...), custom_call_target="tpu_custom_call" | custom-call | flops 10000000000 | tf_op jit(solution)/shard_map/edges/pallas_call | solution.py:492
  1.8 0.5 %collective-permute-start.1 = (f32[104,128]{1,0:T(8,128)S(1)}, f32[104,128]{1,0:T(8,128)S(1)}, u32[]{:S(2)}, u32[]{:S(2)}) collective-permute-start(f32[104,128]{1,0:T(8,128)S(1)} %get-tuple-element.21), channel_id=1, source_target_pairs={{0,1},{1,0},{2,3},{3,2},{4,5},{5,4},{6,7},{7,6},{8,9},{9,8},{10,11... | collective-permute-start | bytes 159752 | tf_op jit(solution)/shard_map/ppermute | solution.py:450
  2.4 0.1 collective-permute-start
  2.4 0.0 copy-done
  2.4 0.0 copy-start.1
  2.4 0.0 copy-start.2
  2.4 0.0 copy-start.3
  2.4 0.3 %row_messages.1 = s16[656,128]{1,0:T(8,128)(2,1)S(1)} custom-call(f32[1536,128]{1,0:T(8,128)S(1)} %bitcast.7, f32[8,128]{1,0:T(8,128)S(1)} %get-tuple-element.17.active), custom_call_target="tpu_custom_call" | custom-call | flops 10000000000 | tf_op jit(solution)/shard_map/row_messages/pallas_call | solution.py:503
  2.8 3.0 %collective-permute-start.5 = (s16[656,128]{1,0:T(8,128)(2,1)S(1)}, s16[656,128]{1,0:T(8,128)(2,1)S(1)}, u32[]{:S(2)}, u32[]{:S(2)}) collective-permute-start(s16[656,128]{1,0:T(8,128)(2,1)S(1)} %row_messages.1), channel_id=1, source_target_pairs={{0,2},{1,3},{2,0},{3,1},{4,6},{5,7},{6,4},{7,5},{8,10},{9,11},{10,... | collective-permute-start | bytes 503816 | tf_op jit(solution)/shard_map/ppermute | solution.py:478
  5.8 0.0 collective-permute-done.1
  5.8 1.6 %collective-permute-start.3 = (f32[104,128]{1,0:T(8,128)S(1)}, f32[104,128]{1,0:T(8,128)S(1)}, u32[]{:S(2)}, u32[]{:S(2)}) collective-permute-start(f32[104,128]{1,0:T(8,128)S(1)} %add.13.packs), channel_id=1, source_target_pairs={{0,6},{1,15},{2,4},{3,13},{4,10},{5,3},{6,8},{7,1},{8,14},{9,7},{1... | collective-permute-start | bytes 159752 | tf_op jit(solution)/shard_map/ppermute | solution.py:478
  7.4 1.6 %collective-permute-start.2 = (f32[104,128]{1,0:T(8,128)S(1)}, f32[104,128]{1,0:T(8,128)S(1)}, u32[]{:S(2)}, u32[]{:S(2)}) collective-permute-start(f32[104,128]{1,0:T(8,128)S(1)} %add.13.packs), channel_id=1, source_target_pairs={{0,4},{1,13},{2,6},{3,15},{4,8},{5,1},{6,10},{7,3},{8,12},{9,5},{1... | collective-permute-start | bytes 159752 | tf_op jit(solution)/shard_map/ppermute | solution.py:478
  8.9 0.0 collective-permute-done.other
  8.9 0.0 copy-done.1
  8.9 0.0 copy-done.2
  9.0 0.0 copy-done.3
  9.0 1.5 %own_network.1.tendency = bf16[192,1024]{1,0:T(8,128)(2,1)S(1)} custom-call(bf16[8,192,128]{2,1,0:T(8,128)(2,1)S(1)} %get-tuple-element.15.mine, bf16[8,192,128]{2,1,0:T(8,128)(2,1)S(1)} %collective-permute-done.other, bf16[256,384]{1,0:T(8,128)(2,1)S(1)} %copy-done.2, bf16[3,256,256]{2,1,0:T(8,128)(2,1)S(1)} %copy-done.1, bf16[384,256]{1,0:T(8,128)(2,1)S(1)} %copy-done.3), custom_call_target="tpu_custom_call" | custom-call | flops 10000000000 | tf_op jit(solution)/shard_map/own_network/pallas_call | solution.py:514
  10.5 1.3 %own_sweep.1 = (f32[8,192,128]{2,1,0:T(8,128)S(1)}, f32[18,64,128]{2,1,0:T(8,128)S(1)}, s16[16,128]{1,0:T(8,128)(2,1)S(1)}) custom-call(f32[1536,128]{1,0:T(8,128)S(1)} %bitcast.8, bf16[192,1024]{1,0:T(8,128)(2,1)S(1)} %own_network.1.tendency, f32[8,128]{1,0:T(8,128)S(1)} %get-tuple-element.16.small, f32[8,128]{1,0:T(8,128)S(1)} %get-tuple-element.17.active), custom_call_target="tpu_custom_call" | custom-call | flops 10000000000 | tf_op jit(solution)/shard_map/own_sweep/pallas_call | solution.py:520
  11.8 0.0 collective-permute-done.5.refs_0_
  11.8 0.3 %collective-permute-start.6 = (s16[656,128]{1,0:T(8,128)(2,1)S(1)}, s16[656,128]{1,0:T(8,128)(2,1)S(1)}, u32[]{:S(2)}, u32[]{:S(2)}) collective-permute-start(s16[656,128]{1,0:T(8,128)(2,1)S(1)} %broadcast_add_fusion), channel_id=1, source_target_pairs={{0,1},{1,0},{2,3},{3,2},{4,5},{5,4},{6,7},{7,6},{8,9},{9,8},{10,11... | collective-permute-start | bytes 503816 | tf_op jit(solution)/shard_map/ppermute | solution.py:450
  12.1 0.8 %collective-permute-done.3.refs_0_ = f32[104,128]{1,0:T(8,128)S(1)} collective-permute-done((f32[104,128]{1,0:T(8,128)S(1)}, f32[104,128]{1,0:T(8,128)S(1)}, u32[]{:S(2)}, u32[]{:S(2)}) %collective-permute-start.3) | collective-permute-done | bytes 53280 | tf_op jit(solution)/shard_map/ppermute | solution.py:478
  13.0 0.3 %collective-permute-done.2.ring = f32[104,128]{1,0:T(8,128)S(1)} collective-permute-done((f32[104,128]{1,0:T(8,128)S(1)}, f32[104,128]{1,0:T(8,128)S(1)}, u32[]{:S(2)}, u32[]{:S(2)}) %collective-permute-start.2) | collective-permute-done | bytes 53280 | tf_op jit(solution)/shard_map/ppermute | solution.py:478
  13.3 1.3 %edge_network.1 = (f32[3,64,128]{2,1,0:T(8,128)S(1)}, f32[3,64,128]{2,1,0:T(8,128)S(1)}) custom-call(f32[104,128]{1,0:T(8,128)S(1)} %collective-permute-done.2.ring, f32[104,128]{1,0:T(8,128)S(1)} %collective-permute-done.3.refs_0_, f32[18,64,128]{2,1,0:T(8,128)S(1)} %get-tuple-element.19.refs_1_.refs_2_.weights, bf16[256,384]{1,0:T(8,128)(2,1)S(1)} %copy-done.2, ...), custom_call_target="tpu_custom_call" | custom-call | flops 10000000000 | tf_op jit(solution)/shard_map/edge_network/pallas_call | solution.py:529
  14.6 0.1 collective-permute-start.4
  14.7 0.0 collective-permute-done.6.refs_1_
  14.7 1.5 %row_network.1.beyond = f32[9,64,128]{2,1,0:T(8,128)S(1)} custom-call(f32[104,128]{1,0:T(8,128)S(1)} %add.13.packs, s16[656,128]{1,0:T(8,128)(2,1)S(1)} %collective-permute-done.5.refs_0_, s16[656,128]{1,0:T(8,128)(2,1)S(1)} %collective-permute-done.6.refs_1_, f32[18,64,128]{2,1,0:T(8,128)S(1)} %get-tuple-element.19.refs_1_.refs_2_.weights, ...), custom_call_target="tpu_custom_call" | custom-call | flops 10000000000 | tf_op jit(solution)/shard_map/row_network/pallas_call | solution.py:538
  16.2 0.0 collective-permute-done.4.fix_other
  16.2 1.2 %finish.1 = f32[1536,128]{1,0:T(8,128)} custom-call(f32[8,192,128]{2,1,0:T(8,128)S(1)} %get-tuple-element.18.swept, f32[18,64,128]{2,1,0:T(8,128)S(1)} %get-tuple-element.19.refs_1_.refs_2_.weights, f32[3,64,128]{2,1,0:T(8,128)S(1)} %get-tuple-element.22.fix_mine, f32[3,64,128]{2,1,0:T(8,128)S(1)} %collective-permute-done.4.fix_other, ...), custom_call_target="tpu_custom_call" | custom-call | flops 10000000000 | tf_op jit(solution)/shard_map/finish/pallas_call | solution.py:545
  (3 shorter events, 0.1 us)
Async XLA Ops:
  0.0 2.4 %copy-start = (f32[3,64,8,128]{3,2,1,0:T(8,128)S(1)}, f32[3,64,8,128]{3,2,1,0:T(8,128)}, u32[]{:S(2)}) copy-start(f32[3,64,8,128]{3,2,1,0:T(8,128)} %param.10) | copy-start | bytes 2359300
  1.8 3.9 %collective-permute-start.1 = (f32[104,128]{1,0:T(8,128)S(1)}, f32[104,128]{1,0:T(8,128)S(1)}, u32[]{:S(2)}, u32[]{:S(2)}) collective-permute-start(f32[104,128]{1,0:T(8,128)S(1)} %get-tuple-element.21), channel_id=1, source_target_pairs={{0,1},{1,0},{2,3},{3,2},{4,5},{5,4},{6,7},{7,6},{8,9},{9,8},{10,11... | collective-permute-start | bytes 159752 | tf_op jit(solution)/shard_map/ppermute | solution.py:450
  2.4 6.6 %collective-permute-start = (bf16[8,192,128]{2,1,0:T(8,128)(2,1)S(1)}, bf16[8,192,128]{2,1,0:T(8,128)(2,1)S(1)}, u32[]{:S(2)}, u32[]{:S(2)}) collective-permute-start(bf16[8,192,128]{2,1,0:T(8,128)(2,1)S(1)} %get-tuple-element.15.mine), channel_id=1, source_target_pairs={{0,1},{1,0},{2,3},{3,2},{4,5},{5,4},{6,7},{7,6},{8,9},{9,8},{10,11... | collective-permute-start | bytes 1179656 | tf_op jit(solution)/shard_map/ppermute | solution.py:450
  2.4 6.5 %copy-start.1 = (bf16[3,256,256]{2,1,0:T(8,128)(2,1)S(1)}, bf16[3,256,256]{2,1,0:T(8,128)(2,1)}, u32[]{:S(2)}) copy-start(bf16[3,256,256]{2,1,0:T(8,128)(2,1)} %refs_4_.5) | copy-start | bytes 1179652
  2.4 6.5 %copy-start.2 = (bf16[256,384]{1,0:T(8,128)(2,1)S(1)}, bf16[256,384]{1,0:T(8,128)(2,1)}, u32[]{:S(2)}) copy-start(bf16[256,384]{1,0:T(8,128)(2,1)} %refs_3_.3) | copy-start | bytes 589828
  2.4 6.5 %copy-start.3 = (bf16[384,256]{1,0:T(8,128)(2,1)S(1)}, bf16[384,256]{1,0:T(8,128)(2,1)}, u32[]{:S(2)}) copy-start(bf16[384,256]{1,0:T(8,128)(2,1)} %refs_5_.3) | copy-start | bytes 589828
  2.8 9.0 %collective-permute-start.5 = (s16[656,128]{1,0:T(8,128)(2,1)S(1)}, s16[656,128]{1,0:T(8,128)(2,1)S(1)}, u32[]{:S(2)}, u32[]{:S(2)}) collective-permute-start(s16[656,128]{1,0:T(8,128)(2,1)S(1)} %row_messages.1), channel_id=1, source_target_pairs={{0,2},{1,3},{2,0},{3,1},{4,6},{5,7},{6,4},{7,5},{8,10},{9,11},{10,... | collective-permute-start | bytes 503816 | tf_op jit(solution)/shard_map/ppermute | solution.py:478
  5.8 7.2 %collective-permute-start.3 = (f32[104,128]{1,0:T(8,128)S(1)}, f32[104,128]{1,0:T(8,128)S(1)}, u32[]{:S(2)}, u32[]{:S(2)}) collective-permute-start(f32[104,128]{1,0:T(8,128)S(1)} %add.13.packs), channel_id=1, source_target_pairs={{0,6},{1,15},{2,4},{3,13},{4,10},{5,3},{6,8},{7,1},{8,14},{9,7},{1... | collective-permute-start | bytes 159752 | tf_op jit(solution)/shard_map/ppermute | solution.py:478
  7.4 5.9 %collective-permute-start.2 = (f32[104,128]{1,0:T(8,128)S(1)}, f32[104,128]{1,0:T(8,128)S(1)}, u32[]{:S(2)}, u32[]{:S(2)}) collective-permute-start(f32[104,128]{1,0:T(8,128)S(1)} %add.13.packs), channel_id=1, source_target_pairs={{0,4},{1,13},{2,6},{3,15},{4,8},{5,1},{6,10},{7,3},{8,12},{9,5},{1... | collective-permute-start | bytes 159752 | tf_op jit(solution)/shard_map/ppermute | solution.py:478
  11.8 2.9 %collective-permute-start.6 = (s16[656,128]{1,0:T(8,128)(2,1)S(1)}, s16[656,128]{1,0:T(8,128)(2,1)S(1)}, u32[]{:S(2)}, u32[]{:S(2)}) collective-permute-start(s16[656,128]{1,0:T(8,128)(2,1)S(1)} %broadcast_add_fusion), channel_id=1, source_target_pairs={{0,1},{1,0},{2,3},{3,2},{4,5},{5,4},{6,7},{7,6},{8,9},{9,8},{10,11... | collective-permute-start | bytes 503816 | tf_op jit(solution)/shard_map/ppermute | solution.py:450
  14.6 1.6 %collective-permute-start.4 = (f32[3,64,128]{2,1,0:T(8,128)S(1)}, f32[3,64,128]{2,1,0:T(8,128)S(1)}, u32[]{:S(2)}, u32[]{:S(2)}) collective-permute-start(f32[3,64,128]{2,1,0:T(8,128)S(1)} %get-tuple-element.23), channel_id=1, source_target_pairs={{0,1},{1,0},{2,3},{3,2},{4,5},{5,4},{6,7},{7,6},{8,9},{9,8},{10,11... | collective-permute-start | bytes 294920 | tf_op jit(solution)/shard_map/ppermute | solution.py:450

commit v5 on v4

--- a/solution.py
+++ b/solution.py
@@ -214,11 +214,14 @@
     )
 
 
-def narrow_network(x, w_in, w_mid, w_last):
+def first_layer(x, w_in):
+    return silu(lax.dot_general(x, w_in, (((0,), (1,)), ((), ())), preferred_element_type=F32)).astype(BF16)
+
+
+def further_layers(hidden, w_mid, w_last):
     def layer(hidden, w):
         return lax.dot_general(hidden, w, (((1,), (1,)), ((), ())), preferred_element_type=F32)
 
-    hidden = silu(lax.dot_general(x, w_in, (((0,), (1,)), ((), ())), preferred_element_type=F32)).astype(BF16)
     for k in range(len(w_mid)):
         hidden = silu(layer(hidden, w_mid[k])).astype(BF16)
     return layer(w_last, hidden).astype(BF16)
@@ -264,7 +267,8 @@
     return [w[0] * q + w[1] * turned(q, 1) + w[2] * turned(q, 2) + w[3] * turned(q, 3) for q in values]
 
 
-def own_network_kernel(tracers, levels, rows, mine, other, w_in, w_mid, w_out, tendency, x):
+def own_network_kernel(tracers, levels, rows, mine, other, w_in, w_mid, w_out, tendency, token, x):
+    token[...] = jnp.zeros_like(token)
     lev = lax.axis_index("lev")
     width = tracers * levels
     near = pl.ds(pl.multiple_of(lev * width, width), width)
@@ -276,8 +280,7 @@
     tendency[...] = network(x[...], w_in[...], w_mid, w_last)
 
 
-def own_sweep_kernel(tracers, levels, rows, fields, tendency, small, active, swept, weights, token):
-    token[...] = jnp.zeros_like(token)
+def own_sweep_kernel(tracers, levels, rows, fields, tendency, small, active, swept, weights):
     write_weights(weights, small, tracers, levels)
     for g in range(0, levels, GROUP):
         span = slice(g, g + GROUP)
@@ -298,9 +301,36 @@
     return jnp.broadcast_to(message[:levels, at : at + 1], (levels, LANES))
 
 
-def edge_network_kernel(tracers, levels, rows, moves, ring, *refs):
+def row_input_kernel(tracers, levels, moves, packs, *refs):
     count = len(moves)
-    corner, (weights, w_in, w_mid, w_out, mine, other, x) = refs[:count], refs[count:]
+    edge, edge_other, (w_in, hidden, fields, masks, x) = refs[:count], refs[count : 2 * count], refs[2 * count :]
+    lev = lax.axis_index("lev")
+    width = tracers * levels
+    tail = W * width
+    for which, source in ((0, edge), (1, edge_other)):
+        start = lev * width if which == 0 else (1 - lev) * width
+        for n in range(count):
+            unit = inverse_scale(from_fixed(source[n][tail : tail + levels, :])) * (1.0 / FIXED_ONE)
+            for t in range(tracers):
+                in_scale = read_scale(packs, which, t, tracers, levels)
+                scale = jnp.broadcast_to(unit[:, t : t + 1], (levels, LANES))
+                to = pl.ds(pl.multiple_of(start + t * levels, levels), levels)
+                parts = [(r * tracers + t) * levels for r in range(W)]
+                values = [from_fixed(source[n][part : part + levels, :]) * scale for part in parts]
+                for r, value in enumerate(values):
+                    column_at = (n * W + r) * LANES
+                    x[to, column_at : column_at + LANES] = (value * in_scale).astype(BF16)
+                    if which == 0:
+                        fields[n, t * W + r] = value
+    for n in range(count):
+        masks[n] = from_fixed(edge[n][tail + levels :, :])
+    hidden[...] = first_layer(x[...], w_in[...])
+
+
+def halo_network_kernel(tracers, levels, rows, moves, _, ring, *refs):
+    count = len(moves)
+    corner = refs[:count]
+    weights, w_in, w_mid, w_out, mine, other, x = refs[count:]
     lat, lev = lax.axis_index("lat"), lax.axis_index("lev")
     width = tracers * levels
     head = lev == 0
@@ -341,7 +371,7 @@
             halos.append(value)
             scales.append(out_scale)
             x[pl.ds(pl.multiple_of(start + t * levels, levels), levels), :] = (value * in_scale).astype(BF16)
-    tendency = narrow_network(x[...], w_in[...], w_mid, w_out[...]).astype(F32)
+    tendency = further_layers(first_layer(x[...], w_in[...]), w_mid, w_out[...]).astype(F32)
     x_tendency = [tendency[n * levels : (n + 1) * levels] for n in range(2 * tracers)]
     x_tendency = [
         jnp.where(head, x_tendency[n], x_tendency[(n + tracers) % (2 * tracers)]) for n in range(2 * tracers)
@@ -358,41 +388,21 @@
         other[t] = fix[tracers + t]
 
 
-def row_kernel(tracers, levels, moves, packs, *refs):
-    count = len(moves)
-    edge, edge_other, (weights, w_in, w_mid, w_out, beyond, x, tendency, fields) = refs[:count], refs[count : 2 * count], refs[2 * count :]
+def row_kernel(tracers, levels, moves, hidden, fields, masks, weights, w_mid, w_out, beyond, tendency):
     lev = lax.axis_index("lev")
     width = tracers * levels
     near = pl.ds(pl.multiple_of(lev * width, width), width)
-    tail = W * tracers * levels
-    for which, source in ((0, edge), (1, edge_other)):
-        start = lev * width if which == 0 else (1 - lev) * width
-        unscale = [inverse_scale(from_fixed(source[n][tail : tail + levels, :])) * (1.0 / FIXED_ONE) for n in range(count)]
-        for t in range(tracers):
-            in_scale = read_scale(packs, which, t, tracers, levels)
-            to = pl.ds(pl.multiple_of(start + t * levels, levels), levels)
-            for n in range(count):
-                scale = jnp.broadcast_to(unscale[n][:, t : t + 1], (levels, LANES))
-                for r in range(W):
-                    column_at = (n * W + r) * LANES
-                    part = (r * tracers + t) * levels
-                    value = from_fixed(source[n][part : part + levels, :]) * scale
-                    x[to, column_at : column_at + LANES] = (value * in_scale).astype(BF16)
-                    if which == 0:
-                        fields[n, part : part + levels, :] = value
-    masks = [from_fixed(e[tail + levels :, :]) for e in edge]
-    tendency[...] = narrow_network(x[...], w_in[...], w_mid, w_out[near, :])
+    tendency[...] = further_layers(hidden[...], w_mid, w_out[near, :])
     up = weights[LAT_SIGN] > 0.5
     values = []
     for t in range(tracers):
         for r in range(W):
             rows_q = []
-            for n in range(count):
+            for n in range(len(moves)):
                 column_at = (n * W + r) * LANES
                 moist = tendency[t * levels : (t + 1) * levels, column_at : column_at + LANES].astype(F32)
-                value = fields[n, (r * tracers + t) * levels : (r * tracers + t + 1) * levels, :]
-                rows_q.append(value + weights[OUT_SCALE + t] * moist * masks[n][r : r + 1, :])
-            values.append(jnp.where(up, rows_q[0], rows_q[1]) if count > 1 else rows_q[0])
+                rows_q.append(fields[n, t * W + r] + weights[OUT_SCALE + t] * moist * masks[n, r : r + 1, :])
+            values.append(jnp.where(up, rows_q[0], rows_q[1]) if len(moves) == 2 else rows_q[0])
     for n, q in enumerate(sweep_lon(values, weights, slice(0, levels))):
         beyond[n] = q
 
@@ -511,37 +521,43 @@
     ring = send(packs, None, True)
     edge = [send(e, move, False) for e, move in zip(edge_rows, moves)]
 
-    tendency = call(
+    tendency, token = call(
         functools.partial(own_network_kernel, tracers, levels, rows),
-        jax.ShapeDtypeStruct((width, rows * columns), BF16),
+        [jax.ShapeDtypeStruct((width, rows * columns), BF16), jax.ShapeDtypeStruct((2 * EXTRA, LANES), jnp.int16)],
         [pltpu.VMEM((2 * width, rows * columns), BF16)],
         10000000000, 0, "own_network",
     )(features, features_other, w_in, w_mid, w_out)
-    swept, weights, token = call(
+    swept, weights = call(
         functools.partial(own_sweep_kernel, tracers, levels, rows),
-        [jax.ShapeDtypeStruct((rows, width, columns), F32), jax.ShapeDtypeStruct((PLANES, levels, LANES), F32),
-         jax.ShapeDtypeStruct((2 * EXTRA, LANES), jnp.int16)],
+        [jax.ShapeDtypeStruct((rows, width, columns), F32), jax.ShapeDtypeStruct((PLANES, levels, LANES), F32)],
         [],
         10000000000, 0, "own_sweep",
     )(flat, tendency, small, active)
 
     fix_shape = jax.ShapeDtypeStruct((tracers, levels, LANES), F32)
+    edge_other = [swap_cores(e + token[:1]) for e in edge]
+    total = W * count * LANES
+    physics_shape = jax.ShapeDtypeStruct((count, tracers * W, levels, LANES), F32)
+    hidden, row_fields, row_masks = call(
+        functools.partial(row_input_kernel, tracers, levels, moves),
+        [jax.ShapeDtypeStruct((total, w_in.shape[0]), BF16), physics_shape,
+         jax.ShapeDtypeStruct((count, 2 * EXTRA, LANES), F32)],
+        [pltpu.VMEM((2 * width, total), BF16)],
+        10**10, 0, "row_input",
+    )(packs, *edge, *edge_other, w_in)
     fix_mine, fix_given = call(
-        functools.partial(edge_network_kernel, tracers, levels, rows, moves),
+        functools.partial(halo_network_kernel, tracers, levels, rows, moves),
         [fix_shape, fix_shape],
         [pltpu.VMEM((2 * width, LANES), BF16)],
-        10000000000, 0, "edge_network",
-    )(ring, *corner, weights, w_in, w_mid, w_out)
+        10**10, 0, "halo_network",
+    )(row_masks, ring, *corner, weights, w_in, w_mid, w_out)
     fix_other = swap_cores(fix_given)
-    edge_other = [swap_cores(e + token[:1]) for e in edge]
-    total = W * count * LANES
     beyond = call(
         functools.partial(row_kernel, tracers, levels, moves),
         jax.ShapeDtypeStruct((tracers * W, levels, LANES), F32),
-        [pltpu.VMEM((2 * width, total), BF16), pltpu.VMEM((width, total), BF16),
-         pltpu.VMEM((count, W * width, LANES), F32)],
-        10000000000, 0, "row_network",
-    )(packs, *edge, *edge_other, weights, w_in, w_mid, w_out)
+        [pltpu.VMEM((width, total), BF16)],
+        10**10, 0, "row_network",
+    )(hidden, row_fields, row_masks, weights, w_mid, w_out)
     out = call(
         functools.partial(finish_kernel, tracers, levels, rows, moves),
         jax.ShapeDtypeStruct((width * rows, columns), F32),

time: 17.6 us -> 17.3 us (0.983)
  starting transfers between devices: 7.13 us -> 6.94 us
    pallas_call x2 -> x3, Pallas kernels: 2.82 us -> 3.37 us  [the longest x1 1.49 us: on_device(): call(functools.partial(own_network_kernel, tracers, levels, rows), [jax.S...]
    pallas_call x1, Pallas kernels: 1.51 us -> 1.06 us  [on_device(): call(functools.partial(row_kernel, tracers, levels, moves), jax.ShapeDtyp...]
    ppermute x3, waiting for transfers between devices: 1.18 us -> 0.75 us  [send(): return lax.ppermute(x, axes, pairs)]
    ppermute x4, waiting for transfers between devices: 0.01 us -> 0.3 us  [swap_cores(): return lax.ppermute(x, 'lev', [(0, 1), (1, 0)])]
    ppermute x4, starting transfers between devices: 0.97 us -> 0.78 us  [swap_cores(): return lax.ppermute(x, 'lev', [(0, 1), (1, 0)])]
  transfers between devices with their start and end apart: 7 -> 7, of which waited for: 2 -> 4; matrix products, arithmetic and copies ran while one was open for 0% -> 0% of each run, Pallas kernels for 34% -> 27%
where the time goes in v5:
time: 17.3 us; the launch traced here: 17.1 us
  Pallas kernels  8.99 us (52%)
  starting transfers between devices  6.94 us (40%)
  waiting for transfers between devices  1.05 us (6%)
    ppermute x3, starting transfers between devices, send(): return lax.ppermute(x, axes, pairs)  6.16 us
    pallas_call x1, Pallas kernels, on_device(): call(functools.partial(edge_kernel, tracers, levels, rows), [pack_shape,...  1.83 us
    pallas_call x1, Pallas kernels, on_device(): call(functools.partial(own_network_kernel, tracers, levels, rows), [jax.S...  1.49 us
    pallas_call x1, Pallas kernels, on_device(): call(functools.partial(halo_network_kernel, tracers, levels, rows, moves)...  1.32 us
    pallas_call x1, Pallas kernels, on_device(): call(functools.partial(own_sweep_kernel, tracers, levels, rows), [jax.Sha...  1.28 us
    pallas_call x1, Pallas kernels, on_device(): call(functools.partial(finish_kernel, tracers, levels, rows, moves), jax....  1.15 us
    pallas_call x1, Pallas kernels, on_device(): call(functools.partial(row_kernel, tracers, levels, moves), jax.ShapeDtyp...  1.06 us
    ppermute x4, starting transfers between devices, swap_cores(): return lax.ppermute(x, 'lev', [(0, 1), (1, 0)])  0.78 us
  transfers between devices with their start and end apart: 7, of which 4 were waited for; matrix products, arithmetic and copies ran while one was open for 0% of the time, Pallas kernels for 27%

profile of v5, /device:TPU:0, one launch (start us, length us, event | category | flops | bytes accessed | tf_op | source)
XLA Modules:
  0.0 17.1 jit_solution(14891815772141873303)
XLA Ops:
  0.0 0.0 copy-start
  0.0 1.8 %edges.1 = (f32[104,128]{1,0:T(8,128)S(1)}, f32[104,128]{1,0:T(8,128)S(1)}, f32[8,128]{1,0:T(8,128)S(1)}, f32[8,128]{1,0:T(8,128)S(1)}, bf16[8,192,128]{2,1,0:T(8,128)(2,1)S(1)}) custom-call(f32[1536,128]{1,0:T(8,128)} %bitcast.6, f32[3,64]{1,0:T(4,128)} %refs_1_.1, s32[8,128]{1,0:T(8,128)} %refs_2_.3, s32[4,8]{1,0:T(4,128)} %bitcast.9, f32[3,64]{1,0:T(4,128)} %refs_4_.2, ...), custom_call_target="tpu_custom_call" | custom-call | flops 10000000000 | tf_op jit(solution)/shard_map/edges/pallas_call | solution.py:502
  1.8 0.5 %collective-permute-start.1 = (f32[104,128]{1,0:T(8,128)S(1)}, f32[104,128]{1,0:T(8,128)S(1)}, u32[]{:S(2)}, u32[]{:S(2)}) collective-permute-start(f32[104,128]{1,0:T(8,128)S(1)} %get-tuple-element.26), channel_id=1, source_target_pairs={{0,1},{1,0},{2,3},{3,2},{4,5},{5,4},{6,7},{7,6},{8,9},{9,8},{10,11... | collective-permute-start | bytes 159752 | tf_op jit(solution)/shard_map/ppermute | solution.py:460
  2.4 0.1 collective-permute-start
  2.4 0.0 copy-done
  2.4 0.0 copy-start.1
  2.4 0.0 copy-start.2
  2.4 0.0 copy-start.3
  2.4 0.3 %row_messages.1 = s16[656,128]{1,0:T(8,128)(2,1)S(1)} custom-call(f32[1536,128]{1,0:T(8,128)S(1)} %bitcast.7, f32[8,128]{1,0:T(8,128)S(1)} %get-tuple-element.22.active), custom_call_target="tpu_custom_call" | custom-call | flops 10000000000 | tf_op jit(solution)/shard_map/row_messages/pallas_call | solution.py:513
  2.8 3.0 %collective-permute-start.2 = (s16[656,128]{1,0:T(8,128)(2,1)S(1)}, s16[656,128]{1,0:T(8,128)(2,1)S(1)}, u32[]{:S(2)}, u32[]{:S(2)}) collective-permute-start(s16[656,128]{1,0:T(8,128)(2,1)S(1)} %row_messages.1), channel_id=1, source_target_pairs={{0,2},{1,3},{2,0},{3,1},{4,6},{5,7},{6,4},{7,5},{8,10},{9,11},{10,... | collective-permute-start | bytes 503816 | tf_op jit(solution)/shard_map/ppermute | solution.py:488
  5.8 0.0 collective-permute-done.1
  5.8 1.6 %collective-permute-start.5 = (f32[104,128]{1,0:T(8,128)S(1)}, f32[104,128]{1,0:T(8,128)S(1)}, u32[]{:S(2)}, u32[]{:S(2)}) collective-permute-start(f32[104,128]{1,0:T(8,128)S(1)} %add.13.packs), channel_id=1, source_target_pairs={{0,6},{1,15},{2,4},{3,13},{4,10},{5,3},{6,8},{7,1},{8,14},{9,7},{1... | collective-permute-start | bytes 159752 | tf_op jit(solution)/shard_map/ppermute | solution.py:488
  7.4 1.6 %collective-permute-start.4 = (f32[104,128]{1,0:T(8,128)S(1)}, f32[104,128]{1,0:T(8,128)S(1)}, u32[]{:S(2)}, u32[]{:S(2)}) collective-permute-start(f32[104,128]{1,0:T(8,128)S(1)} %add.13.packs), channel_id=1, source_target_pairs={{0,4},{1,13},{2,6},{3,15},{4,8},{5,1},{6,10},{7,3},{8,12},{9,5},{1... | collective-permute-start | bytes 159752 | tf_op jit(solution)/shard_map/ppermute | solution.py:488
  8.9 0.0 collective-permute-done.other
  8.9 0.0 copy-done.1
  8.9 0.0 copy-done.2
  9.0 0.0 copy-done.3
  9.0 1.5 %own_network.1 = (bf16[192,1024]{1,0:T(8,128)(2,1)S(1)}, s16[16,128]{1,0:T(8,128)(2,1)S(1)}) custom-call(bf16[8,192,128]{2,1,0:T(8,128)(2,1)S(1)} %get-tuple-element.19.mine, bf16[8,192,128]{2,1,0:T(8,128)(2,1)S(1)} %collective-permute-done.other, bf16[256,384]{1,0:T(8,128)(2,1)S(1)} %copy-done.2, bf16[3,256,256]{2,1,0:T(8,128)(2,1)S(1)} %copy-done.1, ...), custom_call_target="tpu_custom_call" | custom-call | flops 10000000000 | tf_op jit(solution)/shard_map/own_network/pallas_call | solution.py:524
  10.5 0.4 %collective-permute-done.2.refs_0_ = s16[656,128]{1,0:T(8,128)(2,1)S(1)} collective-permute-done((s16[656,128]{1,0:T(8,128)(2,1)S(1)}, s16[656,128]{1,0:T(8,128)(2,1)S(1)}, u32[]{:S(2)}, u32[]{:S(2)}) %collective-permute-start.2) | collective-permute-done | bytes 167968 | tf_op jit(solution)/shard_map/ppermute | solution.py:488
  10.9 0.1 collective-permute-start.3
  11.0 1.3 %own_sweep.1 = (f32[8,192,128]{2,1,0:T(8,128)S(1)}, f32[18,64,128]{2,1,0:T(8,128)S(1)}) custom-call(f32[1536,128]{1,0:T(8,128)S(1)} %bitcast.8, bf16[192,1024]{1,0:T(8,128)(2,1)S(1)} %get-tuple-element.20.tendency, f32[8,128]{1,0:T(8,128)S(1)} %get-tuple-element.21.small, f32[8,128]{1,0:T(8,128)S(1)} %get-tuple-element.22.active), custom_call_target="tpu_custom_call" | custom-call | flops 10000000000 | tf_op jit(solution)/shard_map/own_sweep/pallas_call | solution.py:530
  12.3 0.1 collective-permute-done.3.refs_1_
  12.4 0.6 %row_input.1 = (bf16[384,256]{1,0:T(8,128)(2,1)S(1)}, f32[1,9,64,128]{3,2,1,0:T(8,128)S(1)}, f32[1,16,128]{2,1,0:T(8,128)S(1)}) custom-call(f32[104,128]{1,0:T(8,128)S(1)} %add.13.packs, s16[656,128]{1,0:T(8,128)(2,1)S(1)} %collective-permute-done.2.refs_0_, s16[656,128]{1,0:T(8,128)(2,1)S(1)} %collective-permute-done.3.refs_1_, bf16[256,384]{1,0:T(8,128)(2,1)S(1)} %copy-done.2), custom_call_target="tpu_custom_call" | custom-call | flops 10000000000 | tf_op jit(solution)/shard_map/row_input/pallas_call | solution.py:541
  12.9 0.0 collective-permute-done.5.refs_0_
  13.0 0.3 %collective-permute-done.4.ring = f32[104,128]{1,0:T(8,128)S(1)} collective-permute-done((f32[104,128]{1,0:T(8,128)S(1)}, f32[104,128]{1,0:T(8,128)S(1)}, u32[]{:S(2)}, u32[]{:S(2)}) %collective-permute-start.4) | collective-permute-done | bytes 53280 | tf_op jit(solution)/shard_map/ppermute | solution.py:488
  13.3 1.3 %halo_network.1 = (f32[3,64,128]{2,1,0:T(8,128)S(1)}, f32[3,64,128]{2,1,0:T(8,128)S(1)}) custom-call(f32[1,16,128]{2,1,0:T(8,128)S(1)} %get-tuple-element.28._.masks, f32[104,128]{1,0:T(8,128)S(1)} %collective-permute-done.4.ring, f32[104,128]{1,0:T(8,128)S(1)} %collective-permute-done.5.refs_0_, f32[18,64,128]{2,1,0:T(8,128)S(1)} %get-tuple-element.24.refs_1_.weights, ...), custom_call_target="tpu_custom_call" | custom-call | flops 10000000000 | tf_op jit(solution)/shard_map/halo_network/pallas_call | solution.py:548
  14.6 0.1 collective-permute-start.6
  14.7 1.1 %row_network.1.beyond = f32[9,64,128]{2,1,0:T(8,128)S(1)} custom-call(bf16[384,256]{1,0:T(8,128)(2,1)S(1)} %get-tuple-element.31.hidden, f32[1,9,64,128]{3,2,1,0:T(8,128)S(1)} %get-tuple-element.32.fields, f32[1,16,128]{2,1,0:T(8,128)S(1)} %get-tuple-element.28._.masks, f32[18,64,128]{2,1,0:T(8,128)S(1)} %get-tuple-element.24.refs_1_.weights, ...), custom_call_target="tpu_custom_call" | custom-call | flops 10000000000 | tf_op jit(solution)/shard_map/row_network/pallas_call | solution.py:555
  15.8 0.2 %collective-permute-done.6.fix_other = f32[3,64,128]{2,1,0:T(8,128)S(1)} collective-permute-done((f32[3,64,128]{2,1,0:T(8,128)S(1)}, f32[3,64,128]{2,1,0:T(8,128)S(1)}, u32[]{:S(2)}, u32[]{:S(2)}) %collective-permute-start.6) | collective-permute-done | bytes 98336 | tf_op jit(solution)/shard_map/ppermute | solution.py:460
  16.0 1.1 %finish.1 = f32[1536,128]{1,0:T(8,128)} custom-call(f32[8,192,128]{2,1,0:T(8,128)S(1)} %get-tuple-element.23.swept, f32[18,64,128]{2,1,0:T(8,128)S(1)} %get-tuple-element.24.refs_1_.weights, f32[3,64,128]{2,1,0:T(8,128)S(1)} %get-tuple-element.29.fix_mine, f32[3,64,128]{2,1,0:T(8,128)S(1)} %collective-permute-done.6.fix_other, ...), custom_call_target="tpu_custom_call" | custom-call | flops 10000000000 | tf_op jit(solution)/shard_map/finish/pallas_call | solution.py:561
  (3 shorter events, 0.0 us)
Async XLA Ops:
  0.0 2.4 %copy-start = (f32[3,64,8,128]{3,2,1,0:T(8,128)S(1)}, f32[3,64,8,128]{3,2,1,0:T(8,128)}, u32[]{:S(2)}) copy-start(f32[3,64,8,128]{3,2,1,0:T(8,128)} %param.10) | copy-start | bytes 2359300
  1.8 3.9 %collective-permute-start.1 = (f32[104,128]{1,0:T(8,128)S(1)}, f32[104,128]{1,0:T(8,128)S(1)}, u32[]{:S(2)}, u32[]{:S(2)}) collective-permute-start(f32[104,128]{1,0:T(8,128)S(1)} %get-tuple-element.26), channel_id=1, source_target_pairs={{0,1},{1,0},{2,3},{3,2},{4,5},{5,4},{6,7},{7,6},{8,9},{9,8},{10,11... | collective-permute-start | bytes 159752 | tf_op jit(solution)/shard_map/ppermute | solution.py:460
  2.4 6.6 %collective-permute-start = (bf16[8,192,128]{2,1,0:T(8,128)(2,1)S(1)}, bf16[8,192,128]{2,1,0:T(8,128)(2,1)S(1)}, u32[]{:S(2)}, u32[]{:S(2)}) collective-permute-start(bf16[8,192,128]{2,1,0:T(8,128)(2,1)S(1)} %get-tuple-element.19.mine), channel_id=1, source_target_pairs={{0,1},{1,0},{2,3},{3,2},{4,5},{5,4},{6,7},{7,6},{8,9},{9,8},{10,11... | collective-permute-start | bytes 1179656 | tf_op jit(solution)/shard_map/ppermute | solution.py:460
  2.4 6.5 %copy-start.1 = (bf16[3,256,256]{2,1,0:T(8,128)(2,1)S(1)}, bf16[3,256,256]{2,1,0:T(8,128)(2,1)}, u32[]{:S(2)}) copy-start(bf16[3,256,256]{2,1,0:T(8,128)(2,1)} %w_mid.3) | copy-start | bytes 1179652
  2.4 6.5 %copy-start.2 = (bf16[256,384]{1,0:T(8,128)(2,1)S(1)}, bf16[256,384]{1,0:T(8,128)(2,1)}, u32[]{:S(2)}) copy-start(bf16[256,384]{1,0:T(8,128)(2,1)} %refs_2_.5) | copy-start | bytes 589828
  2.4 6.5 %copy-start.3 = (bf16[384,256]{1,0:T(8,128)(2,1)S(1)}, bf16[384,256]{1,0:T(8,128)(2,1)}, u32[]{:S(2)}) copy-start(bf16[384,256]{1,0:T(8,128)(2,1)} %w_out.3) | copy-start | bytes 589828
  2.8 8.1 %collective-permute-start.2 = (s16[656,128]{1,0:T(8,128)(2,1)S(1)}, s16[656,128]{1,0:T(8,128)(2,1)S(1)}, u32[]{:S(2)}, u32[]{:S(2)}) collective-permute-start(s16[656,128]{1,0:T(8,128)(2,1)S(1)} %row_messages.1), channel_id=1, source_target_pairs={{0,2},{1,3},{2,0},{3,1},{4,6},{5,7},{6,4},{7,5},{8,10},{9,11},{10,... | collective-permute-start | bytes 503816 | tf_op jit(solution)/shard_map/ppermute | solution.py:488
  5.8 7.2 %collective-permute-start.5 = (f32[104,128]{1,0:T(8,128)S(1)}, f32[104,128]{1,0:T(8,128)S(1)}, u32[]{:S(2)}, u32[]{:S(2)}) collective-permute-start(f32[104,128]{1,0:T(8,128)S(1)} %add.13.packs), channel_id=1, source_target_pairs={{0,6},{1,15},{2,4},{3,13},{4,10},{5,3},{6,8},{7,1},{8,14},{9,7},{1... | collective-permute-start | bytes 159752 | tf_op jit(solution)/shard_map/ppermute | solution.py:488
  7.4 5.9 %collective-permute-start.4 = (f32[104,128]{1,0:T(8,128)S(1)}, f32[104,128]{1,0:T(8,128)S(1)}, u32[]{:S(2)}, u32[]{:S(2)}) collective-permute-start(f32[104,128]{1,0:T(8,128)S(1)} %add.13.packs), channel_id=1, source_target_pairs={{0,4},{1,13},{2,6},{3,15},{4,8},{5,1},{6,10},{7,3},{8,12},{9,5},{1... | collective-permute-start | bytes 159752 | tf_op jit(solution)/shard_map/ppermute | solution.py:488
  10.9 1.5 %collective-permute-start.3 = (s16[656,128]{1,0:T(8,128)(2,1)S(1)}, s16[656,128]{1,0:T(8,128)(2,1)S(1)}, u32[]{:S(2)}, u32[]{:S(2)}) collective-permute-start(s16[656,128]{1,0:T(8,128)(2,1)S(1)} %broadcast_add_fusion), channel_id=1, source_target_pairs={{0,1},{1,0},{2,3},{3,2},{4,5},{5,4},{6,7},{7,6},{8,9},{9,8},{10,11... | collective-permute-start | bytes 503816 | tf_op jit(solution)/shard_map/ppermute | solution.py:460
  14.6 1.4 %collective-permute-start.6 = (f32[3,64,128]{2,1,0:T(8,128)S(1)}, f32[3,64,128]{2,1,0:T(8,128)S(1)}, u32[]{:S(2)}, u32[]{:S(2)}) collective-permute-start(f32[3,64,128]{2,1,0:T(8,128)S(1)} %get-tuple-element.30), channel_id=1, source_target_pairs={{0,1},{1,0},{2,3},{3,2},{4,5},{5,4},{6,7},{7,6},{8,9},{9,8},{10,11... | collective-permute-start | bytes 294920 | tf_op jit(solution)/shard_map/ppermute | solution.py:460

commit v6 on v5

--- a/solution.py
+++ b/solution.py
@@ -63,19 +63,13 @@
     return last, first
 
 
-def edge_kernel(tracers, levels, rows, *refs):
-    sources, (keep, give, active, small, features), refs = refs[:7], refs[7:12], refs[12:]
-    (fields, in_scale, storm, balance, *loads), scratch, sems = refs[:7], refs[7], refs[8]
-    part = levels * rows
-    chunks = [
-        pltpu.make_async_copy(sources[0].at[pl.ds(t * part, part)], fields.at[pl.ds(t * part, part)], sems.at[t])
-        for t in range(tracers)
+def scalar_kernel(tracers, levels, rows, *refs):
+    sources, (small, active, scale_lanes, mask_rows, in_scales), refs = refs[:6], refs[6:11], refs[11:]
+    (in_scale, storm, balance, *loads), scratch, sems = refs[:6], refs[6], refs[7]
+    copies = [
+        pltpu.make_async_copy(source, into, sems.at[n]) for n, (source, into) in enumerate(zip(sources, refs[:6]))
     ]
-    copies = [
-        pltpu.make_async_copy(source, into, sems.at[tracers + n])
-        for n, (source, into) in enumerate(zip(sources[1:], (in_scale, storm, balance, *loads)))
-    ]
-    for copy in copies + chunks:
+    for copy in copies:
         copy.start()
     for copy in copies:
         copy.wait()
@@ -96,6 +90,9 @@
         scale = column(scales, n, levels)
         own_scales = jnp.where(lane == SCALE_LANE + n, scale, own_scales)
         given_scales = jnp.where(lane == SCALE_LANE + 2 * tracers + n, scale, given_scales)
+        if n < tracers:
+            in_scales[n] = scale
+    scale_lanes[0], scale_lanes[1] = own_scales, given_scales
     lane = lane_ids(1)
     mask_pack = jnp.zeros((1, LANES), F32)
     for i in range(rows):
@@ -104,26 +101,33 @@
     east = lane % 6 < 3
     last_mask = jnp.where(east, mask_pack, 0.0)
     first_mask = turned(jnp.where(east, 0.0, mask_pack), -W)
+    head = lev == 0
+    mask_rows[0] = jnp.where(head, last_mask, first_mask)
+    mask_rows[1] = turned(jnp.where(head, first_mask, last_mask), HALF_LANES)
+
+
+def edge_kernel(tracers, levels, rows, fields, scale_lanes, mask_rows, in_scales, keep, give, features):
+    lane = lane_ids(levels)
     half = levels // 2
-    head = lev == 0
-    keep[levels + half :] = jnp.where(head, last_mask, first_mask)
-    give[levels + half :] = turned(jnp.where(head, first_mask, last_mask), HALF_LANES)
-    lane = lane_ids(levels)
-    edges = []
+    head = lax.axis_index("lev") == 0
+    edges, values = [], []
     for t in range(tracers):
-        chunks[t].wait()
-        scale = column(scales, t, levels)
         pack = jnp.zeros((levels, LANES), F32)
         for i in range(rows):
-            x = fields[pl.ds(t * part + i, levels, stride=rows), :]
-            features[i, t * levels : (t + 1) * levels, :] = (x * scale).astype(BF16)
+            x = fields[pl.ds((t * levels) * rows + i, levels, stride=rows), :]
+            values.append((x * in_scales[t]).astype(BF16))
             pack = jnp.where((lane >= 6 * i) & (lane < 6 * i + 6), turned(x, 6 * i + W), pack)
         edges.append(pack)
     last, first = side_messages(edges)
-    keep[:levels] = jnp.where(head, last[0], first[0]) + own_scales
-    give[:levels] = turned(jnp.where(head, first[0], last[0]), HALF_LANES) + given_scales
+    keep[:levels] = jnp.where(head, last[0], first[0]) + scale_lanes[0]
+    give[:levels] = turned(jnp.where(head, first[0], last[0]), HALF_LANES) + scale_lanes[1]
     keep[levels : levels + half] = jnp.where(head, last[1], first[1])
     give[levels : levels + half] = turned(jnp.where(head, first[1], last[1]), HALF_LANES)
+    keep[levels + half :] = mask_rows[0]
+    give[levels + half :] = mask_rows[1]
+    for n, x in enumerate(values):
+        t, i = n // rows, n % rows
+        features[i, t * levels : (t + 1) * levels, :] = x
 
 
 def binary_scale(largest):
@@ -327,6 +331,12 @@
     hidden[...] = first_layer(x[...], w_in[...])
 
 
+def edge_corrections(values, weights, head):
+    east = jnp.where(head, LANES - 1, 1), jnp.where(head, LANES - 2, 2)
+    w = [jnp.where(head, weights[EDGE + 2 * k], weights[EDGE + 2 * k - 1]) for k in (1, 2)]
+    return [weights[EDGE] * q + w[0] * turned(q, east[0]) + w[1] * turned(q, east[1]) for q in values]
+
+
 def halo_network_kernel(tracers, levels, rows, moves, _, ring, *refs):
     count = len(moves)
     corner = refs[:count]
@@ -380,16 +390,16 @@
     if count == 2:
         up = weights[LAT_SIGN] > 0.5
         values = [jnp.where(up | (lane < 48), q, turned(q, -18)) for q in values]
-    fix = [weights[EDGE] * q for q in values]
-    for k, shift in ((1, 1), (2, -1), (3, 2), (4, -2)):
-        fix = [f + weights[EDGE + k] * turned(q, shift) for f, q in zip(fix, values)]
+    for t, q in enumerate(edge_corrections(values[tracers:], weights, head)):
+        other[t] = q
     for t in range(tracers):
-        mine[t] = fix[t]
-        other[t] = fix[tracers + t]
-
-
-def row_kernel(tracers, levels, moves, hidden, fields, masks, weights, w_mid, w_out, beyond, tendency):
+        mine[t] = values[t]
+
+
+def row_kernel(tracers, levels, moves, hidden, fields, masks, halo, weights, w_mid, w_out, beyond, fix, tendency):
     lev = lax.axis_index("lev")
+    for t, q in enumerate(edge_corrections([halo[t] for t in range(tracers)], weights, lev == 0)):
+        fix[t] = q
     width = tracers * levels
     near = pl.ds(pl.multiple_of(lev * width, width), width)
     tendency[...] = further_layers(hidden[...], w_mid, w_out[near, :])
@@ -496,18 +506,24 @@
     flat = fields.reshape(width * rows, columns)
     edge_shape = jax.ShapeDtypeStruct((W * width + levels + 2 * EXTRA, columns), jnp.int16)
     pack_shape = jax.ShapeDtypeStruct((levels + levels // 2 + EXTRA, LANES), F32)
-    inputs = (flat, in_scale, storm_mask, balance.T, out_scale, courant, substeps.reshape(1, levels))
+    inputs = (in_scale, storm_mask, balance.T, out_scale, courant, substeps.reshape(1, levels))
     inputs = [pltpu.with_memory_space_constraint(x, pltpu.HBM) for x in inputs]
-    small_shape = jax.ShapeDtypeStruct((EXTRA, LANES), F32)
-    keep, give, active, small, features = call(
-        functools.partial(edge_kernel, tracers, levels, rows),
-        [pack_shape, pack_shape, jax.ShapeDtypeStruct((rows, columns), F32), small_shape,
-         jax.ShapeDtypeStruct((rows, width, columns), BF16)],
+    small, active, scale_lanes, mask_rows, in_scales = call(
+        functools.partial(scalar_kernel, tracers, levels, rows),
+        [jax.ShapeDtypeStruct((EXTRA, LANES), F32), jax.ShapeDtypeStruct((rows, columns), F32),
+         jax.ShapeDtypeStruct((2, levels, LANES), F32), jax.ShapeDtypeStruct((2, EXTRA, LANES), F32),
+         jax.ShapeDtypeStruct((tracers, levels, LANES), F32)],
         [pltpu.VMEM(x.shape, x.dtype) for x in inputs]
-        + [pltpu.VMEM((EXTRA, LANES), F32), pltpu.SemaphoreType.DMA((len(inputs) - 1 + tracers,))],
-        10000000000, 0, "edges",
+        + [pltpu.VMEM((EXTRA, LANES), F32), pltpu.SemaphoreType.DMA((len(inputs),))],
+        10**10, 0, "scalars",
         in_specs=[pl.BlockSpec(memory_space=pltpu.HBM)] * len(inputs),
     )(*inputs)
+    keep, give, features = call(
+        functools.partial(edge_kernel, tracers, levels, rows),
+        [pack_shape, pack_shape, jax.ShapeDtypeStruct((rows, width, columns), BF16)],
+        [],
+        10**10, 0, "edges",
+    )(flat, scale_lanes, mask_rows, in_scales)
     given = swap_cores(give)
     features_other = swap_cores(features)
     edge_rows = call(
@@ -545,19 +561,19 @@
         [pltpu.VMEM((2 * width, total), BF16)],
         10**10, 0, "row_input",
     )(packs, *edge, *edge_other, w_in)
-    fix_mine, fix_given = call(
+    halo, fix_given = call(
         functools.partial(halo_network_kernel, tracers, levels, rows, moves),
         [fix_shape, fix_shape],
         [pltpu.VMEM((2 * width, LANES), BF16)],
         10**10, 0, "halo_network",
     )(row_masks, ring, *corner, weights, w_in, w_mid, w_out)
     fix_other = swap_cores(fix_given)
-    beyond = call(
+    beyond, fix_mine = call(
         functools.partial(row_kernel, tracers, levels, moves),
-        jax.ShapeDtypeStruct((tracers * W, levels, LANES), F32),
+        [jax.ShapeDtypeStruct((tracers * W, levels, LANES), F32), fix_shape],
         [pltpu.VMEM((width, total), BF16)],
         10**10, 0, "row_network",
-    )(hidden, row_fields, row_masks, weights, w_mid, w_out)
+    )(hidden, row_fields, row_masks, halo, weights, w_mid, w_out)
     out = call(
         functools.partial(finish_kernel, tracers, levels, rows, moves),
         jax.ShapeDtypeStruct((width * rows, columns), F32),

time: 17.3 us -> 16.9 us (0.977)
  Pallas kernels: 8.99 us -> 8.67 us
    pallas_call x1, Pallas kernels: 1.83 us -> 0.43 us  [on_device(): call(functools.partial(edge_kernel, tracers, levels, rows), [pack_shape,...]
    pallas_call x1 -> x2, Pallas kernels: 1.06 us -> 2.3 us  [the longest x1 1.25 us: on_device(): call(functools.partial(scalar_kernel, tracers, levels, rows), [jax.ShapeD...]
  transfers between devices with their start and end apart: 7 -> 7, of which waited for: 4 -> 4; matrix products, arithmetic and copies ran while one was open for 0% -> 0% of each run, Pallas kernels for 27% -> 28%
where the time goes in v6:
time: 16.9 us; the launch traced here: 16.8 us
  Pallas kernels  8.67 us (51%)
  starting transfers between devices  6.9 us (41%)
  waiting for transfers between devices  1.05 us (6%)
    ppermute x3, starting transfers between devices, send(): return lax.ppermute(x, axes, pairs)  6.16 us
    pallas_call x1, Pallas kernels, on_device(): call(functools.partial(own_network_kernel, tracers, levels, rows), [jax.S...  1.49 us
    pallas_call x1, Pallas kernels, on_device(): call(functools.partial(own_sweep_kernel, tracers, levels, rows), [jax.Sha...  1.28 us
    pallas_call x1, Pallas kernels, on_device(): call(functools.partial(scalar_kernel, tracers, levels, rows), [jax.ShapeD...  1.25 us
    pallas_call x1, Pallas kernels, on_device(): call(functools.partial(halo_network_kernel, tracers, levels, rows, moves)...  1.17 us
    pallas_call x1, Pallas kernels, on_device(): call(functools.partial(finish_kernel, tracers, levels, rows, moves), jax....  1.14 us
    pallas_call x1, Pallas kernels, on_device(): call(functools.partial(row_kernel, tracers, levels, moves), [jax.ShapeDty...  1.05 us
    ppermute x3, waiting for transfers between devices, send(): return lax.ppermute(x, axes, pairs)  0.75 us
  transfers between devices with their start and end apart: 7, of which 4 were waited for; matrix products, arithmetic and copies ran while one was open for 0% of the time, Pallas kernels for 28%

profile of v6, /device:TPU:0, one launch (start us, length us, event | category | flops | bytes accessed | tf_op | source)
XLA Modules:
  0.0 16.8 jit_solution(9407793639578126690)
XLA Ops:
  0.0 0.0 copy-start
  0.0 1.2 %scalars.1 = (f32[8,128]{1,0:T(8,128)S(1)}, f32[8,128]{1,0:T(8,128)S(1)}, f32[2,64,128]{2,1,0:T(8,128)S(1)}, f32[2,8,128]{2,1,0:T(8,128)S(1)}, f32[3,64,128]{2,1,0:T(8,128)S(1)}) custom-call(f32[3,64]{1,0:T(4,128)} %refs_0_.1, s32[8,128]{1,0:T(8,128)} %refs_1_.1, s32[4,8]{1,0:T(4,128)} %bitcast.9, f32[3,64]{1,0:T(4,128)} %refs_3_.2, f32[2,64]{1,0:T(2,128)} %refs_4_.2, ...), custom_call_target="tpu_custom_call" | custom-call | flops 10000000000 | tf_op jit(solution)/shard_map/scalars/pallas_call | solution.py:511
  1.3 0.0 copy-done
  1.3 0.4 %edges.1 = (f32[104,128]{1,0:T(8,128)S(1)}, f32[104,128]{1,0:T(8,128)S(1)}, bf16[8,192,128]{2,1,0:T(8,128)(2,1)S(1)}) custom-call(f32[1536,128]{1,0:T(8,128)S(1)} %bitcast.6, f32[2,64,128]{2,1,0:T(8,128)S(1)} %get-tuple-element.24.scale_lanes, f32[2,8,128]{2,1,0:T(8,128)S(1)} %get-tuple-element.25.mask_rows, f32[3,64,128]{2,1,0:T(8,128)S(1)} %get-tuple-element.26.in_scales), custom_call_target="tpu_custom_call" | custom-call | flops 10000000000 | tf_op jit(solution)/shard_map/edges/pallas_call | solution.py:521
  1.7 0.5 %collective-permute-start.1 = (f32[104,128]{1,0:T(8,128)S(1)}, f32[104,128]{1,0:T(8,128)S(1)}, u32[]{:S(2)}, u32[]{:S(2)}) collective-permute-start(f32[104,128]{1,0:T(8,128)S(1)} %get-tuple-element.34), channel_id=1, source_target_pairs={{0,1},{1,0},{2,3},{3,2},{4,5},{5,4},{6,7},{7,6},{8,9},{9,8},{10,11... | collective-permute-start | bytes 159752 | tf_op jit(solution)/shard_map/ppermute | solution.py:470
  2.2 0.1 collective-permute-start
  2.3 0.0 copy-start.1
  2.3 0.0 copy-start.2
  2.3 0.0 copy-start.3
  2.3 0.3 %row_messages.1 = s16[656,128]{1,0:T(8,128)(2,1)S(1)} custom-call(f32[1536,128]{1,0:T(8,128)S(1)} %bitcast.7, f32[8,128]{1,0:T(8,128)S(1)} %get-tuple-element.30.active), custom_call_target="tpu_custom_call" | custom-call | flops 10000000000 | tf_op jit(solution)/shard_map/row_messages/pallas_call | solution.py:529
  2.6 3.0 %collective-permute-start.2 = (s16[656,128]{1,0:T(8,128)(2,1)S(1)}, s16[656,128]{1,0:T(8,128)(2,1)S(1)}, u32[]{:S(2)}, u32[]{:S(2)}) collective-permute-start(s16[656,128]{1,0:T(8,128)(2,1)S(1)} %row_messages.1), channel_id=1, source_target_pairs={{0,2},{1,3},{2,0},{3,1},{4,6},{5,7},{6,4},{7,5},{8,10},{9,11},{10,... | collective-permute-start | bytes 503816 | tf_op jit(solution)/shard_map/ppermute | solution.py:498
  5.6 0.0 collective-permute-done.1
  5.6 1.6 %collective-permute-start.5 = (f32[104,128]{1,0:T(8,128)S(1)}, f32[104,128]{1,0:T(8,128)S(1)}, u32[]{:S(2)}, u32[]{:S(2)}) collective-permute-start(f32[104,128]{1,0:T(8,128)S(1)} %add.13.packs), channel_id=1, source_target_pairs={{0,6},{1,15},{2,4},{3,13},{4,10},{5,3},{6,8},{7,1},{8,14},{9,7},{1... | collective-permute-start | bytes 159752 | tf_op jit(solution)/shard_map/ppermute | solution.py:498
  7.2 1.6 %collective-permute-start.4 = (f32[104,128]{1,0:T(8,128)S(1)}, f32[104,128]{1,0:T(8,128)S(1)}, u32[]{:S(2)}, u32[]{:S(2)}) collective-permute-start(f32[104,128]{1,0:T(8,128)S(1)} %add.13.packs), channel_id=1, source_target_pairs={{0,4},{1,13},{2,6},{3,15},{4,8},{5,1},{6,10},{7,3},{8,12},{9,5},{1... | collective-permute-start | bytes 159752 | tf_op jit(solution)/shard_map/ppermute | solution.py:498
  8.8 0.0 collective-permute-done.other
  8.8 0.0 copy-done.1
  8.8 0.0 copy-done.2
  8.8 0.0 copy-done.3
  8.8 1.5 %own_network.1 = (bf16[192,1024]{1,0:T(8,128)(2,1)S(1)}, s16[16,128]{1,0:T(8,128)(2,1)S(1)}) custom-call(bf16[8,192,128]{2,1,0:T(8,128)(2,1)S(1)} %get-tuple-element.27.mine, bf16[8,192,128]{2,1,0:T(8,128)(2,1)S(1)} %collective-permute-done.other, bf16[256,384]{1,0:T(8,128)(2,1)S(1)} %copy-done.2, bf16[3,256,256]{2,1,0:T(8,128)(2,1)S(1)} %copy-done.1, ...), custom_call_target="tpu_custom_call" | custom-call | flops 10000000000 | tf_op jit(solution)/shard_map/own_network/pallas_call | solution.py:540
  10.3 0.4 %collective-permute-done.2.refs_0_ = s16[656,128]{1,0:T(8,128)(2,1)S(1)} collective-permute-done((s16[656,128]{1,0:T(8,128)(2,1)S(1)}, s16[656,128]{1,0:T(8,128)(2,1)S(1)}, u32[]{:S(2)}, u32[]{:S(2)}) %collective-permute-start.2) | collective-permute-done | bytes 167968 | tf_op jit(solution)/shard_map/ppermute | solution.py:498
  10.7 0.1 collective-permute-start.3
  10.8 1.3 %own_sweep.1 = (f32[8,192,128]{2,1,0:T(8,128)S(1)}, f32[18,64,128]{2,1,0:T(8,128)S(1)}) custom-call(f32[1536,128]{1,0:T(8,128)S(1)} %bitcast.8, bf16[192,1024]{1,0:T(8,128)(2,1)S(1)} %get-tuple-element.28.tendency, f32[8,128]{1,0:T(8,128)S(1)} %get-tuple-element.29.small, f32[8,128]{1,0:T(8,128)S(1)} %get-tuple-element.30.active), custom_call_target="tpu_custom_call" | custom-call | flops 10000000000 | tf_op jit(solution)/shard_map/own_sweep/pallas_call | solution.py:546
  12.1 0.1 collective-permute-done.3.refs_1_
  12.2 0.6 %row_input.1 = (bf16[384,256]{1,0:T(8,128)(2,1)S(1)}, f32[1,9,64,128]{3,2,1,0:T(8,128)S(1)}, f32[1,16,128]{2,1,0:T(8,128)S(1)}) custom-call(f32[104,128]{1,0:T(8,128)S(1)} %add.13.packs, s16[656,128]{1,0:T(8,128)(2,1)S(1)} %collective-permute-done.2.refs_0_, s16[656,128]{1,0:T(8,128)(2,1)S(1)} %collective-permute-done.3.refs_1_, bf16[256,384]{1,0:T(8,128)(2,1)S(1)} %copy-done.2), custom_call_target="tpu_custom_call" | custom-call | flops 10000000000 | tf_op jit(solution)/shard_map/row_input/pallas_call | solution.py:557
  12.7 0.0 collective-permute-done.5.refs_0_
  12.8 0.3 %collective-permute-done.4.ring = f32[104,128]{1,0:T(8,128)S(1)} collective-permute-done((f32[104,128]{1,0:T(8,128)S(1)}, f32[104,128]{1,0:T(8,128)S(1)}, u32[]{:S(2)}, u32[]{:S(2)}) %collective-permute-start.4) | collective-permute-done | bytes 53280 | tf_op jit(solution)/shard_map/ppermute | solution.py:498
  13.1 1.2 %halo_network.1 = (f32[3,64,128]{2,1,0:T(8,128)S(1)}, f32[3,64,128]{2,1,0:T(8,128)S(1)}) custom-call(f32[1,16,128]{2,1,0:T(8,128)S(1)} %get-tuple-element.38._.masks, f32[104,128]{1,0:T(8,128)S(1)} %collective-permute-done.4.ring, f32[104,128]{1,0:T(8,128)S(1)} %collective-permute-done.5.refs_0_, f32[18,64,128]{2,1,0:T(8,128)S(1)} %get-tuple-element.32.refs_1_.weights, ...), custom_call_target="tpu_custom_call" | custom-call | flops 10000000000 | tf_op jit(solution)/shard_map/halo_network/pallas_call | solution.py:564
  14.3 0.1 collective-permute-start.6
  14.4 1.1 %row_network.1 = (f32[9,64,128]{2,1,0:T(8,128)S(1)}, f32[3,64,128]{2,1,0:T(8,128)S(1)}) custom-call(bf16[384,256]{1,0:T(8,128)(2,1)S(1)} %get-tuple-element.36.hidden, f32[1,9,64,128]{3,2,1,0:T(8,128)S(1)} %get-tuple-element.37.fields, f32[1,16,128]{2,1,0:T(8,128)S(1)} %get-tuple-element.38._.masks, f32[3,64,128]{2,1,0:T(8,128)S(1)} %get-tuple-element.39.halo, ...), custom_call_target="tpu_custom_call" | custom-call | flops 10000000000 | tf_op jit(solution)/shard_map/row_network/pallas_call | solution.py:571
  15.5 0.2 %collective-permute-done.6.fix_other = f32[3,64,128]{2,1,0:T(8,128)S(1)} collective-permute-done((f32[3,64,128]{2,1,0:T(8,128)S(1)}, f32[3,64,128]{2,1,0:T(8,128)S(1)}, u32[]{:S(2)}, u32[]{:S(2)}) %collective-permute-start.6) | collective-permute-done | bytes 98336 | tf_op jit(solution)/shard_map/ppermute | solution.py:470
  15.7 1.1 %finish.1 = f32[1536,128]{1,0:T(8,128)} custom-call(f32[8,192,128]{2,1,0:T(8,128)S(1)} %get-tuple-element.31.swept, f32[18,64,128]{2,1,0:T(8,128)S(1)} %get-tuple-element.32.refs_1_.weights, f32[3,64,128]{2,1,0:T(8,128)S(1)} %get-tuple-element.40.fix_mine, f32[3,64,128]{2,1,0:T(8,128)S(1)} %collective-permute-done.6.fix_other, ...), custom_call_target="tpu_custom_call" | custom-call | flops 10000000000 | tf_op jit(solution)/shard_map/finish/pallas_call | solution.py:577
  (3 shorter events, 0.0 us)
Async XLA Ops:
  0.0 1.3 %copy-start = (f32[3,64,8,128]{3,2,1,0:T(8,128)S(1)}, f32[3,64,8,128]{3,2,1,0:T(8,128)}, u32[]{:S(2)}) copy-start(f32[3,64,8,128]{3,2,1,0:T(8,128)} %param.10) | copy-start | bytes 2359300
  1.7 3.9 %collective-permute-start.1 = (f32[104,128]{1,0:T(8,128)S(1)}, f32[104,128]{1,0:T(8,128)S(1)}, u32[]{:S(2)}, u32[]{:S(2)}) collective-permute-start(f32[104,128]{1,0:T(8,128)S(1)} %get-tuple-element.34), channel_id=1, source_target_pairs={{0,1},{1,0},{2,3},{3,2},{4,5},{5,4},{6,7},{7,6},{8,9},{9,8},{10,11... | collective-permute-start | bytes 159752 | tf_op jit(solution)/shard_map/ppermute | solution.py:470
  2.2 6.6 %collective-permute-start = (bf16[8,192,128]{2,1,0:T(8,128)(2,1)S(1)}, bf16[8,192,128]{2,1,0:T(8,128)(2,1)S(1)}, u32[]{:S(2)}, u32[]{:S(2)}) collective-permute-start(bf16[8,192,128]{2,1,0:T(8,128)(2,1)S(1)} %get-tuple-element.27.mine), channel_id=1, source_target_pairs={{0,1},{1,0},{2,3},{3,2},{4,5},{5,4},{6,7},{7,6},{8,9},{9,8},{10,11... | collective-permute-start | bytes 1179656 | tf_op jit(solution)/shard_map/ppermute | solution.py:470
  2.3 6.5 %copy-start.1 = (bf16[3,256,256]{2,1,0:T(8,128)(2,1)S(1)}, bf16[3,256,256]{2,1,0:T(8,128)(2,1)}, u32[]{:S(2)}) copy-start(bf16[3,256,256]{2,1,0:T(8,128)(2,1)} %w_mid.3) | copy-start | bytes 1179652
  2.3 6.5 %copy-start.2 = (bf16[256,384]{1,0:T(8,128)(2,1)S(1)}, bf16[256,384]{1,0:T(8,128)(2,1)}, u32[]{:S(2)}) copy-start(bf16[256,384]{1,0:T(8,128)(2,1)} %refs_2_.3) | copy-start | bytes 589828
  2.3 6.5 %copy-start.3 = (bf16[384,256]{1,0:T(8,128)(2,1)S(1)}, bf16[384,256]{1,0:T(8,128)(2,1)}, u32[]{:S(2)}) copy-start(bf16[384,256]{1,0:T(8,128)(2,1)} %w_out.3) | copy-start | bytes 589828
  2.6 8.1 %collective-permute-start.2 = (s16[656,128]{1,0:T(8,128)(2,1)S(1)}, s16[656,128]{1,0:T(8,128)(2,1)S(1)}, u32[]{:S(2)}, u32[]{:S(2)}) collective-permute-start(s16[656,128]{1,0:T(8,128)(2,1)S(1)} %row_messages.1), channel_id=1, source_target_pairs={{0,2},{1,3},{2,0},{3,1},{4,6},{5,7},{6,4},{7,5},{8,10},{9,11},{10,... | collective-permute-start | bytes 503816 | tf_op jit(solution)/shard_map/ppermute | solution.py:498
  5.6 7.2 %collective-permute-start.5 = (f32[104,128]{1,0:T(8,128)S(1)}, f32[104,128]{1,0:T(8,128)S(1)}, u32[]{:S(2)}, u32[]{:S(2)}) collective-permute-start(f32[104,128]{1,0:T(8,128)S(1)} %add.13.packs), channel_id=1, source_target_pairs={{0,6},{1,15},{2,4},{3,13},{4,10},{5,3},{6,8},{7,1},{8,14},{9,7},{1... | collective-permute-start | bytes 159752 | tf_op jit(solution)/shard_map/ppermute | solution.py:498
  7.2 5.9 %collective-permute-start.4 = (f32[104,128]{1,0:T(8,128)S(1)}, f32[104,128]{1,0:T(8,128)S(1)}, u32[]{:S(2)}, u32[]{:S(2)}) collective-permute-start(f32[104,128]{1,0:T(8,128)S(1)} %add.13.packs), channel_id=1, source_target_pairs={{0,4},{1,13},{2,6},{3,15},{4,8},{5,1},{6,10},{7,3},{8,12},{9,5},{1... | collective-permute-start | bytes 159752 | tf_op jit(solution)/shard_map/ppermute | solution.py:498
  10.7 1.5 %collective-permute-start.3 = (s16[656,128]{1,0:T(8,128)(2,1)S(1)}, s16[656,128]{1,0:T(8,128)(2,1)S(1)}, u32[]{:S(2)}, u32[]{:S(2)}) collective-permute-start(s16[656,128]{1,0:T(8,128)(2,1)S(1)} %broadcast_add_fusion), channel_id=1, source_target_pairs={{0,1},{1,0},{2,3},{3,2},{4,5},{5,4},{6,7},{7,6},{8,9},{9,8},{10,11... | collective-permute-start | bytes 503816 | tf_op jit(solution)/shard_map/ppermute | solution.py:470
  14.3 1.4 %collective-permute-start.6 = (f32[3,64,128]{2,1,0:T(8,128)S(1)}, f32[3,64,128]{2,1,0:T(8,128)S(1)}, u32[]{:S(2)}, u32[]{:S(2)}) collective-permute-start(f32[3,64,128]{2,1,0:T(8,128)S(1)} %get-tuple-element.41), channel_id=1, source_target_pairs={{0,1},{1,0},{2,3},{3,2},{4,5},{5,4},{6,7},{7,6},{8,9},{9,8},{10,11... | collective-permute-start | bytes 294920 | tf_op jit(solution)/shard_map/ppermute | solution.py:470

commit v7 on v6

--- a/solution.py
+++ b/solution.py
@@ -10,6 +10,7 @@
 W = 3
 LANES = 128
 HALF_LANES = 48
+TARGET_ROW = 6
 SCALE_LANE = 96
 FIELD_BOUND = 8.0
 FIXED_ONE = 32768.0 / FIELD_BOUND
@@ -64,26 +65,19 @@
 
 
 def scalar_kernel(tracers, levels, rows, *refs):
-    sources, (small, active, scale_lanes, mask_rows, in_scales), refs = refs[:6], refs[6:11], refs[11:]
+    sources, (small, mask, scale_lanes, in_scales), refs = refs[:6], refs[6:10], refs[10:]
     (in_scale, storm, balance, *loads), scratch, sems = refs[:6], refs[6], refs[7]
     copies = [
         pltpu.make_async_copy(source, into, sems.at[n]) for n, (source, into) in enumerate(zip(sources, refs[:6]))
     ]
     for copy in copies:
         copy.start()
-    for copy in copies:
+    for copy in copies[:4]:
         copy.wait()
-    small[...] = jnp.zeros_like(small)
-    at = 0
-    for load in loads:
-        small[at : at + load.shape[0], : load.shape[1]] = load[...].astype(F32)
-        at += load.shape[0]
-    lon, lev = lax.axis_index("lon"), lax.axis_index("lev")
+    lon = lax.axis_index("lon")
     position = lax.broadcasted_iota(jnp.int32, balance.shape, 0)
     target = jnp.max(jnp.where(position == lon, balance[...], -1).astype(F32), axis=0, keepdims=True)
-    scales = as_columns(scratch, [in_scale[...], loads[0][...], target])
-    mask = jnp.where(column(scales, 2 * tracers, rows) >= 0.0, storm[...].astype(F32), 0.0)
-    active[...] = mask
+    scales = as_columns(scratch, [in_scale[...], loads[0][...]])
     lane = lane_ids(levels)
     own_scales, given_scales = jnp.zeros((levels, LANES), F32), jnp.zeros((levels, LANES), F32)
     for n in range(2 * tracers):
@@ -93,20 +87,18 @@
         if n < tracers:
             in_scales[n] = scale
     scale_lanes[0], scale_lanes[1] = own_scales, given_scales
-    lane = lane_ids(1)
-    mask_pack = jnp.zeros((1, LANES), F32)
-    for i in range(rows):
-        mask_pack = jnp.where((lane >= 6 * i) & (lane < 6 * i + 6), turned(mask[i : i + 1, :], 6 * i + W), mask_pack)
-    mask_pack = jnp.broadcast_to(mask_pack, (EXTRA, LANES))
-    east = lane % 6 < 3
-    last_mask = jnp.where(east, mask_pack, 0.0)
-    first_mask = turned(jnp.where(east, 0.0, mask_pack), -W)
-    head = lev == 0
-    mask_rows[0] = jnp.where(head, last_mask, first_mask)
-    mask_rows[1] = turned(jnp.where(head, first_mask, last_mask), HALF_LANES)
-
-
-def edge_kernel(tracers, levels, rows, fields, scale_lanes, mask_rows, in_scales, keep, give, features):
+    for copy in copies[4:]:
+        copy.wait()
+    small[...] = jnp.zeros_like(small)
+    at = 0
+    for load in loads:
+        small[at : at + load.shape[0], : load.shape[1]] = load[...].astype(F32)
+        at += load.shape[0]
+    small[at : at + 1, :rows] = target
+    mask[...] = storm[...].astype(F32)
+
+
+def edge_kernel(tracers, levels, rows, fields, small, storm, scale_lanes, in_scales, keep, give, active, features):
     lane = lane_ids(levels)
     half = levels // 2
     head = lax.axis_index("lev") == 0
@@ -118,13 +110,24 @@
             values.append((x * in_scales[t]).astype(BF16))
             pack = jnp.where((lane >= 6 * i) & (lane < 6 * i + 6), turned(x, 6 * i + W), pack)
         edges.append(pack)
+    mask = jnp.where(column(small[...].T, TARGET_ROW, rows) >= 0.0, storm[...], 0.0)
+    lane = lane_ids(rows)
+    row = lax.broadcasted_iota(jnp.int32, (rows, LANES), 0)
+    mask_pack = pltpu.roll(mask, W, 1, stride=6, stride_axis=0)
+    mask_pack = jnp.where((lane >= 6 * row) & (lane < 6 * row + 6), mask_pack, 0.0)
+    mask_pack = jnp.broadcast_to(jnp.sum(mask_pack, axis=0, keepdims=True), (EXTRA, LANES))
+    lane = lane_ids(1)
+    east = lane % 6 < 3
+    last_mask = jnp.where(east, mask_pack, 0.0)
+    first_mask = turned(jnp.where(east, 0.0, mask_pack), -W)
+    keep[levels + half :] = jnp.where(head, last_mask, first_mask)
+    give[levels + half :] = turned(jnp.where(head, first_mask, last_mask), HALF_LANES)
     last, first = side_messages(edges)
     keep[:levels] = jnp.where(head, last[0], first[0]) + scale_lanes[0]
     give[:levels] = turned(jnp.where(head, first[0], last[0]), HALF_LANES) + scale_lanes[1]
     keep[levels : levels + half] = jnp.where(head, last[1], first[1])
     give[levels : levels + half] = turned(jnp.where(head, first[1], last[1]), HALF_LANES)
-    keep[levels + half :] = mask_rows[0]
-    give[levels + half :] = mask_rows[1]
+    active[...] = mask
     for n, x in enumerate(values):
         t, i = n // rows, n % rows
         features[i, t * levels : (t + 1) * levels, :] = x
@@ -508,22 +511,22 @@
     pack_shape = jax.ShapeDtypeStruct((levels + levels // 2 + EXTRA, LANES), F32)
     inputs = (in_scale, storm_mask, balance.T, out_scale, courant, substeps.reshape(1, levels))
     inputs = [pltpu.with_memory_space_constraint(x, pltpu.HBM) for x in inputs]
-    small, active, scale_lanes, mask_rows, in_scales = call(
+    mask_shape = jax.ShapeDtypeStruct((rows, columns), F32)
+    small, storm, scale_lanes, in_scales = call(
         functools.partial(scalar_kernel, tracers, levels, rows),
-        [jax.ShapeDtypeStruct((EXTRA, LANES), F32), jax.ShapeDtypeStruct((rows, columns), F32),
-         jax.ShapeDtypeStruct((2, levels, LANES), F32), jax.ShapeDtypeStruct((2, EXTRA, LANES), F32),
+        [jax.ShapeDtypeStruct((EXTRA, LANES), F32), mask_shape, jax.ShapeDtypeStruct((2, levels, LANES), F32),
          jax.ShapeDtypeStruct((tracers, levels, LANES), F32)],
         [pltpu.VMEM(x.shape, x.dtype) for x in inputs]
         + [pltpu.VMEM((EXTRA, LANES), F32), pltpu.SemaphoreType.DMA((len(inputs),))],
         10**10, 0, "scalars",
         in_specs=[pl.BlockSpec(memory_space=pltpu.HBM)] * len(inputs),
     )(*inputs)
-    keep, give, features = call(
+    keep, give, active, features = call(
         functools.partial(edge_kernel, tracers, levels, rows),
-        [pack_shape, pack_shape, jax.ShapeDtypeStruct((rows, width, columns), BF16)],
+        [pack_shape, pack_shape, mask_shape, jax.ShapeDtypeStruct((rows, width, columns), BF16)],
         [],
         10**10, 0, "edges",
-    )(flat, scale_lanes, mask_rows, in_scales)
+    )(flat, small, storm, scale_lanes, in_scales)
     given = swap_cores(give)
     features_other = swap_cores(features)
     edge_rows = call(

time: 16.9 us -> 16.9 us (level)
  no operation moved by 1% of the time
where the time goes in v7:
time: 16.9 us; the launch traced here: 16.8 us
  Pallas kernels  8.54 us (51%)
  starting transfers between devices  6.9 us (41%)
  waiting for transfers between devices  1.05 us (6%)
    ppermute x3, starting transfers between devices, send(): return lax.ppermute(x, axes, pairs)  6.16 us
    pallas_call x1, Pallas kernels, on_device(): call(functools.partial(own_network_kernel, tracers, levels, rows), [jax.S...  1.5 us
    pallas_call x1, Pallas kernels, on_device(): call(functools.partial(own_sweep_kernel, tracers, levels, rows), [jax.Sha...  1.28 us
    pallas_call x1, Pallas kernels, on_device(): call(functools.partial(halo_network_kernel, tracers, levels, rows, moves)...  1.17 us
    pallas_call x1, Pallas kernels, on_device(): call(functools.partial(finish_kernel, tracers, levels, rows, moves), jax....  1.14 us
    pallas_call x1, Pallas kernels, on_device(): call(functools.partial(scalar_kernel, tracers, levels, rows), [jax.ShapeD...  1.09 us
    pallas_call x1, Pallas kernels, on_device(): call(functools.partial(row_kernel, tracers, levels, moves), [jax.ShapeDty...  1.06 us
    ppermute x3, waiting for transfers between devices, send(): return lax.ppermute(x, axes, pairs)  0.75 us
  transfers between devices with their start and end apart: 7, of which 4 were waited for; matrix products, arithmetic and copies ran while one was open for 0% of the time, Pallas kernels for 28%

profile of v7, /device:TPU:0, one launch (start us, length us, event | category | flops | bytes accessed | tf_op | source)
XLA Modules:
  0.0 16.8 jit_solution(14121679520145919647)
XLA Ops:
  0.0 0.0 copy-start
  0.0 1.1 %scalars.1 = (f32[8,128]{1,0:T(8,128)S(1)}, f32[8,128]{1,0:T(8,128)S(1)}, f32[2,64,128]{2,1,0:T(8,128)S(1)}, f32[3,64,128]{2,1,0:T(8,128)S(1)}) custom-call(f32[3,64]{1,0:T(4,128)} %refs_0_.1, s32[8,128]{1,0:T(8,128)} %refs_1_.1, s32[4,8]{1,0:T(4,128)} %bitcast.9, f32[3,64]{1,0:T(4,128)} %refs_3_.2, f32[2,64]{1,0:T(2,128)} %refs_4_.2, s32[1,64]{1,0:T(1,128)} %bitcast.10), custom_call_target="tpu_custom_call" | custom-call | flops 10000000000 | tf_op jit(solution)/shard_map/scalars/pallas_call | solution.py:515
  1.1 0.1 copy-done
  1.2 0.5 %edges.1 = (f32[104,128]{1,0:T(8,128)S(1)}, f32[104,128]{1,0:T(8,128)S(1)}, f32[8,128]{1,0:T(8,128)S(1)}, bf16[8,192,128]{2,1,0:T(8,128)(2,1)S(1)}) custom-call(f32[1536,128]{1,0:T(8,128)S(1)} %bitcast.6, f32[8,128]{1,0:T(8,128)S(1)} %get-tuple-element.24.small, f32[8,128]{1,0:T(8,128)S(1)} %get-tuple-element.25.storm, ...), custom_call_target="tpu_custom_call" | custom-call | flops 10000000000 | tf_op jit(solution)/shard_map/edges/pallas_call | solution.py:524
  1.7 0.5 %collective-permute-start.1 = (f32[104,128]{1,0:T(8,128)S(1)}, f32[104,128]{1,0:T(8,128)S(1)}, u32[]{:S(2)}, u32[]{:S(2)}) collective-permute-start(f32[104,128]{1,0:T(8,128)S(1)} %get-tuple-element.34), channel_id=1, source_target_pairs={{0,1},{1,0},{2,3},{3,2},{4,5},{5,4},{6,7},{7,6},{8,9},{9,8},{10,11... | collective-permute-start | bytes 159752 | tf_op jit(solution)/shard_map/ppermute | solution.py:473
  2.2 0.1 collective-permute-start
  2.2 0.0 copy-start.1
  2.2 0.0 copy-start.2
  2.2 0.0 copy-start.3
  2.2 0.3 %row_messages.1 = s16[656,128]{1,0:T(8,128)(2,1)S(1)} custom-call(f32[1536,128]{1,0:T(8,128)S(1)} %bitcast.7, f32[8,128]{1,0:T(8,128)S(1)} %get-tuple-element.30.active), custom_call_target="tpu_custom_call" | custom-call | flops 10000000000 | tf_op jit(solution)/shard_map/row_messages/pallas_call | solution.py:532
  2.6 3.0 %collective-permute-start.2 = (s16[656,128]{1,0:T(8,128)(2,1)S(1)}, s16[656,128]{1,0:T(8,128)(2,1)S(1)}, u32[]{:S(2)}, u32[]{:S(2)}) collective-permute-start(s16[656,128]{1,0:T(8,128)(2,1)S(1)} %row_messages.1), channel_id=1, source_target_pairs={{0,2},{1,3},{2,0},{3,1},{4,6},{5,7},{6,4},{7,5},{8,10},{9,11},{10,... | collective-permute-start | bytes 503816 | tf_op jit(solution)/shard_map/ppermute | solution.py:501
  5.5 0.0 collective-permute-done.1
  5.6 1.6 %collective-permute-start.5 = (f32[104,128]{1,0:T(8,128)S(1)}, f32[104,128]{1,0:T(8,128)S(1)}, u32[]{:S(2)}, u32[]{:S(2)}) collective-permute-start(f32[104,128]{1,0:T(8,128)S(1)} %add.13.packs), channel_id=1, source_target_pairs={{0,6},{1,15},{2,4},{3,13},{4,10},{5,3},{6,8},{7,1},{8,14},{9,7},{1... | collective-permute-start | bytes 159752 | tf_op jit(solution)/shard_map/ppermute | solution.py:501
  7.2 1.6 %collective-permute-start.4 = (f32[104,128]{1,0:T(8,128)S(1)}, f32[104,128]{1,0:T(8,128)S(1)}, u32[]{:S(2)}, u32[]{:S(2)}) collective-permute-start(f32[104,128]{1,0:T(8,128)S(1)} %add.13.packs), channel_id=1, source_target_pairs={{0,4},{1,13},{2,6},{3,15},{4,8},{5,1},{6,10},{7,3},{8,12},{9,5},{1... | collective-permute-start | bytes 159752 | tf_op jit(solution)/shard_map/ppermute | solution.py:501
  8.7 0.0 collective-permute-done.other
  8.7 0.0 copy-done.1
  8.7 0.0 copy-done.2
  8.7 0.0 copy-done.3
  8.8 1.5 %own_network.1 = (bf16[192,1024]{1,0:T(8,128)(2,1)S(1)}, s16[16,128]{1,0:T(8,128)(2,1)S(1)}) custom-call(bf16[8,192,128]{2,1,0:T(8,128)(2,1)S(1)} %get-tuple-element.28.mine, bf16[8,192,128]{2,1,0:T(8,128)(2,1)S(1)} %collective-permute-done.other, bf16[256,384]{1,0:T(8,128)(2,1)S(1)} %copy-done.2, bf16[3,256,256]{2,1,0:T(8,128)(2,1)S(1)} %copy-done.1, ...), custom_call_target="tpu_custom_call" | custom-call | flops 10000000000 | tf_op jit(solution)/shard_map/own_network/pallas_call | solution.py:543
  10.3 0.4 %collective-permute-done.2.refs_0_ = s16[656,128]{1,0:T(8,128)(2,1)S(1)} collective-permute-done((s16[656,128]{1,0:T(8,128)(2,1)S(1)}, s16[656,128]{1,0:T(8,128)(2,1)S(1)}, u32[]{:S(2)}, u32[]{:S(2)}) %collective-permute-start.2) | collective-permute-done | bytes 167968 | tf_op jit(solution)/shard_map/ppermute | solution.py:501
  10.7 0.1 collective-permute-start.3
  10.8 1.3 %own_sweep.1 = (f32[8,192,128]{2,1,0:T(8,128)S(1)}, f32[18,64,128]{2,1,0:T(8,128)S(1)}) custom-call(f32[1536,128]{1,0:T(8,128)S(1)} %bitcast.8, bf16[192,1024]{1,0:T(8,128)(2,1)S(1)} %get-tuple-element.29.tendency, f32[8,128]{1,0:T(8,128)S(1)} %get-tuple-element.24.small, f32[8,128]{1,0:T(8,128)S(1)} %get-tuple-element.30.active), custom_call_target="tpu_custom_call" | custom-call | flops 10000000000 | tf_op jit(solution)/shard_map/own_sweep/pallas_call | solution.py:549
  12.0 0.1 collective-permute-done.3.refs_1_
  12.1 0.6 %row_input.1 = (bf16[384,256]{1,0:T(8,128)(2,1)S(1)}, f32[1,9,64,128]{3,2,1,0:T(8,128)S(1)}, f32[1,16,128]{2,1,0:T(8,128)S(1)}) custom-call(f32[104,128]{1,0:T(8,128)S(1)} %add.13.packs, s16[656,128]{1,0:T(8,128)(2,1)S(1)} %collective-permute-done.2.refs_0_, s16[656,128]{1,0:T(8,128)(2,1)S(1)} %collective-permute-done.3.refs_1_, bf16[256,384]{1,0:T(8,128)(2,1)S(1)} %copy-done.2), custom_call_target="tpu_custom_call" | custom-call | flops 10000000000 | tf_op jit(solution)/shard_map/row_input/pallas_call | solution.py:560
  12.7 0.0 collective-permute-done.5.refs_0_
  12.7 0.3 %collective-permute-done.4.ring = f32[104,128]{1,0:T(8,128)S(1)} collective-permute-done((f32[104,128]{1,0:T(8,128)S(1)}, f32[104,128]{1,0:T(8,128)S(1)}, u32[]{:S(2)}, u32[]{:S(2)}) %collective-permute-start.4) | collective-permute-done | bytes 53280 | tf_op jit(solution)/shard_map/ppermute | solution.py:501
  13.1 1.2 %halo_network.1 = (f32[3,64,128]{2,1,0:T(8,128)S(1)}, f32[3,64,128]{2,1,0:T(8,128)S(1)}) custom-call(f32[1,16,128]{2,1,0:T(8,128)S(1)} %get-tuple-element.38._.masks, f32[104,128]{1,0:T(8,128)S(1)} %collective-permute-done.4.ring, f32[104,128]{1,0:T(8,128)S(1)} %collective-permute-done.5.refs_0_, f32[18,64,128]{2,1,0:T(8,128)S(1)} %get-tuple-element.32.refs_1_.weights, ...), custom_call_target="tpu_custom_call" | custom-call | flops 10000000000 | tf_op jit(solution)/shard_map/halo_network/pallas_call | solution.py:567
  14.3 0.1 collective-permute-start.6
  14.4 1.1 %row_network.1 = (f32[9,64,128]{2,1,0:T(8,128)S(1)}, f32[3,64,128]{2,1,0:T(8,128)S(1)}) custom-call(bf16[384,256]{1,0:T(8,128)(2,1)S(1)} %get-tuple-element.36.hidden, f32[1,9,64,128]{3,2,1,0:T(8,128)S(1)} %get-tuple-element.37.fields, f32[1,16,128]{2,1,0:T(8,128)S(1)} %get-tuple-element.38._.masks, f32[3,64,128]{2,1,0:T(8,128)S(1)} %get-tuple-element.39.halo, ...), custom_call_target="tpu_custom_call" | custom-call | flops 10000000000 | tf_op jit(solution)/shard_map/row_network/pallas_call | solution.py:574
  15.4 0.2 %collective-permute-done.6.fix_other = f32[3,64,128]{2,1,0:T(8,128)S(1)} collective-permute-done((f32[3,64,128]{2,1,0:T(8,128)S(1)}, f32[3,64,128]{2,1,0:T(8,128)S(1)}, u32[]{:S(2)}, u32[]{:S(2)}) %collective-permute-start.6) | collective-permute-done | bytes 98336 | tf_op jit(solution)/shard_map/ppermute | solution.py:473
  15.6 1.1 %finish.1 = f32[1536,128]{1,0:T(8,128)} custom-call(f32[8,192,128]{2,1,0:T(8,128)S(1)} %get-tuple-element.31.swept, f32[18,64,128]{2,1,0:T(8,128)S(1)} %get-tuple-element.32.refs_1_.weights, f32[3,64,128]{2,1,0:T(8,128)S(1)} %get-tuple-element.40.fix_mine, f32[3,64,128]{2,1,0:T(8,128)S(1)} %collective-permute-done.6.fix_other, ...), custom_call_target="tpu_custom_call" | custom-call | flops 10000000000 | tf_op jit(solution)/shard_map/finish/pallas_call | solution.py:580
  (3 shorter events, 0.0 us)
Async XLA Ops:
  0.0 1.2 %copy-start = (f32[3,64,8,128]{3,2,1,0:T(8,128)S(1)}, f32[3,64,8,128]{3,2,1,0:T(8,128)}, u32[]{:S(2)}) copy-start(f32[3,64,8,128]{3,2,1,0:T(8,128)} %param.10) | copy-start | bytes 2359300
  1.7 3.9 %collective-permute-start.1 = (f32[104,128]{1,0:T(8,128)S(1)}, f32[104,128]{1,0:T(8,128)S(1)}, u32[]{:S(2)}, u32[]{:S(2)}) collective-permute-start(f32[104,128]{1,0:T(8,128)S(1)} %get-tuple-element.34), channel_id=1, source_target_pairs={{0,1},{1,0},{2,3},{3,2},{4,5},{5,4},{6,7},{7,6},{8,9},{9,8},{10,11... | collective-permute-start | bytes 159752 | tf_op jit(solution)/shard_map/ppermute | solution.py:473
  2.2 6.6 %collective-permute-start = (bf16[8,192,128]{2,1,0:T(8,128)(2,1)S(1)}, bf16[8,192,128]{2,1,0:T(8,128)(2,1)S(1)}, u32[]{:S(2)}, u32[]{:S(2)}) collective-permute-start(bf16[8,192,128]{2,1,0:T(8,128)(2,1)S(1)} %get-tuple-element.28.mine), channel_id=1, source_target_pairs={{0,1},{1,0},{2,3},{3,2},{4,5},{5,4},{6,7},{7,6},{8,9},{9,8},{10,11... | collective-permute-start | bytes 1179656 | tf_op jit(solution)/shard_map/ppermute | solution.py:473
  2.2 6.5 %copy-start.1 = (bf16[3,256,256]{2,1,0:T(8,128)(2,1)S(1)}, bf16[3,256,256]{2,1,0:T(8,128)(2,1)}, u32[]{:S(2)}) copy-start(bf16[3,256,256]{2,1,0:T(8,128)(2,1)} %w_mid.3) | copy-start | bytes 1179652
  2.2 6.5 %copy-start.2 = (bf16[256,384]{1,0:T(8,128)(2,1)S(1)}, bf16[256,384]{1,0:T(8,128)(2,1)}, u32[]{:S(2)}) copy-start(bf16[256,384]{1,0:T(8,128)(2,1)} %refs_2_.3) | copy-start | bytes 589828
  2.2 6.5 %copy-start.3 = (bf16[384,256]{1,0:T(8,128)(2,1)S(1)}, bf16[384,256]{1,0:T(8,128)(2,1)}, u32[]{:S(2)}) copy-start(bf16[384,256]{1,0:T(8,128)(2,1)} %w_out.3) | copy-start | bytes 589828
  2.6 8.1 %collective-permute-start.2 = (s16[656,128]{1,0:T(8,128)(2,1)S(1)}, s16[656,128]{1,0:T(8,128)(2,1)S(1)}, u32[]{:S(2)}, u32[]{:S(2)}) collective-permute-start(s16[656,128]{1,0:T(8,128)(2,1)S(1)} %row_messages.1), channel_id=1, source_target_pairs={{0,2},{1,3},{2,0},{3,1},{4,6},{5,7},{6,4},{7,5},{8,10},{9,11},{10,... | collective-permute-start | bytes 503816 | tf_op jit(solution)/shard_map/ppermute | solution.py:501
  5.6 7.2 %collective-permute-start.5 = (f32[104,128]{1,0:T(8,128)S(1)}, f32[104,128]{1,0:T(8,128)S(1)}, u32[]{:S(2)}, u32[]{:S(2)}) collective-permute-start(f32[104,128]{1,0:T(8,128)S(1)} %add.13.packs), channel_id=1, source_target_pairs={{0,6},{1,15},{2,4},{3,13},{4,10},{5,3},{6,8},{7,1},{8,14},{9,7},{1... | collective-permute-start | bytes 159752 | tf_op jit(solution)/shard_map/ppermute | solution.py:501
  7.2 5.9 %collective-permute-start.4 = (f32[104,128]{1,0:T(8,128)S(1)}, f32[104,128]{1,0:T(8,128)S(1)}, u32[]{:S(2)}, u32[]{:S(2)}) collective-permute-start(f32[104,128]{1,0:T(8,128)S(1)} %add.13.packs), channel_id=1, source_target_pairs={{0,4},{1,13},{2,6},{3,15},{4,8},{5,1},{6,10},{7,3},{8,12},{9,5},{1... | collective-permute-start | bytes 159752 | tf_op jit(solution)/shard_map/ppermute | solution.py:501
  10.7 1.5 %collective-permute-start.3 = (s16[656,128]{1,0:T(8,128)(2,1)S(1)}, s16[656,128]{1,0:T(8,128)(2,1)S(1)}, u32[]{:S(2)}, u32[]{:S(2)}) collective-permute-start(s16[656,128]{1,0:T(8,128)(2,1)S(1)} %broadcast_add_fusion), channel_id=1, source_target_pairs={{0,1},{1,0},{2,3},{3,2},{4,5},{5,4},{6,7},{7,6},{8,9},{9,8},{10,11... | collective-permute-start | bytes 503816 | tf_op jit(solution)/shard_map/ppermute | solution.py:473
  14.3 1.4 %collective-permute-start.6 = (f32[3,64,128]{2,1,0:T(8,128)S(1)}, f32[3,64,128]{2,1,0:T(8,128)S(1)}, u32[]{:S(2)}, u32[]{:S(2)}) collective-permute-start(f32[3,64,128]{2,1,0:T(8,128)S(1)} %get-tuple-element.41), channel_id=1, source_target_pairs={{0,1},{1,0},{2,3},{3,2},{4,5},{5,4},{6,7},{7,6},{8,9},{9,8},{10,11... | collective-permute-start | bytes 294920 | tf_op jit(solution)/shard_map/ppermute | solution.py:473

commit v8 on v7

--- a/solution.py
+++ b/solution.py
@@ -457,14 +457,14 @@
         copy.wait()
 
 
-def call(kernel, out_shape, scratch, flops, moved, name, **specs):
+def call(kernel, out_shape, scratch, name, **specs):
     return pl.pallas_call(
         kernel,
         out_shape=out_shape,
         **specs,
         scratch_shapes=scratch,
         compiler_params=pltpu.CompilerParams(vmem_limit_bytes=VMEM_LIMIT),
-        cost_estimate=pl.CostEstimate(flops=flops, bytes_accessed=moved, transcendentals=0),
+        cost_estimate=pl.CostEstimate(flops=10**10, bytes_accessed=0, transcendentals=0),
         name=name,
     )
 
@@ -473,31 +473,18 @@
     return lax.ppermute(x, "lev", [(0, 1), (1, 0)])
 
 
-def routes(lon_count, lat_count, move, along_lon):
+def send(x, move, along_lon):
+    axes = ("lon", "lat", "lev")
+    lon_count, lat_count = lax.axis_size("lon"), lax.axis_size("lat")
     pairs = []
     for i in range(lon_count):
         for j in range(lat_count):
-            to_lat = 1 - j if move == 0 else j + (move or 0)
+            to_lat = j if move is None else 1 - j if move == 0 else j + move
             if not 0 <= to_lat < lat_count:
                 continue
             for k in range(2):
-                to_lon = (i + (1 - 2 * k)) % lon_count if along_lon else i
-                pairs.append((((i * lat_count) + j) * 2 + k, ((to_lon * lat_count) + to_lat) * 2 + k))
-    return pairs
-
-
-def send(x, move, along_lon):
-    axes = ("lon", "lat", "lev")
-    lon_count, lat_count = lax.axis_size("lon"), lax.axis_size("lat")
-    if move is None:
-        pairs = []
-        for i in range(lon_count):
-            for j in range(lat_count):
-                for k in range(2):
-                    to_lon = (i + (1 - 2 * k)) % lon_count
-                    pairs.append(((i * lat_count + j) * 2 + k, (to_lon * lat_count + j) * 2 + k))
-    else:
-        pairs = routes(lon_count, lat_count, move, along_lon)
+                to_lon = (i + 1 - 2 * k) % lon_count if along_lon else i
+                pairs.append(((i * lat_count + j) * 2 + k, (to_lon * lat_count + to_lat) * 2 + k))
     return lax.ppermute(x, axes, pairs)
 
 
@@ -518,14 +505,14 @@
          jax.ShapeDtypeStruct((tracers, levels, LANES), F32)],
         [pltpu.VMEM(x.shape, x.dtype) for x in inputs]
         + [pltpu.VMEM((EXTRA, LANES), F32), pltpu.SemaphoreType.DMA((len(inputs),))],
-        10**10, 0, "scalars",
+        "scalars",
         in_specs=[pl.BlockSpec(memory_space=pltpu.HBM)] * len(inputs),
     )(*inputs)
     keep, give, active, features = call(
         functools.partial(edge_kernel, tracers, levels, rows),
         [pack_shape, pack_shape, mask_shape, jax.ShapeDtypeStruct((rows, width, columns), BF16)],
         [],
-        10**10, 0, "edges",
+        "edges",
     )(flat, small, storm, scale_lanes, in_scales)
     given = swap_cores(give)
     features_other = swap_cores(features)
@@ -533,7 +520,7 @@
         functools.partial(row_message_kernel, tracers, levels, rows, moves),
         [edge_shape] * count,
         [],
-        10000000000, 0, "row_messages",
+        "row_messages",
     )(flat, active)
     packs = keep + given
     corner = [send(packs, move, True) for move in moves]
@@ -544,13 +531,13 @@
         functools.partial(own_network_kernel, tracers, levels, rows),
         [jax.ShapeDtypeStruct((width, rows * columns), BF16), jax.ShapeDtypeStruct((2 * EXTRA, LANES), jnp.int16)],
         [pltpu.VMEM((2 * width, rows * columns), BF16)],
-        10000000000, 0, "own_network",
+        "own_network",
     )(features, features_other, w_in, w_mid, w_out)
     swept, weights = call(
         functools.partial(own_sweep_kernel, tracers, levels, rows),
         [jax.ShapeDtypeStruct((rows, width, columns), F32), jax.ShapeDtypeStruct((PLANES, levels, LANES), F32)],
         [],
-        10000000000, 0, "own_sweep",
+        "own_sweep",
     )(flat, tendency, small, active)
 
     fix_shape = jax.ShapeDtypeStruct((tracers, levels, LANES), F32)
@@ -562,26 +549,26 @@
         [jax.ShapeDtypeStruct((total, w_in.shape[0]), BF16), physics_shape,
          jax.ShapeDtypeStruct((count, 2 * EXTRA, LANES), F32)],
         [pltpu.VMEM((2 * width, total), BF16)],
-        10**10, 0, "row_input",
+        "row_input",
     )(packs, *edge, *edge_other, w_in)
     halo, fix_given = call(
         functools.partial(halo_network_kernel, tracers, levels, rows, moves),
         [fix_shape, fix_shape],
         [pltpu.VMEM((2 * width, LANES), BF16)],
-        10**10, 0, "halo_network",
+        "halo_network",
     )(row_masks, ring, *corner, weights, w_in, w_mid, w_out)
     fix_other = swap_cores(fix_given)
     beyond, fix_mine = call(
         functools.partial(row_kernel, tracers, levels, moves),
         [jax.ShapeDtypeStruct((tracers * W, levels, LANES), F32), fix_shape],
         [pltpu.VMEM((width, total), BF16)],
-        10**10, 0, "row_network",
+        "row_network",
     )(hidden, row_fields, row_masks, halo, weights, w_mid, w_out)
     out = call(
         functools.partial(finish_kernel, tracers, levels, rows, moves),
         jax.ShapeDtypeStruct((width * rows, columns), F32),
         [pltpu.VMEM((width * rows, columns), F32), pltpu.SemaphoreType.DMA((width // HALF_GROUP,))],
-        10000000000, 0, "finish",
+        "finish",
         out_specs=pl.BlockSpec(memory_space=pltpu.HBM),
     )(swept, weights, fix_mine, fix_other, beyond)
     return out.reshape(fields.shape)

time: 16.9 us -> 16.9 us (level)
  no operation moved by 1% of the time
where the time goes in v8:
time: 16.9 us; the launch traced here: 16.8 us
  Pallas kernels  8.54 us (51%)
  starting transfers between devices  6.9 us (41%)
  waiting for transfers between devices  1.05 us (6%)
    ppermute x3, starting transfers between devices, send(): return lax.ppermute(x, axes, pairs)  6.16 us
    pallas_call x1, Pallas kernels, on_device(): call(functools.partial(own_network_kernel, tracers, levels, rows), [jax.S...  1.5 us
    pallas_call x1, Pallas kernels, on_device(): call(functools.partial(own_sweep_kernel, tracers, levels, rows), [jax.Sha...  1.28 us
    pallas_call x1, Pallas kernels, on_device(): call(functools.partial(halo_network_kernel, tracers, levels, rows, moves)...  1.17 us
    pallas_call x1, Pallas kernels, on_device(): call(functools.partial(finish_kernel, tracers, levels, rows, moves), jax....  1.14 us
    pallas_call x1, Pallas kernels, on_device(): call(functools.partial(scalar_kernel, tracers, levels, rows), [jax.ShapeD...  1.09 us
    pallas_call x1, Pallas kernels, on_device(): call(functools.partial(row_kernel, tracers, levels, moves), [jax.ShapeDty...  1.06 us
    ppermute x3, waiting for transfers between devices, send(): return lax.ppermute(x, axes, pairs)  0.75 us
  transfers between devices with their start and end apart: 7, of which 4 were waited for; matrix products, arithmetic and copies ran while one was open for 0% of the time, Pallas kernels for 28%

profile of v8, /device:TPU:0, one launch (start us, length us, event | category | flops | bytes accessed | tf_op | source)
XLA Modules:
  0.0 16.8 jit_solution(14121679520145919647)
XLA Ops:
  0.0 0.0 copy-start
  0.0 1.1 %scalars.1 = (f32[8,128]{1,0:T(8,128)S(1)}, f32[8,128]{1,0:T(8,128)S(1)}, f32[2,64,128]{2,1,0:T(8,128)S(1)}, f32[3,64,128]{2,1,0:T(8,128)S(1)}) custom-call(f32[3,64]{1,0:T(4,128)} %refs_0_.1, s32[8,128]{1,0:T(8,128)} %refs_1_.1, s32[4,8]{1,0:T(4,128)} %bitcast.9, f32[3,64]{1,0:T(4,128)} %refs_3_.2, f32[2,64]{1,0:T(2,128)} %refs_4_.2, s32[1,64]{1,0:T(1,128)} %bitcast.10), custom_call_target="tpu_custom_call" | custom-call | flops 10000000000 | tf_op jit(solution)/shard_map/scalars/pallas_call | solution.py:502
  1.1 0.1 copy-done
  1.2 0.5 %edges.1 = (f32[104,128]{1,0:T(8,128)S(1)}, f32[104,128]{1,0:T(8,128)S(1)}, f32[8,128]{1,0:T(8,128)S(1)}, bf16[8,192,128]{2,1,0:T(8,128)(2,1)S(1)}) custom-call(f32[1536,128]{1,0:T(8,128)S(1)} %bitcast.6, f32[8,128]{1,0:T(8,128)S(1)} %get-tuple-element.24.small, f32[8,128]{1,0:T(8,128)S(1)} %get-tuple-element.25.storm, ...), custom_call_target="tpu_custom_call" | custom-call | flops 10000000000 | tf_op jit(solution)/shard_map/edges/pallas_call | solution.py:511
  1.7 0.5 %collective-permute-start.1 = (f32[104,128]{1,0:T(8,128)S(1)}, f32[104,128]{1,0:T(8,128)S(1)}, u32[]{:S(2)}, u32[]{:S(2)}) collective-permute-start(f32[104,128]{1,0:T(8,128)S(1)} %get-tuple-element.34), channel_id=1, source_target_pairs={{0,1},{1,0},{2,3},{3,2},{4,5},{5,4},{6,7},{7,6},{8,9},{9,8},{10,11... | collective-permute-start | bytes 159752 | tf_op jit(solution)/shard_map/ppermute | solution.py:473
  2.2 0.1 collective-permute-start
  2.2 0.0 copy-start.1
  2.2 0.0 copy-start.2
  2.2 0.0 copy-start.3
  2.2 0.3 %row_messages.1 = s16[656,128]{1,0:T(8,128)(2,1)S(1)} custom-call(f32[1536,128]{1,0:T(8,128)S(1)} %bitcast.7, f32[8,128]{1,0:T(8,128)S(1)} %get-tuple-element.30.active), custom_call_target="tpu_custom_call" | custom-call | flops 10000000000 | tf_op jit(solution)/shard_map/row_messages/pallas_call | solution.py:519
  2.6 3.0 %collective-permute-start.2 = (s16[656,128]{1,0:T(8,128)(2,1)S(1)}, s16[656,128]{1,0:T(8,128)(2,1)S(1)}, u32[]{:S(2)}, u32[]{:S(2)}) collective-permute-start(s16[656,128]{1,0:T(8,128)(2,1)S(1)} %row_messages.1), channel_id=1, source_target_pairs={{0,2},{1,3},{2,0},{3,1},{4,6},{5,7},{6,4},{7,5},{8,10},{9,11},{10,... | collective-permute-start | bytes 503816 | tf_op jit(solution)/shard_map/ppermute | solution.py:488
  5.5 0.0 collective-permute-done.1
  5.6 1.6 %collective-permute-start.5 = (f32[104,128]{1,0:T(8,128)S(1)}, f32[104,128]{1,0:T(8,128)S(1)}, u32[]{:S(2)}, u32[]{:S(2)}) collective-permute-start(f32[104,128]{1,0:T(8,128)S(1)} %add.13.packs), channel_id=1, source_target_pairs={{0,6},{1,15},{2,4},{3,13},{4,10},{5,3},{6,8},{7,1},{8,14},{9,7},{1... | collective-permute-start | bytes 159752 | tf_op jit(solution)/shard_map/ppermute | solution.py:488
  7.2 1.6 %collective-permute-start.4 = (f32[104,128]{1,0:T(8,128)S(1)}, f32[104,128]{1,0:T(8,128)S(1)}, u32[]{:S(2)}, u32[]{:S(2)}) collective-permute-start(f32[104,128]{1,0:T(8,128)S(1)} %add.13.packs), channel_id=1, source_target_pairs={{0,4},{1,13},{2,6},{3,15},{4,8},{5,1},{6,10},{7,3},{8,12},{9,5},{1... | collective-permute-start | bytes 159752 | tf_op jit(solution)/shard_map/ppermute | solution.py:488
  8.7 0.0 collective-permute-done.other
  8.7 0.0 copy-done.1
  8.7 0.0 copy-done.2
  8.7 0.0 copy-done.3
  8.8 1.5 %own_network.1 = (bf16[192,1024]{1,0:T(8,128)(2,1)S(1)}, s16[16,128]{1,0:T(8,128)(2,1)S(1)}) custom-call(bf16[8,192,128]{2,1,0:T(8,128)(2,1)S(1)} %get-tuple-element.28.mine, bf16[8,192,128]{2,1,0:T(8,128)(2,1)S(1)} %collective-permute-done.other, bf16[256,384]{1,0:T(8,128)(2,1)S(1)} %copy-done.2, bf16[3,256,256]{2,1,0:T(8,128)(2,1)S(1)} %copy-done.1, ...), custom_call_target="tpu_custom_call" | custom-call | flops 10000000000 | tf_op jit(solution)/shard_map/own_network/pallas_call | solution.py:530
  10.3 0.4 %collective-permute-done.2.refs_0_ = s16[656,128]{1,0:T(8,128)(2,1)S(1)} collective-permute-done((s16[656,128]{1,0:T(8,128)(2,1)S(1)}, s16[656,128]{1,0:T(8,128)(2,1)S(1)}, u32[]{:S(2)}, u32[]{:S(2)}) %collective-permute-start.2) | collective-permute-done | bytes 167968 | tf_op jit(solution)/shard_map/ppermute | solution.py:488
  10.7 0.1 collective-permute-start.3
  10.8 1.3 %own_sweep.1 = (f32[8,192,128]{2,1,0:T(8,128)S(1)}, f32[18,64,128]{2,1,0:T(8,128)S(1)}) custom-call(f32[1536,128]{1,0:T(8,128)S(1)} %bitcast.8, bf16[192,1024]{1,0:T(8,128)(2,1)S(1)} %get-tuple-element.29.tendency, f32[8,128]{1,0:T(8,128)S(1)} %get-tuple-element.24.small, f32[8,128]{1,0:T(8,128)S(1)} %get-tuple-element.30.active), custom_call_target="tpu_custom_call" | custom-call | flops 10000000000 | tf_op jit(solution)/shard_map/own_sweep/pallas_call | solution.py:536
  12.0 0.1 collective-permute-done.3.refs_1_
  12.1 0.6 %row_input.1 = (bf16[384,256]{1,0:T(8,128)(2,1)S(1)}, f32[1,9,64,128]{3,2,1,0:T(8,128)S(1)}, f32[1,16,128]{2,1,0:T(8,128)S(1)}) custom-call(f32[104,128]{1,0:T(8,128)S(1)} %add.13.packs, s16[656,128]{1,0:T(8,128)(2,1)S(1)} %collective-permute-done.2.refs_0_, s16[656,128]{1,0:T(8,128)(2,1)S(1)} %collective-permute-done.3.refs_1_, bf16[256,384]{1,0:T(8,128)(2,1)S(1)} %copy-done.2), custom_call_target="tpu_custom_call" | custom-call | flops 10000000000 | tf_op jit(solution)/shard_map/row_input/pallas_call | solution.py:547
  12.7 0.0 collective-permute-done.5.refs_0_
  12.7 0.3 %collective-permute-done.4.ring = f32[104,128]{1,0:T(8,128)S(1)} collective-permute-done((f32[104,128]{1,0:T(8,128)S(1)}, f32[104,128]{1,0:T(8,128)S(1)}, u32[]{:S(2)}, u32[]{:S(2)}) %collective-permute-start.4) | collective-permute-done | bytes 53280 | tf_op jit(solution)/shard_map/ppermute | solution.py:488
  13.1 1.2 %halo_network.1 = (f32[3,64,128]{2,1,0:T(8,128)S(1)}, f32[3,64,128]{2,1,0:T(8,128)S(1)}) custom-call(f32[1,16,128]{2,1,0:T(8,128)S(1)} %get-tuple-element.38._.masks, f32[104,128]{1,0:T(8,128)S(1)} %collective-permute-done.4.ring, f32[104,128]{1,0:T(8,128)S(1)} %collective-permute-done.5.refs_0_, f32[18,64,128]{2,1,0:T(8,128)S(1)} %get-tuple-element.32.refs_1_.weights, ...), custom_call_target="tpu_custom_call" | custom-call | flops 10000000000 | tf_op jit(solution)/shard_map/halo_network/pallas_call | solution.py:554
  14.3 0.1 collective-permute-start.6
  14.4 1.1 %row_network.1 = (f32[9,64,128]{2,1,0:T(8,128)S(1)}, f32[3,64,128]{2,1,0:T(8,128)S(1)}) custom-call(bf16[384,256]{1,0:T(8,128)(2,1)S(1)} %get-tuple-element.36.hidden, f32[1,9,64,128]{3,2,1,0:T(8,128)S(1)} %get-tuple-element.37.fields, f32[1,16,128]{2,1,0:T(8,128)S(1)} %get-tuple-element.38._.masks, f32[3,64,128]{2,1,0:T(8,128)S(1)} %get-tuple-element.39.halo, ...), custom_call_target="tpu_custom_call" | custom-call | flops 10000000000 | tf_op jit(solution)/shard_map/row_network/pallas_call | solution.py:561
  15.4 0.2 %collective-permute-done.6.fix_other = f32[3,64,128]{2,1,0:T(8,128)S(1)} collective-permute-done((f32[3,64,128]{2,1,0:T(8,128)S(1)}, f32[3,64,128]{2,1,0:T(8,128)S(1)}, u32[]{:S(2)}, u32[]{:S(2)}) %collective-permute-start.6) | collective-permute-done | bytes 98336 | tf_op jit(solution)/shard_map/ppermute | solution.py:473
  15.6 1.1 %finish.1 = f32[1536,128]{1,0:T(8,128)} custom-call(f32[8,192,128]{2,1,0:T(8,128)S(1)} %get-tuple-element.31.swept, f32[18,64,128]{2,1,0:T(8,128)S(1)} %get-tuple-element.32.refs_1_.weights, f32[3,64,128]{2,1,0:T(8,128)S(1)} %get-tuple-element.40.fix_mine, f32[3,64,128]{2,1,0:T(8,128)S(1)} %collective-permute-done.6.fix_other, ...), custom_call_target="tpu_custom_call" | custom-call | flops 10000000000 | tf_op jit(solution)/shard_map/finish/pallas_call | solution.py:567
  (3 shorter events, 0.0 us)
Async XLA Ops:
  0.0 1.2 %copy-start = (f32[3,64,8,128]{3,2,1,0:T(8,128)S(1)}, f32[3,64,8,128]{3,2,1,0:T(8,128)}, u32[]{:S(2)}) copy-start(f32[3,64,8,128]{3,2,1,0:T(8,128)} %param.10) | copy-start | bytes 2359300
  1.7 3.9 %collective-permute-start.1 = (f32[104,128]{1,0:T(8,128)S(1)}, f32[104,128]{1,0:T(8,128)S(1)}, u32[]{:S(2)}, u32[]{:S(2)}) collective-permute-start(f32[104,128]{1,0:T(8,128)S(1)} %get-tuple-element.34), channel_id=1, source_target_pairs={{0,1},{1,0},{2,3},{3,2},{4,5},{5,4},{6,7},{7,6},{8,9},{9,8},{10,11... | collective-permute-start | bytes 159752 | tf_op jit(solution)/shard_map/ppermute | solution.py:473
  2.2 6.6 %collective-permute-start = (bf16[8,192,128]{2,1,0:T(8,128)(2,1)S(1)}, bf16[8,192,128]{2,1,0:T(8,128)(2,1)S(1)}, u32[]{:S(2)}, u32[]{:S(2)}) collective-permute-start(bf16[8,192,128]{2,1,0:T(8,128)(2,1)S(1)} %get-tuple-element.28.mine), channel_id=1, source_target_pairs={{0,1},{1,0},{2,3},{3,2},{4,5},{5,4},{6,7},{7,6},{8,9},{9,8},{10,11... | collective-permute-start | bytes 1179656 | tf_op jit(solution)/shard_map/ppermute | solution.py:473
  2.2 6.5 %copy-start.1 = (bf16[3,256,256]{2,1,0:T(8,128)(2,1)S(1)}, bf16[3,256,256]{2,1,0:T(8,128)(2,1)}, u32[]{:S(2)}) copy-start(bf16[3,256,256]{2,1,0:T(8,128)(2,1)} %w_mid.3) | copy-start | bytes 1179652
  2.2 6.5 %copy-start.2 = (bf16[256,384]{1,0:T(8,128)(2,1)S(1)}, bf16[256,384]{1,0:T(8,128)(2,1)}, u32[]{:S(2)}) copy-start(bf16[256,384]{1,0:T(8,128)(2,1)} %refs_2_.3) | copy-start | bytes 589828
  2.2 6.5 %copy-start.3 = (bf16[384,256]{1,0:T(8,128)(2,1)S(1)}, bf16[384,256]{1,0:T(8,128)(2,1)}, u32[]{:S(2)}) copy-start(bf16[384,256]{1,0:T(8,128)(2,1)} %w_out.3) | copy-start | bytes 589828
  2.6 8.1 %collective-permute-start.2 = (s16[656,128]{1,0:T(8,128)(2,1)S(1)}, s16[656,128]{1,0:T(8,128)(2,1)S(1)}, u32[]{:S(2)}, u32[]{:S(2)}) collective-permute-start(s16[656,128]{1,0:T(8,128)(2,1)S(1)} %row_messages.1), channel_id=1, source_target_pairs={{0,2},{1,3},{2,0},{3,1},{4,6},{5,7},{6,4},{7,5},{8,10},{9,11},{10,... | collective-permute-start | bytes 503816 | tf_op jit(solution)/shard_map/ppermute | solution.py:488
  5.6 7.2 %collective-permute-start.5 = (f32[104,128]{1,0:T(8,128)S(1)}, f32[104,128]{1,0:T(8,128)S(1)}, u32[]{:S(2)}, u32[]{:S(2)}) collective-permute-start(f32[104,128]{1,0:T(8,128)S(1)} %add.13.packs), channel_id=1, source_target_pairs={{0,6},{1,15},{2,4},{3,13},{4,10},{5,3},{6,8},{7,1},{8,14},{9,7},{1... | collective-permute-start | bytes 159752 | tf_op jit(solution)/shard_map/ppermute | solution.py:488
  7.2 5.9 %collective-permute-start.4 = (f32[104,128]{1,0:T(8,128)S(1)}, f32[104,128]{1,0:T(8,128)S(1)}, u32[]{:S(2)}, u32[]{:S(2)}) collective-permute-start(f32[104,128]{1,0:T(8,128)S(1)} %add.13.packs), channel_id=1, source_target_pairs={{0,4},{1,13},{2,6},{3,15},{4,8},{5,1},{6,10},{7,3},{8,12},{9,5},{1... | collective-permute-start | bytes 159752 | tf_op jit(solution)/shard_map/ppermute | solution.py:488
  10.7 1.5 %collective-permute-start.3 = (s16[656,128]{1,0:T(8,128)(2,1)S(1)}, s16[656,128]{1,0:T(8,128)(2,1)S(1)}, u32[]{:S(2)}, u32[]{:S(2)}) collective-permute-start(s16[656,128]{1,0:T(8,128)(2,1)S(1)} %broadcast_add_fusion), channel_id=1, source_target_pairs={{0,1},{1,0},{2,3},{3,2},{4,5},{5,4},{6,7},{7,6},{8,9},{9,8},{10,11... | collective-permute-start | bytes 503816 | tf_op jit(solution)/shard_map/ppermute | solution.py:473
  14.3 1.4 %collective-permute-start.6 = (f32[3,64,128]{2,1,0:T(8,128)S(1)}, f32[3,64,128]{2,1,0:T(8,128)S(1)}, u32[]{:S(2)}, u32[]{:S(2)}) collective-permute-start(f32[3,64,128]{2,1,0:T(8,128)S(1)} %get-tuple-element.41), channel_id=1, source_target_pairs={{0,1},{1,0},{2,3},{3,2},{4,5},{5,4},{6,7},{7,6},{8,9},{9,8},{10,11... | collective-permute-start | bytes 294920 | tf_op jit(solution)/shard_map/ppermute | solution.py:473

commit v9 on v8

--- a/solution.py
+++ b/solution.py
@@ -20,6 +20,7 @@
 BF16 = jnp.bfloat16
 GROUP = 32
 HALF_GROUP = 16
+EARLY_LAYERS = 1
 VMEM_LIMIT = 40 * 1024 * 1024
 
 
@@ -118,15 +119,18 @@
     mask_pack = jnp.broadcast_to(jnp.sum(mask_pack, axis=0, keepdims=True), (EXTRA, LANES))
     lane = lane_ids(1)
     east = lane % 6 < 3
-    last_mask = jnp.where(east, mask_pack, 0.0)
-    first_mask = turned(jnp.where(east, 0.0, mask_pack), -W)
-    keep[levels + half :] = jnp.where(head, last_mask, first_mask)
-    give[levels + half :] = turned(jnp.where(head, first_mask, last_mask), HALF_LANES)
+    side_mask = jnp.where(head, jnp.where(east, mask_pack, 0.0), turned(jnp.where(east, 0.0, mask_pack), -W))
+    free = (lane >= SCALE_LANE) & (lane < SCALE_LANE + HALF_LANES // 2)
+    side_masks = [jnp.where(free, turned(side_mask, SCALE_LANE - HALF_LANES // 2 * n), 0.0) for n in range(2)]
     last, first = side_messages(edges)
     keep[:levels] = jnp.where(head, last[0], first[0]) + scale_lanes[0]
     give[:levels] = turned(jnp.where(head, first[0], last[0]), HALF_LANES) + scale_lanes[1]
-    keep[levels : levels + half] = jnp.where(head, last[1], first[1])
-    give[levels : levels + half] = turned(jnp.where(head, first[1], last[1]), HALF_LANES)
+    third = jnp.where(head, last[1], first[1])
+    for n in range(2):
+        at = EXTRA * n
+        keep[levels + at : levels + at + EXTRA] = third[at : at + EXTRA] + side_masks[n]
+    keep[levels + 2 * EXTRA :] = third[2 * EXTRA :]
+    give[levels:] = turned(jnp.where(head, first[1], last[1]), HALF_LANES)
     active[...] = mask
     for n, x in enumerate(values):
         t, i = n // rows, n % rows
@@ -225,13 +229,18 @@
     return silu(lax.dot_general(x, w_in, (((0,), (1,)), ((), ())), preferred_element_type=F32)).astype(BF16)
 
 
-def further_layers(hidden, w_mid, w_last):
-    def layer(hidden, w):
-        return lax.dot_general(hidden, w, (((1,), (1,)), ((), ())), preferred_element_type=F32)
-
-    for k in range(len(w_mid)):
-        hidden = silu(layer(hidden, w_mid[k])).astype(BF16)
-    return layer(w_last, hidden).astype(BF16)
+def weights_times(hidden, w):
+    return lax.dot_general(hidden, w, (((1,), (1,)), ((), ())), preferred_element_type=F32)
+
+
+def middle_layers(hidden, w_mid, layers):
+    for k in layers:
+        hidden = silu(weights_times(hidden, w_mid[k])).astype(BF16)
+    return hidden
+
+
+def last_layer(hidden, w_last):
+    return weights_times(w_last, hidden).astype(BF16)
 
 
 OUT_SCALE, LON, LON_SIGN, LAT, LAT_SIGN, EDGE, PLANES = 0, 3, 7, 8, 12, 13, 18
@@ -310,7 +319,7 @@
 
 def row_input_kernel(tracers, levels, moves, packs, *refs):
     count = len(moves)
-    edge, edge_other, (w_in, hidden, fields, masks, x) = refs[:count], refs[count : 2 * count], refs[2 * count :]
+    edge, edge_other, (w_in, w_mid, hidden, fields, masks, x) = refs[:count], refs[count : 2 * count], refs[2 * count :]
     lev = lax.axis_index("lev")
     width = tracers * levels
     tail = W * width
@@ -331,10 +340,13 @@
                         fields[n, t * W + r] = value
     for n in range(count):
         masks[n] = from_fixed(edge[n][tail + levels :, :])
-    hidden[...] = first_layer(x[...], w_in[...])
-
-
-def edge_corrections(values, weights, head):
+    hidden[...] = middle_layers(first_layer(x[...], w_in[...]), w_mid, range(EARLY_LAYERS))
+
+
+def edge_corrections(values, weights, head, moves):
+    if len(moves) == 2:
+        near = (weights[LAT_SIGN] > 0.5) | (lane_ids(values[0].shape[0]) < 48)
+        values = [jnp.where(near, q, turned(q, -18)) for q in values]
     east = jnp.where(head, LANES - 1, 1), jnp.where(head, LANES - 2, 2)
     w = [jnp.where(head, weights[EDGE + 2 * k], weights[EDGE + 2 * k - 1]) for k in (1, 2)]
     return [weights[EDGE] * q + w[0] * turned(q, east[0]) + w[1] * turned(q, east[1]) for q in values]
@@ -343,7 +355,7 @@
 def halo_network_kernel(tracers, levels, rows, moves, _, ring, *refs):
     count = len(moves)
     corner = refs[:count]
-    weights, w_in, w_mid, w_out, mine, other, x = refs[count:]
+    weights, w_in, w_mid, w_out, mine, other, hidden, masks, x = refs[count:]
     lat, lev = lax.axis_index("lat"), lax.axis_index("lev")
     width = tracers * levels
     head = lev == 0
@@ -352,67 +364,76 @@
     shifts = [jnp.where(head, a, b) for a, b in ((W, 0), (0, LANES - W))]
     half = levels // 2
 
-    def place(message, part, which, extra):
+    def place(numbers, which, extra):
         moved = []
         for shift in shifts:
             shift = shift + (extra + LANES - HALF_LANES * which)
             shift = jnp.where(shift >= 2 * LANES, shift - 2 * LANES, jnp.where(shift >= LANES, shift - LANES, shift))
-            moved.append(turned(message[part, :], shift))
+            moved.append(turned(numbers, shift))
         return moved
 
-    def unpack(part, which):
-        lane_part = lane[: part.stop - part.start]
-        values = place(ring, part, which, 0)
+    def unpack(numbers_of, size, which):
+        lane_part = lane[:size]
+        values = place(numbers_of(ring), which, 0)
         used = lane_part < 48
         for n, move in enumerate(moves):
             base = 48 + 18 * n
             here = (lane_part >= base) & (lane_part < base + 18)
-            far = place(corner[n], part, which, base - 6 * first_row_received(move, lat, rows))
-            values = [jnp.where(here, q, value) for q, value in zip(far, values)]
+            beside = place(numbers_of(corner[n]), which, base - 6 * first_row_received(move, lat, rows))
+            values = [jnp.where(here, q, value) for q, value in zip(beside, values)]
             used = used | here
-        used = used & west[: lane_part.shape[0]]
+        used = used & west[:size]
         return [jnp.where(used, value, 0.0) for value in values]
 
-    mask = unpack(slice(levels + half, levels + half + EXTRA), 0)[0][:1]
+    def mask_of(message):
+        low, high = (
+            turned(message[levels + EXTRA * n : levels + EXTRA * (n + 1), :], HALF_LANES // 2 * n - SCALE_LANE) for n in range(2)
+        )
+        lane_part = lane[:EXTRA]
+        return jnp.where(lane_part < HALF_LANES // 2, low, jnp.where(lane_part < HALF_LANES, high, 0.0))
+
+    mask = unpack(mask_of, EXTRA, 0)[0][:1]
+    far = pl.ds(pl.multiple_of((1 - lev) * width, width), width)
     halos, scales = [], []
     for which in range(2):
         start = lev * width if which == 0 else (1 - lev) * width
-        values = unpack(slice(0, levels), which)
-        values.append(jnp.concatenate(unpack(slice(levels, levels + half), which), axis=0))
+        values = unpack(lambda message: message[:levels, :], levels, which)
+        values.append(jnp.concatenate(unpack(lambda message: message[levels:, :], half, which), axis=0))
         for t, value in enumerate(values):
             in_scale, out_scale = (read_scale(ring, which, n, tracers, levels) for n in (t, tracers + t))
             halos.append(value)
             scales.append(out_scale)
             x[pl.ds(pl.multiple_of(start + t * levels, levels), levels), :] = (value * in_scale).astype(BF16)
-    tendency = further_layers(first_layer(x[...], w_in[...]), w_mid, w_out[...]).astype(F32)
-    x_tendency = [tendency[n * levels : (n + 1) * levels] for n in range(2 * tracers)]
-    x_tendency = [
-        jnp.where(head, x_tendency[n], x_tendency[(n + tracers) % (2 * tracers)]) for n in range(2 * tracers)
+    hidden[...] = middle_layers(first_layer(x[...], w_in[...]), w_mid, range(len(w_mid)))
+    mine[...] = jnp.stack(halos[:tracers])
+    masks[...] = jnp.broadcast_to(mask, masks.shape)
+    tendency = last_layer(hidden[...], w_out[far, :]).astype(F32)
+    values = [
+        halos[tracers + t] + scales[tracers + t] * tendency[t * levels : (t + 1) * levels] * mask for t in range(tracers)
     ]
-    values = [halo + scale * moist * mask for halo, scale, moist in zip(halos, scales, x_tendency)]
-    if count == 2:
-        up = weights[LAT_SIGN] > 0.5
-        values = [jnp.where(up | (lane < 48), q, turned(q, -18)) for q in values]
-    for t, q in enumerate(edge_corrections(values[tracers:], weights, head)):
+    for t, q in enumerate(edge_corrections(values, weights, lev == 0, moves)):
         other[t] = q
-    for t in range(tracers):
-        mine[t] = values[t]
-
-
-def row_kernel(tracers, levels, moves, hidden, fields, masks, halo, weights, w_mid, w_out, beyond, fix, tendency):
+
+
+def row_kernel(tracers, levels, moves, hidden, fields, masks, halo, edge_hidden, edge_mask, weights, w_mid, w_out, beyond, fix, tendency):
     lev = lax.axis_index("lev")
-    for t, q in enumerate(edge_corrections([halo[t] for t in range(tracers)], weights, lev == 0)):
-        fix[t] = q
     width = tracers * levels
     near = pl.ds(pl.multiple_of(lev * width, width), width)
-    tendency[...] = further_layers(hidden[...], w_mid, w_out[near, :])
+    outer = middle_layers(hidden[...], w_mid, range(EARLY_LAYERS, len(w_mid)))
+    tendency[...] = last_layer(jnp.concatenate([edge_hidden[...], outer], axis=0), w_out[near, :])
+    values = [
+        halo[t] + weights[OUT_SCALE + t] * tendency[t * levels : (t + 1) * levels, :LANES].astype(F32) * edge_mask[0:1, :]
+        for t in range(tracers)
+    ]
+    for t, q in enumerate(edge_corrections(values, weights, lev == 0, moves)):
+        fix[t] = q
     up = weights[LAT_SIGN] > 0.5
     values = []
     for t in range(tracers):
         for r in range(W):
             rows_q = []
             for n in range(len(moves)):
-                column_at = (n * W + r) * LANES
+                column_at = (1 + n * W + r) * LANES
                 moist = tendency[t * levels : (t + 1) * levels, column_at : column_at + LANES].astype(F32)
                 rows_q.append(fields[n, t * W + r] + weights[OUT_SCALE + t] * moist * masks[n, r : r + 1, :])
             values.append(jnp.where(up, rows_q[0], rows_q[1]) if len(moves) == 2 else rows_q[0])
@@ -495,7 +516,7 @@
     count = len(moves)
     flat = fields.reshape(width * rows, columns)
     edge_shape = jax.ShapeDtypeStruct((W * width + levels + 2 * EXTRA, columns), jnp.int16)
-    pack_shape = jax.ShapeDtypeStruct((levels + levels // 2 + EXTRA, LANES), F32)
+    pack_shape = jax.ShapeDtypeStruct((levels + levels // 2, LANES), F32)
     inputs = (in_scale, storm_mask, balance.T, out_scale, courant, substeps.reshape(1, levels))
     inputs = [pltpu.with_memory_space_constraint(x, pltpu.HBM) for x in inputs]
     mask_shape = jax.ShapeDtypeStruct((rows, columns), F32)
@@ -550,10 +571,11 @@
          jax.ShapeDtypeStruct((count, 2 * EXTRA, LANES), F32)],
         [pltpu.VMEM((2 * width, total), BF16)],
         "row_input",
-    )(packs, *edge, *edge_other, w_in)
-    halo, fix_given = call(
+    )(packs, *edge, *edge_other, w_in, w_mid)
+    halo, fix_given, edge_hidden, edge_mask = call(
         functools.partial(halo_network_kernel, tracers, levels, rows, moves),
-        [fix_shape, fix_shape],
+        [fix_shape, fix_shape, jax.ShapeDtypeStruct((LANES, w_in.shape[0]), BF16),
+         jax.ShapeDtypeStruct((EXTRA, LANES), F32)],
         [pltpu.VMEM((2 * width, LANES), BF16)],
         "halo_network",
     )(row_masks, ring, *corner, weights, w_in, w_mid, w_out)
@@ -561,9 +583,9 @@
     beyond, fix_mine = call(
         functools.partial(row_kernel, tracers, levels, moves),
         [jax.ShapeDtypeStruct((tracers * W, levels, LANES), F32), fix_shape],
-        [pltpu.VMEM((width, total), BF16)],
+        [pltpu.VMEM((width, LANES + total), BF16)],
         "row_network",
-    )(hidden, row_fields, row_masks, halo, weights, w_mid, w_out)
+    )(hidden, row_fields, row_masks, halo, edge_hidden, edge_mask, weights, w_mid, w_out)
     out = call(
         functools.partial(finish_kernel, tracers, levels, rows, moves),
         jax.ShapeDtypeStruct((width * rows, columns), F32),

time: 16.9 us -> 16.9 us (level)
  waiting for transfers between devices: 1.05 us -> 0.7 us
  starting transfers between devices: 6.9 us -> 7.12 us
    ppermute x3, waiting for transfers between devices: 0.75 us -> 0.49 us  [send(): return lax.ppermute(x, axes, pairs)]
    ppermute x4, starting transfers between devices: 0.74 us -> 0.96 us  [swap_cores(): return lax.ppermute(x, 'lev', [(0, 1), (1, 0)])]
    pallas_call x1, Pallas kernels: 0.56 us -> 0.76 us  [on_device(): call(functools.partial(row_input_kernel, tracers, levels, moves), [jax.Sh...]
  transfers between devices with their start and end apart: 7 -> 7, of which waited for: 4 -> 4; matrix products, arithmetic and copies ran while one was open for 0% -> 0% of each run, Pallas kernels for 28% -> 29%
where the time goes in v9:
time: 16.9 us; the launch traced here: 16.7 us
  Pallas kernels  8.61 us (51%)
  starting transfers between devices  7.12 us (42%)
  waiting for transfers between devices  0.7 us (4%)
    ppermute x3, starting transfers between devices, send(): return lax.ppermute(x, axes, pairs)  6.16 us
    pallas_call x1, Pallas kernels, on_device(): call(functools.partial(own_network_kernel, tracers, levels, rows), [jax.S...  1.5 us
    pallas_call x1, Pallas kernels, on_device(): call(functools.partial(own_sweep_kernel, tracers, levels, rows), [jax.Sha...  1.28 us
    pallas_call x1, Pallas kernels, on_device(): call(functools.partial(finish_kernel, tracers, levels, rows, moves), jax....  1.15 us
    pallas_call x1, Pallas kernels, on_device(): call(functools.partial(halo_network_kernel, tracers, levels, rows, moves)...  1.14 us
    pallas_call x1, Pallas kernels, on_device(): call(functools.partial(scalar_kernel, tracers, levels, rows), [jax.ShapeD...  1.09 us
    ppermute x4, starting transfers between devices, swap_cores(): return lax.ppermute(x, 'lev', [(0, 1), (1, 0)])  0.96 us
    pallas_call x1, Pallas kernels, on_device(): call(functools.partial(row_kernel, tracers, levels, moves), [jax.ShapeDty...  0.93 us
  transfers between devices with their start and end apart: 7, of which 4 were waited for; matrix products, arithmetic and copies ran while one was open for 0% of the time, Pallas kernels for 29%

profile of v9, /device:TPU:0, one launch (start us, length us, event | category | flops | bytes accessed | tf_op | source)
XLA Modules:
  0.0 16.7 jit_solution(638202306363239924)
XLA Ops:
  0.0 0.0 copy-start
  0.0 1.1 %scalars.1 = (f32[8,128]{1,0:T(8,128)S(1)}, f32[8,128]{1,0:T(8,128)S(1)}, f32[2,64,128]{2,1,0:T(8,128)S(1)}, f32[3,64,128]{2,1,0:T(8,128)S(1)}) custom-call(f32[3,64]{1,0:T(4,128)} %refs_0_.1, s32[8,128]{1,0:T(8,128)} %refs_1_.1, s32[4,8]{1,0:T(4,128)} %bitcast.9, f32[3,64]{1,0:T(4,128)} %refs_3_.3, f32[2,64]{1,0:T(2,128)} %refs_4_.2, s32[1,64]{1,0:T(1,128)} %bitcast.10), custom_call_target="tpu_custom_call" | custom-call | flops 10000000000 | tf_op jit(solution)/shard_map/scalars/pallas_call | solution.py:523
  1.1 0.1 copy-done
  1.2 0.5 %edges.1 = (f32[96,128]{1,0:T(8,128)S(1)}, f32[96,128]{1,0:T(8,128)S(1)}, f32[8,128]{1,0:T(8,128)S(1)}, bf16[8,192,128]{2,1,0:T(8,128)(2,1)S(1)}) custom-call(f32[1536,128]{1,0:T(8,128)S(1)} %bitcast.6, f32[8,128]{1,0:T(8,128)S(1)} %get-tuple-element.26.small, f32[8,128]{1,0:T(8,128)S(1)} %get-tuple-element.27.storm, ...), custom_call_target="tpu_custom_call" | custom-call | flops 10000000000 | tf_op jit(solution)/shard_map/edges/pallas_call | solution.py:532
  1.7 0.5 %collective-permute-start.1 = (f32[96,128]{1,0:T(8,128)S(1)}, f32[96,128]{1,0:T(8,128)S(1)}, u32[]{:S(2)}, u32[]{:S(2)}) collective-permute-start(f32[96,128]{1,0:T(8,128)S(1)} %get-tuple-element.36), channel_id=1, source_target_pairs={{0,1},{1,0},{2,3},{3,2},{4,5},{5,4},{6,7},{7,6},{8,9},{9,8},{10,11... | collective-permute-start | bytes 147464 | tf_op jit(solution)/shard_map/ppermute | solution.py:494
  2.2 0.1 collective-permute-start
  2.2 0.0 copy-start.1
  2.2 0.0 copy-start.2
  2.2 0.0 copy-start.3
  2.2 0.3 %row_messages.1 = s16[656,128]{1,0:T(8,128)(2,1)S(1)} custom-call(f32[1536,128]{1,0:T(8,128)S(1)} %bitcast.7, f32[8,128]{1,0:T(8,128)S(1)} %get-tuple-element.32.active), custom_call_target="tpu_custom_call" | custom-call | flops 10000000000 | tf_op jit(solution)/shard_map/row_messages/pallas_call | solution.py:540
  2.6 3.0 %collective-permute-start.2 = (s16[656,128]{1,0:T(8,128)(2,1)S(1)}, s16[656,128]{1,0:T(8,128)(2,1)S(1)}, u32[]{:S(2)}, u32[]{:S(2)}) collective-permute-start(s16[656,128]{1,0:T(8,128)(2,1)S(1)} %row_messages.1), channel_id=1, source_target_pairs={{0,2},{1,3},{2,0},{3,1},{4,6},{5,7},{6,4},{7,5},{8,10},{9,11},{10,... | collective-permute-start | bytes 503816 | tf_op jit(solution)/shard_map/ppermute | solution.py:509
  5.5 0.0 collective-permute-done.1
  5.5 1.6 %collective-permute-start.5 = (f32[96,128]{1,0:T(8,128)S(1)}, f32[96,128]{1,0:T(8,128)S(1)}, u32[]{:S(2)}, u32[]{:S(2)}) collective-permute-start(f32[96,128]{1,0:T(8,128)S(1)} %add.13.packs), channel_id=1, source_target_pairs={{0,6},{1,15},{2,4},{3,13},{4,10},{5,3},{6,8},{7,1},{8,14},{9,7},{1... | collective-permute-start | bytes 147464 | tf_op jit(solution)/shard_map/ppermute | solution.py:509
  7.2 1.6 %collective-permute-start.4 = (f32[96,128]{1,0:T(8,128)S(1)}, f32[96,128]{1,0:T(8,128)S(1)}, u32[]{:S(2)}, u32[]{:S(2)}) collective-permute-start(f32[96,128]{1,0:T(8,128)S(1)} %add.13.packs), channel_id=1, source_target_pairs={{0,4},{1,13},{2,6},{3,15},{4,8},{5,1},{6,10},{7,3},{8,12},{9,5},{1... | collective-permute-start | bytes 147464 | tf_op jit(solution)/shard_map/ppermute | solution.py:509
  8.7 0.0 collective-permute-done.other
  8.7 0.0 copy-done.1
  8.7 0.0 copy-done.2
  8.7 0.0 copy-done.3
  8.7 1.5 %own_network.1 = (bf16[192,1024]{1,0:T(8,128)(2,1)S(1)}, s16[16,128]{1,0:T(8,128)(2,1)S(1)}) custom-call(bf16[8,192,128]{2,1,0:T(8,128)(2,1)S(1)} %get-tuple-element.30.mine, bf16[8,192,128]{2,1,0:T(8,128)(2,1)S(1)} %collective-permute-done.other, bf16[256,384]{1,0:T(8,128)(2,1)S(1)} %copy-done.2, bf16[3,256,256]{2,1,0:T(8,128)(2,1)S(1)} %copy-done.1, ...), custom_call_target="tpu_custom_call" | custom-call | flops 10000000000 | tf_op jit(solution)/shard_map/own_network/pallas_call | solution.py:551
  10.3 0.3 %collective-permute-done.2.refs_0_ = s16[656,128]{1,0:T(8,128)(2,1)S(1)} collective-permute-done((s16[656,128]{1,0:T(8,128)(2,1)S(1)}, s16[656,128]{1,0:T(8,128)(2,1)S(1)}, u32[]{:S(2)}, u32[]{:S(2)}) %collective-permute-start.2) | collective-permute-done | bytes 167968 | tf_op jit(solution)/shard_map/ppermute | solution.py:509
  10.6 0.1 collective-permute-start.3
  10.7 1.3 %own_sweep.1 = (f32[8,192,128]{2,1,0:T(8,128)S(1)}, f32[18,64,128]{2,1,0:T(8,128)S(1)}) custom-call(f32[1536,128]{1,0:T(8,128)S(1)} %bitcast.8, bf16[192,1024]{1,0:T(8,128)(2,1)S(1)} %get-tuple-element.31.tendency, f32[8,128]{1,0:T(8,128)S(1)} %get-tuple-element.26.small, f32[8,128]{1,0:T(8,128)S(1)} %get-tuple-element.32.active), custom_call_target="tpu_custom_call" | custom-call | flops 10000000000 | tf_op jit(solution)/shard_map/own_sweep/pallas_call | solution.py:557
  12.0 0.1 collective-permute-done.3.refs_1_
  12.1 0.8 %row_input.1 = (bf16[384,256]{1,0:T(8,128)(2,1)S(1)}, f32[1,9,64,128]{3,2,1,0:T(8,128)S(1)}, f32[1,16,128]{2,1,0:T(8,128)S(1)}) custom-call(f32[96,128]{1,0:T(8,128)S(1)} %add.13.packs, s16[656,128]{1,0:T(8,128)(2,1)S(1)} %collective-permute-done.2.refs_0_, s16[656,128]{1,0:T(8,128)(2,1)S(1)} %collective-permute-done.3.refs_1_, ...), custom_call_target="tpu_custom_call" | custom-call | flops 10000000000 | tf_op jit(solution)/shard_map/row_input/pallas_call | solution.py:568
  12.9 0.0 collective-permute-done.5.refs_0_
  12.9 0.2 collective-permute-done.4.ring
  13.0 1.1 %halo_network.1 = (f32[3,64,128]{2,1,0:T(8,128)S(1)}, f32[3,64,128]{2,1,0:T(8,128)S(1)}, bf16[128,256]{1,0:T(8,128)(2,1)S(1)}, f32[8,128]{1,0:T(8,128)S(1)}) custom-call(f32[1,16,128]{2,1,0:T(8,128)S(1)} %get-tuple-element.40._.masks, f32[96,128]{1,0:T(8,128)S(1)} %collective-permute-done.4.ring, f32[96,128]{1,0:T(8,128)S(1)} %collective-permute-done.5.refs_0_, ...), custom_call_target="tpu_custom_call" | custom-call | flops 10000000000 | tf_op jit(solution)/shard_map/halo_network/pallas_call | solution.py:575
  14.2 0.3 %collective-permute-start.6 = (f32[3,64,128]{2,1,0:T(8,128)S(1)}, f32[3,64,128]{2,1,0:T(8,128)S(1)}, u32[]{:S(2)}, u32[]{:S(2)}) collective-permute-start(f32[3,64,128]{2,1,0:T(8,128)S(1)} %get-tuple-element.45), channel_id=1, source_target_pairs={{0,1},{1,0},{2,3},{3,2},{4,5},{5,4},{6,7},{7,6},{8,9},{9,8},{10,11... | collective-permute-start | bytes 294920 | tf_op jit(solution)/shard_map/ppermute | solution.py:494
  14.5 0.9 %row_network.1 = (f32[9,64,128]{2,1,0:T(8,128)S(1)}, f32[3,64,128]{2,1,0:T(8,128)S(1)}) custom-call(bf16[384,256]{1,0:T(8,128)(2,1)S(1)} %get-tuple-element.38.hidden, f32[1,9,64,128]{3,2,1,0:T(8,128)S(1)} %get-tuple-element.39.fields, f32[1,16,128]{2,1,0:T(8,128)S(1)} %get-tuple-element.40._.masks, f32[3,64,128]{2,1,0:T(8,128)S(1)} %get-tuple-element.41.halo, ...), custom_call_target="tpu_custom_call" | custom-call | flops 10000000000 | tf_op jit(solution)/shard_map/row_network/pallas_call | solution.py:583
  15.5 0.1 collective-permute-done.6.fix_other
  15.6 1.2 %finish.1 = f32[1536,128]{1,0:T(8,128)} custom-call(f32[8,192,128]{2,1,0:T(8,128)S(1)} %get-tuple-element.33.swept, f32[18,64,128]{2,1,0:T(8,128)S(1)} %get-tuple-element.34.refs_1_.weights, f32[3,64,128]{2,1,0:T(8,128)S(1)} %get-tuple-element.44.fix_mine, f32[3,64,128]{2,1,0:T(8,128)S(1)} %collective-permute-done.6.fix_other, ...), custom_call_target="tpu_custom_call" | custom-call | flops 10000000000 | tf_op jit(solution)/shard_map/finish/pallas_call | solution.py:589
  (3 shorter events, 0.0 us)
Async XLA Ops:
  0.0 1.2 %copy-start = (f32[3,64,8,128]{3,2,1,0:T(8,128)S(1)}, f32[3,64,8,128]{3,2,1,0:T(8,128)}, u32[]{:S(2)}) copy-start(f32[3,64,8,128]{3,2,1,0:T(8,128)} %param.10) | copy-start | bytes 2359300
  1.7 3.9 %collective-permute-start.1 = (f32[96,128]{1,0:T(8,128)S(1)}, f32[96,128]{1,0:T(8,128)S(1)}, u32[]{:S(2)}, u32[]{:S(2)}) collective-permute-start(f32[96,128]{1,0:T(8,128)S(1)} %get-tuple-element.36), channel_id=1, source_target_pairs={{0,1},{1,0},{2,3},{3,2},{4,5},{5,4},{6,7},{7,6},{8,9},{9,8},{10,11... | collective-permute-start | bytes 147464 | tf_op jit(solution)/shard_map/ppermute | solution.py:494
  2.2 6.6 %collective-permute-start = (bf16[8,192,128]{2,1,0:T(8,128)(2,1)S(1)}, bf16[8,192,128]{2,1,0:T(8,128)(2,1)S(1)}, u32[]{:S(2)}, u32[]{:S(2)}) collective-permute-start(bf16[8,192,128]{2,1,0:T(8,128)(2,1)S(1)} %get-tuple-element.30.mine), channel_id=1, source_target_pairs={{0,1},{1,0},{2,3},{3,2},{4,5},{5,4},{6,7},{7,6},{8,9},{9,8},{10,11... | collective-permute-start | bytes 1179656 | tf_op jit(solution)/shard_map/ppermute | solution.py:494
  2.2 6.5 %copy-start.1 = (bf16[3,256,256]{2,1,0:T(8,128)(2,1)S(1)}, bf16[3,256,256]{2,1,0:T(8,128)(2,1)}, u32[]{:S(2)}) copy-start(bf16[3,256,256]{2,1,0:T(8,128)(2,1)} %w_mid.3) | copy-start | bytes 1179652
  2.2 6.5 %copy-start.2 = (bf16[256,384]{1,0:T(8,128)(2,1)S(1)}, bf16[256,384]{1,0:T(8,128)(2,1)}, u32[]{:S(2)}) copy-start(bf16[256,384]{1,0:T(8,128)(2,1)} %refs_2_.3) | copy-start | bytes 589828
  2.2 6.5 %copy-start.3 = (bf16[384,256]{1,0:T(8,128)(2,1)S(1)}, bf16[384,256]{1,0:T(8,128)(2,1)}, u32[]{:S(2)}) copy-start(bf16[384,256]{1,0:T(8,128)(2,1)} %w_out.3) | copy-start | bytes 589828
  2.6 8.0 %collective-permute-start.2 = (s16[656,128]{1,0:T(8,128)(2,1)S(1)}, s16[656,128]{1,0:T(8,128)(2,1)S(1)}, u32[]{:S(2)}, u32[]{:S(2)}) collective-permute-start(s16[656,128]{1,0:T(8,128)(2,1)S(1)} %row_messages.1), channel_id=1, source_target_pairs={{0,2},{1,3},{2,0},{3,1},{4,6},{5,7},{6,4},{7,5},{8,10},{9,11},{10,... | collective-permute-start | bytes 503816 | tf_op jit(solution)/shard_map/ppermute | solution.py:509
  5.5 7.3 %collective-permute-start.5 = (f32[96,128]{1,0:T(8,128)S(1)}, f32[96,128]{1,0:T(8,128)S(1)}, u32[]{:S(2)}, u32[]{:S(2)}) collective-permute-start(f32[96,128]{1,0:T(8,128)S(1)} %add.13.packs), channel_id=1, source_target_pairs={{0,6},{1,15},{2,4},{3,13},{4,10},{5,3},{6,8},{7,1},{8,14},{9,7},{1... | collective-permute-start | bytes 147464 | tf_op jit(solution)/shard_map/ppermute | solution.py:509
  7.2 5.9 %collective-permute-start.4 = (f32[96,128]{1,0:T(8,128)S(1)}, f32[96,128]{1,0:T(8,128)S(1)}, u32[]{:S(2)}, u32[]{:S(2)}) collective-permute-start(f32[96,128]{1,0:T(8,128)S(1)} %add.13.packs), channel_id=1, source_target_pairs={{0,4},{1,13},{2,6},{3,15},{4,8},{5,1},{6,10},{7,3},{8,12},{9,5},{1... | collective-permute-start | bytes 147464 | tf_op jit(solution)/shard_map/ppermute | solution.py:509
  10.6 1.5 %collective-permute-start.3 = (s16[656,128]{1,0:T(8,128)(2,1)S(1)}, s16[656,128]{1,0:T(8,128)(2,1)S(1)}, u32[]{:S(2)}, u32[]{:S(2)}) collective-permute-start(s16[656,128]{1,0:T(8,128)(2,1)S(1)} %broadcast_add_fusion), channel_id=1, source_target_pairs={{0,1},{1,0},{2,3},{3,2},{4,5},{5,4},{6,7},{7,6},{8,9},{9,8},{10,11... | collective-permute-start | bytes 503816 | tf_op jit(solution)/shard_map/ppermute | solution.py:494
  14.2 1.4 %collective-permute-start.6 = (f32[3,64,128]{2,1,0:T(8,128)S(1)}, f32[3,64,128]{2,1,0:T(8,128)S(1)}, u32[]{:S(2)}, u32[]{:S(2)}) collective-permute-start(f32[3,64,128]{2,1,0:T(8,128)S(1)} %get-tuple-element.45), channel_id=1, source_target_pairs={{0,1},{1,0},{2,3},{3,2},{4,5},{5,4},{6,7},{7,6},{8,9},{9,8},{10,11... | collective-permute-start | bytes 294920 | tf_op jit(solution)/shard_map/ppermute | solution.py:494

commit v10 on v9

--- a/solution.py
+++ b/solution.py
@@ -20,7 +20,7 @@
 BF16 = jnp.bfloat16
 GROUP = 32
 HALF_GROUP = 16
-EARLY_LAYERS = 1
+EARLY_LAYERS = 0
 VMEM_LIMIT = 40 * 1024 * 1024
 
 

time: 16.9 us -> 16.9 us (level)
  waiting for transfers between devices: 0.7 us -> 0.99 us
  starting transfers between devices: 7.12 us -> 6.9 us
    ppermute x4, starting transfers between devices: 0.96 us -> 0.75 us  [swap_cores(): return lax.ppermute(x, 'lev', [(0, 1), (1, 0)])]
    ppermute x3, waiting for transfers between devices: 0.49 us -> 0.69 us  [send(): return lax.ppermute(x, axes, pairs)]
    pallas_call x1, Pallas kernels: 0.76 us -> 0.56 us  [on_device(): call(functools.partial(row_input_kernel, tracers, levels, moves), [jax.Sh...]
  transfers between devices with their start and end apart: 7 -> 7, of which waited for: 4 -> 4; matrix products, arithmetic and copies ran while one was open for 0% -> 0% of each run, Pallas kernels for 29% -> 28%
where the time goes in v10:
time: 16.9 us; the launch traced here: 16.7 us
  Pallas kernels  8.53 us (50%)
  starting transfers between devices  6.9 us (41%)
  waiting for transfers between devices  0.99 us (6%)
    ppermute x3, starting transfers between devices, send(): return lax.ppermute(x, axes, pairs)  6.16 us
    pallas_call x1, Pallas kernels, on_device(): call(functools.partial(own_network_kernel, tracers, levels, rows), [jax.S...  1.5 us
    pallas_call x1, Pallas kernels, on_device(): call(functools.partial(own_sweep_kernel, tracers, levels, rows), [jax.Sha...  1.28 us
    pallas_call x1, Pallas kernels, on_device(): call(functools.partial(finish_kernel, tracers, levels, rows, moves), jax....  1.15 us
    pallas_call x1, Pallas kernels, on_device(): call(functools.partial(halo_network_kernel, tracers, levels, rows, moves)...  1.14 us
    pallas_call x1, Pallas kernels, on_device(): call(functools.partial(scalar_kernel, tracers, levels, rows), [jax.ShapeD...  1.09 us
    pallas_call x1, Pallas kernels, on_device(): call(functools.partial(row_kernel, tracers, levels, moves), [jax.ShapeDty...  1.05 us
    ppermute x4, starting transfers between devices, swap_cores(): return lax.ppermute(x, 'lev', [(0, 1), (1, 0)])  0.75 us
  transfers between devices with their start and end apart: 7, of which 4 were waited for; matrix products, arithmetic and copies ran while one was open for 0% of the time, Pallas kernels for 28%

profile of v10, /device:TPU:0, one launch (start us, length us, event | category | flops | bytes accessed | tf_op | source)
XLA Modules:
  0.0 16.7 jit_solution(9170779960396854879)
XLA Ops:
  0.0 0.0 copy-start
  0.0 1.1 %scalars.1 = (f32[8,128]{1,0:T(8,128)S(1)}, f32[8,128]{1,0:T(8,128)S(1)}, f32[2,64,128]{2,1,0:T(8,128)S(1)}, f32[3,64,128]{2,1,0:T(8,128)S(1)}) custom-call(f32[3,64]{1,0:T(4,128)} %refs_0_.1, s32[8,128]{1,0:T(8,128)} %refs_1_.1, s32[4,8]{1,0:T(4,128)} %bitcast.9, f32[3,64]{1,0:T(4,128)} %refs_3_.3, f32[2,64]{1,0:T(2,128)} %refs_4_.2, s32[1,64]{1,0:T(1,128)} %bitcast.10), custom_call_target="tpu_custom_call" | custom-call | flops 10000000000 | tf_op jit(solution)/shard_map/scalars/pallas_call | solution.py:523
  1.1 0.1 copy-done
  1.2 0.5 %edges.1 = (f32[96,128]{1,0:T(8,128)S(1)}, f32[96,128]{1,0:T(8,128)S(1)}, f32[8,128]{1,0:T(8,128)S(1)}, bf16[8,192,128]{2,1,0:T(8,128)(2,1)S(1)}) custom-call(f32[1536,128]{1,0:T(8,128)S(1)} %bitcast.6, f32[8,128]{1,0:T(8,128)S(1)} %get-tuple-element.26.small, f32[8,128]{1,0:T(8,128)S(1)} %get-tuple-element.27.storm, ...), custom_call_target="tpu_custom_call" | custom-call | flops 10000000000 | tf_op jit(solution)/shard_map/edges/pallas_call | solution.py:532
  1.7 0.5 %collective-permute-start.1 = (f32[96,128]{1,0:T(8,128)S(1)}, f32[96,128]{1,0:T(8,128)S(1)}, u32[]{:S(2)}, u32[]{:S(2)}) collective-permute-start(f32[96,128]{1,0:T(8,128)S(1)} %get-tuple-element.36), channel_id=1, source_target_pairs={{0,1},{1,0},{2,3},{3,2},{4,5},{5,4},{6,7},{7,6},{8,9},{9,8},{10,11... | collective-permute-start | bytes 147464 | tf_op jit(solution)/shard_map/ppermute | solution.py:494
  2.2 0.1 collective-permute-start
  2.2 0.0 copy-start.1
  2.2 0.0 copy-start.2
  2.2 0.0 copy-start.3
  2.2 0.3 %row_messages.1 = s16[656,128]{1,0:T(8,128)(2,1)S(1)} custom-call(f32[1536,128]{1,0:T(8,128)S(1)} %bitcast.7, f32[8,128]{1,0:T(8,128)S(1)} %get-tuple-element.32.active), custom_call_target="tpu_custom_call" | custom-call | flops 10000000000 | tf_op jit(solution)/shard_map/row_messages/pallas_call | solution.py:540
  2.6 3.0 %collective-permute-start.2 = (s16[656,128]{1,0:T(8,128)(2,1)S(1)}, s16[656,128]{1,0:T(8,128)(2,1)S(1)}, u32[]{:S(2)}, u32[]{:S(2)}) collective-permute-start(s16[656,128]{1,0:T(8,128)(2,1)S(1)} %row_messages.1), channel_id=1, source_target_pairs={{0,2},{1,3},{2,0},{3,1},{4,6},{5,7},{6,4},{7,5},{8,10},{9,11},{10,... | collective-permute-start | bytes 503816 | tf_op jit(solution)/shard_map/ppermute | solution.py:509
  5.5 0.0 collective-permute-done.1
  5.5 1.6 %collective-permute-start.5 = (f32[96,128]{1,0:T(8,128)S(1)}, f32[96,128]{1,0:T(8,128)S(1)}, u32[]{:S(2)}, u32[]{:S(2)}) collective-permute-start(f32[96,128]{1,0:T(8,128)S(1)} %add.13.packs), channel_id=1, source_target_pairs={{0,6},{1,15},{2,4},{3,13},{4,10},{5,3},{6,8},{7,1},{8,14},{9,7},{1... | collective-permute-start | bytes 147464 | tf_op jit(solution)/shard_map/ppermute | solution.py:509
  7.2 1.6 %collective-permute-start.4 = (f32[96,128]{1,0:T(8,128)S(1)}, f32[96,128]{1,0:T(8,128)S(1)}, u32[]{:S(2)}, u32[]{:S(2)}) collective-permute-start(f32[96,128]{1,0:T(8,128)S(1)} %add.13.packs), channel_id=1, source_target_pairs={{0,4},{1,13},{2,6},{3,15},{4,8},{5,1},{6,10},{7,3},{8,12},{9,5},{1... | collective-permute-start | bytes 147464 | tf_op jit(solution)/shard_map/ppermute | solution.py:509
  8.7 0.0 collective-permute-done.other
  8.7 0.0 copy-done.1
  8.7 0.0 copy-done.2
  8.7 0.0 copy-done.3
  8.7 1.5 %own_network.1 = (bf16[192,1024]{1,0:T(8,128)(2,1)S(1)}, s16[16,128]{1,0:T(8,128)(2,1)S(1)}) custom-call(bf16[8,192,128]{2,1,0:T(8,128)(2,1)S(1)} %get-tuple-element.30.mine, bf16[8,192,128]{2,1,0:T(8,128)(2,1)S(1)} %collective-permute-done.other, bf16[256,384]{1,0:T(8,128)(2,1)S(1)} %copy-done.2, bf16[3,256,256]{2,1,0:T(8,128)(2,1)S(1)} %copy-done.1, ...), custom_call_target="tpu_custom_call" | custom-call | flops 10000000000 | tf_op jit(solution)/shard_map/own_network/pallas_call | solution.py:551
  10.3 0.3 %collective-permute-done.2.refs_0_ = s16[656,128]{1,0:T(8,128)(2,1)S(1)} collective-permute-done((s16[656,128]{1,0:T(8,128)(2,1)S(1)}, s16[656,128]{1,0:T(8,128)(2,1)S(1)}, u32[]{:S(2)}, u32[]{:S(2)}) %collective-permute-start.2) | collective-permute-done | bytes 167968 | tf_op jit(solution)/shard_map/ppermute | solution.py:509
  10.6 0.1 collective-permute-start.3
  10.7 1.3 %own_sweep.1 = (f32[8,192,128]{2,1,0:T(8,128)S(1)}, f32[18,64,128]{2,1,0:T(8,128)S(1)}) custom-call(f32[1536,128]{1,0:T(8,128)S(1)} %bitcast.8, bf16[192,1024]{1,0:T(8,128)(2,1)S(1)} %get-tuple-element.31.tendency, f32[8,128]{1,0:T(8,128)S(1)} %get-tuple-element.26.small, f32[8,128]{1,0:T(8,128)S(1)} %get-tuple-element.32.active), custom_call_target="tpu_custom_call" | custom-call | flops 10000000000 | tf_op jit(solution)/shard_map/own_sweep/pallas_call | solution.py:557
  12.0 0.1 collective-permute-done.3.refs_1_
  12.1 0.6 %row_input.1 = (bf16[384,256]{1,0:T(8,128)(2,1)S(1)}, f32[1,9,64,128]{3,2,1,0:T(8,128)S(1)}, f32[1,16,128]{2,1,0:T(8,128)S(1)}) custom-call(f32[96,128]{1,0:T(8,128)S(1)} %add.13.packs, s16[656,128]{1,0:T(8,128)(2,1)S(1)} %collective-permute-done.2.refs_0_, s16[656,128]{1,0:T(8,128)(2,1)S(1)} %collective-permute-done.3.refs_1_, ...), custom_call_target="tpu_custom_call" | custom-call | flops 10000000000 | tf_op jit(solution)/shard_map/row_input/pallas_call | solution.py:568
  12.7 0.0 collective-permute-done.5.refs_0_
  12.7 0.4 %collective-permute-done.4.ring = f32[96,128]{1,0:T(8,128)S(1)} collective-permute-done((f32[96,128]{1,0:T(8,128)S(1)}, f32[96,128]{1,0:T(8,128)S(1)}, u32[]{:S(2)}, u32[]{:S(2)}) %collective-permute-start.4) | collective-permute-done | bytes 49184 | tf_op jit(solution)/shard_map/ppermute | solution.py:509
  13.0 1.1 %halo_network.1 = (f32[3,64,128]{2,1,0:T(8,128)S(1)}, f32[3,64,128]{2,1,0:T(8,128)S(1)}, bf16[128,256]{1,0:T(8,128)(2,1)S(1)}, f32[8,128]{1,0:T(8,128)S(1)}) custom-call(f32[1,16,128]{2,1,0:T(8,128)S(1)} %get-tuple-element.40._.masks, f32[96,128]{1,0:T(8,128)S(1)} %collective-permute-done.4.ring, f32[96,128]{1,0:T(8,128)S(1)} %collective-permute-done.5.refs_0_, ...), custom_call_target="tpu_custom_call" | custom-call | flops 10000000000 | tf_op jit(solution)/shard_map/halo_network/pallas_call | solution.py:575
  14.2 0.1 collective-permute-start.6
  14.3 1.1 %row_network.1 = (f32[9,64,128]{2,1,0:T(8,128)S(1)}, f32[3,64,128]{2,1,0:T(8,128)S(1)}) custom-call(bf16[384,256]{1,0:T(8,128)(2,1)S(1)} %get-tuple-element.38.hidden, f32[1,9,64,128]{3,2,1,0:T(8,128)S(1)} %get-tuple-element.39.fields, f32[1,16,128]{2,1,0:T(8,128)S(1)} %get-tuple-element.40._.masks, f32[3,64,128]{2,1,0:T(8,128)S(1)} %get-tuple-element.41.halo, ...), custom_call_target="tpu_custom_call" | custom-call | flops 10000000000 | tf_op jit(solution)/shard_map/row_network/pallas_call | solution.py:583
  15.4 0.2 %collective-permute-done.6.fix_other = f32[3,64,128]{2,1,0:T(8,128)S(1)} collective-permute-done((f32[3,64,128]{2,1,0:T(8,128)S(1)}, f32[3,64,128]{2,1,0:T(8,128)S(1)}, u32[]{:S(2)}, u32[]{:S(2)}) %collective-permute-start.6) | collective-permute-done | bytes 98336 | tf_op jit(solution)/shard_map/ppermute | solution.py:494
  15.6 1.2 %finish.1 = f32[1536,128]{1,0:T(8,128)} custom-call(f32[8,192,128]{2,1,0:T(8,128)S(1)} %get-tuple-element.33.swept, f32[18,64,128]{2,1,0:T(8,128)S(1)} %get-tuple-element.34.refs_1_.weights, f32[3,64,128]{2,1,0:T(8,128)S(1)} %get-tuple-element.44.fix_mine, f32[3,64,128]{2,1,0:T(8,128)S(1)} %collective-permute-done.6.fix_other, ...), custom_call_target="tpu_custom_call" | custom-call | flops 10000000000 | tf_op jit(solution)/shard_map/finish/pallas_call | solution.py:589
  (3 shorter events, 0.0 us)
Async XLA Ops:
  0.0 1.2 %copy-start = (f32[3,64,8,128]{3,2,1,0:T(8,128)S(1)}, f32[3,64,8,128]{3,2,1,0:T(8,128)}, u32[]{:S(2)}) copy-start(f32[3,64,8,128]{3,2,1,0:T(8,128)} %param.10) | copy-start | bytes 2359300
  1.7 3.9 %collective-permute-start.1 = (f32[96,128]{1,0:T(8,128)S(1)}, f32[96,128]{1,0:T(8,128)S(1)}, u32[]{:S(2)}, u32[]{:S(2)}) collective-permute-start(f32[96,128]{1,0:T(8,128)S(1)} %get-tuple-element.36), channel_id=1, source_target_pairs={{0,1},{1,0},{2,3},{3,2},{4,5},{5,4},{6,7},{7,6},{8,9},{9,8},{10,11... | collective-permute-start | bytes 147464 | tf_op jit(solution)/shard_map/ppermute | solution.py:494
  2.2 6.6 %collective-permute-start = (bf16[8,192,128]{2,1,0:T(8,128)(2,1)S(1)}, bf16[8,192,128]{2,1,0:T(8,128)(2,1)S(1)}, u32[]{:S(2)}, u32[]{:S(2)}) collective-permute-start(bf16[8,192,128]{2,1,0:T(8,128)(2,1)S(1)} %get-tuple-element.30.mine), channel_id=1, source_target_pairs={{0,1},{1,0},{2,3},{3,2},{4,5},{5,4},{6,7},{7,6},{8,9},{9,8},{10,11... | collective-permute-start | bytes 1179656 | tf_op jit(solution)/shard_map/ppermute | solution.py:494
  2.2 6.5 %copy-start.1 = (bf16[3,256,256]{2,1,0:T(8,128)(2,1)S(1)}, bf16[3,256,256]{2,1,0:T(8,128)(2,1)}, u32[]{:S(2)}) copy-start(bf16[3,256,256]{2,1,0:T(8,128)(2,1)} %w_mid.3) | copy-start | bytes 1179652
  2.2 6.5 %copy-start.2 = (bf16[256,384]{1,0:T(8,128)(2,1)S(1)}, bf16[256,384]{1,0:T(8,128)(2,1)}, u32[]{:S(2)}) copy-start(bf16[256,384]{1,0:T(8,128)(2,1)} %refs_2_.3) | copy-start | bytes 589828
  2.2 6.5 %copy-start.3 = (bf16[384,256]{1,0:T(8,128)(2,1)S(1)}, bf16[384,256]{1,0:T(8,128)(2,1)}, u32[]{:S(2)}) copy-start(bf16[384,256]{1,0:T(8,128)(2,1)} %w_out.3) | copy-start | bytes 589828
  2.6 8.0 %collective-permute-start.2 = (s16[656,128]{1,0:T(8,128)(2,1)S(1)}, s16[656,128]{1,0:T(8,128)(2,1)S(1)}, u32[]{:S(2)}, u32[]{:S(2)}) collective-permute-start(s16[656,128]{1,0:T(8,128)(2,1)S(1)} %row_messages.1), channel_id=1, source_target_pairs={{0,2},{1,3},{2,0},{3,1},{4,6},{5,7},{6,4},{7,5},{8,10},{9,11},{10,... | collective-permute-start | bytes 503816 | tf_op jit(solution)/shard_map/ppermute | solution.py:509
  5.5 7.1 %collective-permute-start.5 = (f32[96,128]{1,0:T(8,128)S(1)}, f32[96,128]{1,0:T(8,128)S(1)}, u32[]{:S(2)}, u32[]{:S(2)}) collective-permute-start(f32[96,128]{1,0:T(8,128)S(1)} %add.13.packs), channel_id=1, source_target_pairs={{0,6},{1,15},{2,4},{3,13},{4,10},{5,3},{6,8},{7,1},{8,14},{9,7},{1... | collective-permute-start | bytes 147464 | tf_op jit(solution)/shard_map/ppermute | solution.py:509
  7.2 5.9 %collective-permute-start.4 = (f32[96,128]{1,0:T(8,128)S(1)}, f32[96,128]{1,0:T(8,128)S(1)}, u32[]{:S(2)}, u32[]{:S(2)}) collective-permute-start(f32[96,128]{1,0:T(8,128)S(1)} %add.13.packs), channel_id=1, source_target_pairs={{0,4},{1,13},{2,6},{3,15},{4,8},{5,1},{6,10},{7,3},{8,12},{9,5},{1... | collective-permute-start | bytes 147464 | tf_op jit(solution)/shard_map/ppermute | solution.py:509
  10.6 1.5 %collective-permute-start.3 = (s16[656,128]{1,0:T(8,128)(2,1)S(1)}, s16[656,128]{1,0:T(8,128)(2,1)S(1)}, u32[]{:S(2)}, u32[]{:S(2)}) collective-permute-start(s16[656,128]{1,0:T(8,128)(2,1)S(1)} %broadcast_add_fusion), channel_id=1, source_target_pairs={{0,1},{1,0},{2,3},{3,2},{4,5},{5,4},{6,7},{7,6},{8,9},{9,8},{10,11... | collective-permute-start | bytes 503816 | tf_op jit(solution)/shard_map/ppermute | solution.py:494
  14.2 1.4 %collective-permute-start.6 = (f32[3,64,128]{2,1,0:T(8,128)S(1)}, f32[3,64,128]{2,1,0:T(8,128)S(1)}, u32[]{:S(2)}, u32[]{:S(2)}) collective-permute-start(f32[3,64,128]{2,1,0:T(8,128)S(1)} %get-tuple-element.45), channel_id=1, source_target_pairs={{0,1},{1,0},{2,3},{3,2},{4,5},{5,4},{6,7},{7,6},{8,9},{9,8},{10,11... | collective-permute-start | bytes 294920 | tf_op jit(solution)/shard_map/ppermute | solution.py:494

commit v11 on v10

--- a/solution.py
+++ b/solution.py
@@ -54,15 +54,15 @@
     return jnp.broadcast_to(turned_rows[:levels, index : index + 1], (levels, LANES))
 
 
-def side_messages(edges):
+def side_message(edges, west, base):
     lane = lane_ids(1)
     east = lane % 6 < 3
-    used = lane < HALF_LANES
+    used = (lane >= base) & (lane < base + HALF_LANES)
     half = edges[2].shape[0] // 2
+    even = jnp.where(west, base - W + LANES, base + LANES) % LANES
+    odd = jnp.where(west, base, base + W)
     pairs = ((edges[0], edges[1]), (edges[2][:half], edges[2][half:]))
-    last = [jnp.where(east, p, turned(q, W)) for p, q in pairs]
-    first = [jnp.where(used, jnp.where(east, turned(p, -W), q), 0.0) for p, q in pairs]
-    return last, first
+    return [jnp.where(used, jnp.where(east, turned(p, even), turned(q, odd)), 0.0) for p, q in pairs]
 
 
 def scalar_kernel(tracers, levels, rows, *refs):
@@ -122,15 +122,15 @@
     side_mask = jnp.where(head, jnp.where(east, mask_pack, 0.0), turned(jnp.where(east, 0.0, mask_pack), -W))
     free = (lane >= SCALE_LANE) & (lane < SCALE_LANE + HALF_LANES // 2)
     side_masks = [jnp.where(free, turned(side_mask, SCALE_LANE - HALF_LANES // 2 * n), 0.0) for n in range(2)]
-    last, first = side_messages(edges)
-    keep[:levels] = jnp.where(head, last[0], first[0]) + scale_lanes[0]
-    give[:levels] = turned(jnp.where(head, first[0], last[0]), HALF_LANES) + scale_lanes[1]
-    third = jnp.where(head, last[1], first[1])
+    kept, third = side_message(edges, ~head, 0)
+    passed = side_message(edges, head, HALF_LANES)
+    keep[:levels] = kept + scale_lanes[0]
+    give[:levels] = passed[0] + scale_lanes[1]
     for n in range(2):
         at = EXTRA * n
         keep[levels + at : levels + at + EXTRA] = third[at : at + EXTRA] + side_masks[n]
     keep[levels + 2 * EXTRA :] = third[2 * EXTRA :]
-    give[levels:] = turned(jnp.where(head, first[1], last[1]), HALF_LANES)
+    give[levels:] = passed[1]
     active[...] = mask
     for n, x in enumerate(values):
         t, i = n // rows, n % rows

time: 16.9 us -> 16.9 us (level)
  no operation moved by 1% of the time
where the time goes in v11:
time: 16.9 us; the launch traced here: 16.7 us
  Pallas kernels  8.5 us (50%)
  starting transfers between devices  6.94 us (41%)
  waiting for transfers between devices  0.99 us (6%)
    ppermute x3, starting transfers between devices, send(): return lax.ppermute(x, axes, pairs)  6.16 us
    pallas_call x1, Pallas kernels, on_device(): call(functools.partial(own_network_kernel, tracers, levels, rows), [jax.S...  1.5 us
    pallas_call x1, Pallas kernels, on_device(): call(functools.partial(own_sweep_kernel, tracers, levels, rows), [jax.Sha...  1.28 us
    pallas_call x1, Pallas kernels, on_device(): call(functools.partial(finish_kernel, tracers, levels, rows, moves), jax....  1.15 us
    pallas_call x1, Pallas kernels, on_device(): call(functools.partial(halo_network_kernel, tracers, levels, rows, moves)...  1.14 us
    pallas_call x1, Pallas kernels, on_device(): call(functools.partial(scalar_kernel, tracers, levels, rows), [jax.ShapeD...  1.09 us
    pallas_call x1, Pallas kernels, on_device(): call(functools.partial(row_kernel, tracers, levels, moves), [jax.ShapeDty...  1.05 us
    ppermute x4, starting transfers between devices, swap_cores(): return lax.ppermute(x, 'lev', [(0, 1), (1, 0)])  0.78 us
  transfers between devices with their start and end apart: 7, of which 4 were waited for; matrix products, arithmetic and copies ran while one was open for 0% of the time, Pallas kernels for 28%

profile of v11, /device:TPU:0, one launch (start us, length us, event | category | flops | bytes accessed | tf_op | source)
XLA Modules:
  0.0 16.7 jit_solution(15194151036174732062)
XLA Ops:
  0.0 0.0 copy-start
  0.0 1.1 %scalars.1 = (f32[8,128]{1,0:T(8,128)S(1)}, f32[8,128]{1,0:T(8,128)S(1)}, f32[2,64,128]{2,1,0:T(8,128)S(1)}, f32[3,64,128]{2,1,0:T(8,128)S(1)}) custom-call(f32[3,64]{1,0:T(4,128)} %refs_0_.1, s32[8,128]{1,0:T(8,128)} %refs_1_.1, s32[4,8]{1,0:T(4,128)} %bitcast.9, f32[3,64]{1,0:T(4,128)} %refs_3_.3, f32[2,64]{1,0:T(2,128)} %refs_4_.2, s32[1,64]{1,0:T(1,128)} %bitcast.10), custom_call_target="tpu_custom_call" | custom-call | flops 10000000000 | tf_op jit(solution)/shard_map/scalars/pallas_call | solution.py:523
  1.1 0.1 copy-done
  1.2 0.4 %edges.1 = (f32[96,128]{1,0:T(8,128)S(1)}, f32[96,128]{1,0:T(8,128)S(1)}, f32[8,128]{1,0:T(8,128)S(1)}, bf16[8,192,128]{2,1,0:T(8,128)(2,1)S(1)}) custom-call(f32[1536,128]{1,0:T(8,128)S(1)} %bitcast.6, f32[8,128]{1,0:T(8,128)S(1)} %get-tuple-element.26.small, f32[8,128]{1,0:T(8,128)S(1)} %get-tuple-element.27.storm, ...), custom_call_target="tpu_custom_call" | custom-call | flops 10000000000 | tf_op jit(solution)/shard_map/edges/pallas_call | solution.py:532
  1.7 0.5 %collective-permute-start.1 = (f32[96,128]{1,0:T(8,128)S(1)}, f32[96,128]{1,0:T(8,128)S(1)}, u32[]{:S(2)}, u32[]{:S(2)}) collective-permute-start(f32[96,128]{1,0:T(8,128)S(1)} %get-tuple-element.36), channel_id=1, source_target_pairs={{0,1},{1,0},{2,3},{3,2},{4,5},{5,4},{6,7},{7,6},{8,9},{9,8},{10,11... | collective-permute-start | bytes 147464 | tf_op jit(solution)/shard_map/ppermute | solution.py:494
  2.2 0.1 collective-permute-start
  2.3 0.0 copy-start.1
  2.3 0.0 copy-start.2
  2.3 0.0 copy-start.3
  2.3 0.3 %row_messages.1 = s16[656,128]{1,0:T(8,128)(2,1)S(1)} custom-call(f32[1536,128]{1,0:T(8,128)S(1)} %bitcast.7, f32[8,128]{1,0:T(8,128)S(1)} %get-tuple-element.32.active), custom_call_target="tpu_custom_call" | custom-call | flops 10000000000 | tf_op jit(solution)/shard_map/row_messages/pallas_call | solution.py:540
  2.6 3.0 %collective-permute-start.2 = (s16[656,128]{1,0:T(8,128)(2,1)S(1)}, s16[656,128]{1,0:T(8,128)(2,1)S(1)}, u32[]{:S(2)}, u32[]{:S(2)}) collective-permute-start(s16[656,128]{1,0:T(8,128)(2,1)S(1)} %row_messages.1), channel_id=1, source_target_pairs={{0,2},{1,3},{2,0},{3,1},{4,6},{5,7},{6,4},{7,5},{8,10},{9,11},{10,... | collective-permute-start | bytes 503816 | tf_op jit(solution)/shard_map/ppermute | solution.py:509
  5.6 0.0 collective-permute-done.1
  5.6 1.6 %collective-permute-start.5 = (f32[96,128]{1,0:T(8,128)S(1)}, f32[96,128]{1,0:T(8,128)S(1)}, u32[]{:S(2)}, u32[]{:S(2)}) collective-permute-start(f32[96,128]{1,0:T(8,128)S(1)} %add.13.packs), channel_id=1, source_target_pairs={{0,6},{1,15},{2,4},{3,13},{4,10},{5,3},{6,8},{7,1},{8,14},{9,7},{1... | collective-permute-start | bytes 147464 | tf_op jit(solution)/shard_map/ppermute | solution.py:509
  7.2 1.6 %collective-permute-start.4 = (f32[96,128]{1,0:T(8,128)S(1)}, f32[96,128]{1,0:T(8,128)S(1)}, u32[]{:S(2)}, u32[]{:S(2)}) collective-permute-start(f32[96,128]{1,0:T(8,128)S(1)} %add.13.packs), channel_id=1, source_target_pairs={{0,4},{1,13},{2,6},{3,15},{4,8},{5,1},{6,10},{7,3},{8,12},{9,5},{1... | collective-permute-start | bytes 147464 | tf_op jit(solution)/shard_map/ppermute | solution.py:509
  8.7 0.0 collective-permute-done.other
  8.7 0.0 copy-done.1
  8.8 0.0 copy-done.2
  8.8 0.0 copy-done.3
  8.8 1.5 %own_network.1 = (bf16[192,1024]{1,0:T(8,128)(2,1)S(1)}, s16[16,128]{1,0:T(8,128)(2,1)S(1)}) custom-call(bf16[8,192,128]{2,1,0:T(8,128)(2,1)S(1)} %get-tuple-element.30.mine, bf16[8,192,128]{2,1,0:T(8,128)(2,1)S(1)} %collective-permute-done.other, bf16[256,384]{1,0:T(8,128)(2,1)S(1)} %copy-done.2, bf16[3,256,256]{2,1,0:T(8,128)(2,1)S(1)} %copy-done.1, ...), custom_call_target="tpu_custom_call" | custom-call | flops 10000000000 | tf_op jit(solution)/shard_map/own_network/pallas_call | solution.py:551
  10.3 0.3 %collective-permute-done.2.refs_0_ = s16[656,128]{1,0:T(8,128)(2,1)S(1)} collective-permute-done((s16[656,128]{1,0:T(8,128)(2,1)S(1)}, s16[656,128]{1,0:T(8,128)(2,1)S(1)}, u32[]{:S(2)}, u32[]{:S(2)}) %collective-permute-start.2) | collective-permute-done | bytes 167968 | tf_op jit(solution)/shard_map/ppermute | solution.py:509
  10.7 0.1 collective-permute-start.3
  10.7 1.3 %own_sweep.1 = (f32[8,192,128]{2,1,0:T(8,128)S(1)}, f32[18,64,128]{2,1,0:T(8,128)S(1)}) custom-call(f32[1536,128]{1,0:T(8,128)S(1)} %bitcast.8, bf16[192,1024]{1,0:T(8,128)(2,1)S(1)} %get-tuple-element.31.tendency, f32[8,128]{1,0:T(8,128)S(1)} %get-tuple-element.26.small, f32[8,128]{1,0:T(8,128)S(1)} %get-tuple-element.32.active), custom_call_target="tpu_custom_call" | custom-call | flops 10000000000 | tf_op jit(solution)/shard_map/own_sweep/pallas_call | solution.py:557
  12.0 0.1 collective-permute-done.3.refs_1_
  12.1 0.6 %row_input.1 = (bf16[384,256]{1,0:T(8,128)(2,1)S(1)}, f32[1,9,64,128]{3,2,1,0:T(8,128)S(1)}, f32[1,16,128]{2,1,0:T(8,128)S(1)}) custom-call(f32[96,128]{1,0:T(8,128)S(1)} %add.13.packs, s16[656,128]{1,0:T(8,128)(2,1)S(1)} %collective-permute-done.2.refs_0_, s16[656,128]{1,0:T(8,128)(2,1)S(1)} %collective-permute-done.3.refs_1_, ...), custom_call_target="tpu_custom_call" | custom-call | flops 10000000000 | tf_op jit(solution)/shard_map/row_input/pallas_call | solution.py:568
  12.7 0.0 collective-permute-done.5.refs_0_
  12.7 0.4 %collective-permute-done.4.ring = f32[96,128]{1,0:T(8,128)S(1)} collective-permute-done((f32[96,128]{1,0:T(8,128)S(1)}, f32[96,128]{1,0:T(8,128)S(1)}, u32[]{:S(2)}, u32[]{:S(2)}) %collective-permute-start.4) | collective-permute-done | bytes 49184 | tf_op jit(solution)/shard_map/ppermute | solution.py:509
  13.1 1.1 %halo_network.1 = (f32[3,64,128]{2,1,0:T(8,128)S(1)}, f32[3,64,128]{2,1,0:T(8,128)S(1)}, bf16[128,256]{1,0:T(8,128)(2,1)S(1)}, f32[8,128]{1,0:T(8,128)S(1)}) custom-call(f32[1,16,128]{2,1,0:T(8,128)S(1)} %get-tuple-element.40._.masks, f32[96,128]{1,0:T(8,128)S(1)} %collective-permute-done.4.ring, f32[96,128]{1,0:T(8,128)S(1)} %collective-permute-done.5.refs_0_, ...), custom_call_target="tpu_custom_call" | custom-call | flops 10000000000 | tf_op jit(solution)/shard_map/halo_network/pallas_call | solution.py:575
  14.2 0.1 collective-permute-start.6
  14.3 1.1 %row_network.1 = (f32[9,64,128]{2,1,0:T(8,128)S(1)}, f32[3,64,128]{2,1,0:T(8,128)S(1)}) custom-call(bf16[384,256]{1,0:T(8,128)(2,1)S(1)} %get-tuple-element.38.hidden, f32[1,9,64,128]{3,2,1,0:T(8,128)S(1)} %get-tuple-element.39.fields, f32[1,16,128]{2,1,0:T(8,128)S(1)} %get-tuple-element.40._.masks, f32[3,64,128]{2,1,0:T(8,128)S(1)} %get-tuple-element.41.halo, ...), custom_call_target="tpu_custom_call" | custom-call | flops 10000000000 | tf_op jit(solution)/shard_map/row_network/pallas_call | solution.py:583
  15.4 0.2 %collective-permute-done.6.fix_other = f32[3,64,128]{2,1,0:T(8,128)S(1)} collective-permute-done((f32[3,64,128]{2,1,0:T(8,128)S(1)}, f32[3,64,128]{2,1,0:T(8,128)S(1)}, u32[]{:S(2)}, u32[]{:S(2)}) %collective-permute-start.6) | collective-permute-done | bytes 98336 | tf_op jit(solution)/shard_map/ppermute | solution.py:494
  15.6 1.2 %finish.1 = f32[1536,128]{1,0:T(8,128)} custom-call(f32[8,192,128]{2,1,0:T(8,128)S(1)} %get-tuple-element.33.swept, f32[18,64,128]{2,1,0:T(8,128)S(1)} %get-tuple-element.34.refs_1_.weights, f32[3,64,128]{2,1,0:T(8,128)S(1)} %get-tuple-element.44.fix_mine, f32[3,64,128]{2,1,0:T(8,128)S(1)} %collective-permute-done.6.fix_other, ...), custom_call_target="tpu_custom_call" | custom-call | flops 10000000000 | tf_op jit(solution)/shard_map/finish/pallas_call | solution.py:589
  (3 shorter events, 0.0 us)
Async XLA Ops:
  0.0 1.2 %copy-start = (f32[3,64,8,128]{3,2,1,0:T(8,128)S(1)}, f32[3,64,8,128]{3,2,1,0:T(8,128)}, u32[]{:S(2)}) copy-start(f32[3,64,8,128]{3,2,1,0:T(8,128)} %param.10) | copy-start | bytes 2359300
  1.7 3.9 %collective-permute-start.1 = (f32[96,128]{1,0:T(8,128)S(1)}, f32[96,128]{1,0:T(8,128)S(1)}, u32[]{:S(2)}, u32[]{:S(2)}) collective-permute-start(f32[96,128]{1,0:T(8,128)S(1)} %get-tuple-element.36), channel_id=1, source_target_pairs={{0,1},{1,0},{2,3},{3,2},{4,5},{5,4},{6,7},{7,6},{8,9},{9,8},{10,11... | collective-permute-start | bytes 147464 | tf_op jit(solution)/shard_map/ppermute | solution.py:494
  2.2 6.6 %collective-permute-start = (bf16[8,192,128]{2,1,0:T(8,128)(2,1)S(1)}, bf16[8,192,128]{2,1,0:T(8,128)(2,1)S(1)}, u32[]{:S(2)}, u32[]{:S(2)}) collective-permute-start(bf16[8,192,128]{2,1,0:T(8,128)(2,1)S(1)} %get-tuple-element.30.mine), channel_id=1, source_target_pairs={{0,1},{1,0},{2,3},{3,2},{4,5},{5,4},{6,7},{7,6},{8,9},{9,8},{10,11... | collective-permute-start | bytes 1179656 | tf_op jit(solution)/shard_map/ppermute | solution.py:494
  2.3 6.5 %copy-start.1 = (bf16[3,256,256]{2,1,0:T(8,128)(2,1)S(1)}, bf16[3,256,256]{2,1,0:T(8,128)(2,1)}, u32[]{:S(2)}) copy-start(bf16[3,256,256]{2,1,0:T(8,128)(2,1)} %w_mid.3) | copy-start | bytes 1179652
  2.3 6.5 %copy-start.2 = (bf16[256,384]{1,0:T(8,128)(2,1)S(1)}, bf16[256,384]{1,0:T(8,128)(2,1)}, u32[]{:S(2)}) copy-start(bf16[256,384]{1,0:T(8,128)(2,1)} %refs_2_.3) | copy-start | bytes 589828
  2.3 6.5 %copy-start.3 = (bf16[384,256]{1,0:T(8,128)(2,1)S(1)}, bf16[384,256]{1,0:T(8,128)(2,1)}, u32[]{:S(2)}) copy-start(bf16[384,256]{1,0:T(8,128)(2,1)} %w_out.3) | copy-start | bytes 589828
  2.6 8.0 %collective-permute-start.2 = (s16[656,128]{1,0:T(8,128)(2,1)S(1)}, s16[656,128]{1,0:T(8,128)(2,1)S(1)}, u32[]{:S(2)}, u32[]{:S(2)}) collective-permute-start(s16[656,128]{1,0:T(8,128)(2,1)S(1)} %row_messages.1), channel_id=1, source_target_pairs={{0,2},{1,3},{2,0},{3,1},{4,6},{5,7},{6,4},{7,5},{8,10},{9,11},{10,... | collective-permute-start | bytes 503816 | tf_op jit(solution)/shard_map/ppermute | solution.py:509
  5.6 7.1 %collective-permute-start.5 = (f32[96,128]{1,0:T(8,128)S(1)}, f32[96,128]{1,0:T(8,128)S(1)}, u32[]{:S(2)}, u32[]{:S(2)}) collective-permute-start(f32[96,128]{1,0:T(8,128)S(1)} %add.13.packs), channel_id=1, source_target_pairs={{0,6},{1,15},{2,4},{3,13},{4,10},{5,3},{6,8},{7,1},{8,14},{9,7},{1... | collective-permute-start | bytes 147464 | tf_op jit(solution)/shard_map/ppermute | solution.py:509
  7.2 5.9 %collective-permute-start.4 = (f32[96,128]{1,0:T(8,128)S(1)}, f32[96,128]{1,0:T(8,128)S(1)}, u32[]{:S(2)}, u32[]{:S(2)}) collective-permute-start(f32[96,128]{1,0:T(8,128)S(1)} %add.13.packs), channel_id=1, source_target_pairs={{0,4},{1,13},{2,6},{3,15},{4,8},{5,1},{6,10},{7,3},{8,12},{9,5},{1... | collective-permute-start | bytes 147464 | tf_op jit(solution)/shard_map/ppermute | solution.py:509
  10.7 1.5 %collective-permute-start.3 = (s16[656,128]{1,0:T(8,128)(2,1)S(1)}, s16[656,128]{1,0:T(8,128)(2,1)S(1)}, u32[]{:S(2)}, u32[]{:S(2)}) collective-permute-start(s16[656,128]{1,0:T(8,128)(2,1)S(1)} %broadcast_add_fusion), channel_id=1, source_target_pairs={{0,1},{1,0},{2,3},{3,2},{4,5},{5,4},{6,7},{7,6},{8,9},{9,8},{10,11... | collective-permute-start | bytes 503816 | tf_op jit(solution)/shard_map/ppermute | solution.py:494
  14.2 1.4 %collective-permute-start.6 = (f32[3,64,128]{2,1,0:T(8,128)S(1)}, f32[3,64,128]{2,1,0:T(8,128)S(1)}, u32[]{:S(2)}, u32[]{:S(2)}) collective-permute-start(f32[3,64,128]{2,1,0:T(8,128)S(1)} %get-tuple-element.45), channel_id=1, source_target_pairs={{0,1},{1,0},{2,3},{3,2},{4,5},{5,4},{6,7},{7,6},{8,9},{9,8},{10,11... | collective-permute-start | bytes 294920 | tf_op jit(solution)/shard_map/ppermute | solution.py:494
